TPU v7x, 32 devices: a whole 2x2x4 slice. The times are simulated.
32 devices in a mesh: videos: 2 (over y), tm: 4 (over z), sub: 4 (over x, core).
Axes of the slice: x: 2, y: 2, z: 4, core: 2. Of those that a mesh axis runs over, the one named last changes fastest.
Arguments:
- embeddings: bfloat16 [12288, 1024], P(('videos', 'tm', 'sub')), parts along dimension 0, may hold values from -2 to 2
- offsets: int32 [12288], P(('videos', 'tm', 'sub')), parts along dimension 0, may hold values from 1 to 1024
- limits: int32 [4], P('videos'), parts along dimension 0, may hold values from 0 to 192, as said below
Outputs:
- gradient: float32 [12288, 1024], P(('videos', 'tm', 'sub')), parts along dimension 0
There are 2 independent parts, one for each index of `videos`. A program takes and returns all parts, laid end to end along the dimension named above; each array names one. Nothing has to cross between parts.
Inputs may be any that keep to these rules, and one draw needn't show every extreme that they name: `limits`: one entry is exactly 192, less than one device's frames; the other is smaller.
All inputs are finite; a program needn't handle non-finite values.
Results may differ from a plain program's by a relative error of at most 0.0019.
Values may be sent and summed in bfloat16 or wider, within the bound.
No kernel may reach another device: no remote copies, remote signals or barrier semaphores. Data moves between devices by JAX's collectives and lax.ppermute only.
A program may use at most 64 MiB of HBM per device.

v0:
```python
import jax
import jax.numpy as jnp
from jax import lax
from jax.sharding import PartitionSpec as P

BAND = 1024


scale_factor = 16.0


def from_behind(x, axis, by):
    count = lax.axis_size(axis)
    pairs = [(i, i + by) for i in range(count) if 0 <= i + by < count]
    return lax.ppermute(x, axis, pairs)


def pair_mask(row_index, col_index, row_valid, col_valid):
    spacing = row_index[:, None] - col_index[None, :]
    inside = (jnp.abs(spacing) <= BAND) & (spacing != 0)
    return inside & row_valid[:, None] & col_valid[None, :]


def per_device(embeddings, offsets, limits):
    row_count = embeddings.shape[0]
    device = lax.axis_index(("tm", "sub"))
    frames = row_count * lax.axis_size(("tm", "sub"))
    reach_hops = (BAND + row_count - 1) // row_count
    lengths = [min(row_count, BAND - (step - 1) * row_count) for step in range(1, reach_hops + 1)]
    start_valid = limits[0]
    end_valid = frames - limits[1]
    own_index = device * row_count + jnp.arange(row_count, dtype=jnp.int32)
    win_index = device * row_count - BAND + jnp.arange(row_count + 2 * BAND, dtype=jnp.int32)
    own_valid = (own_index >= start_valid) & (own_index < end_valid)
    win_valid = (win_index >= start_valid) & (win_index < end_valid)
    forward = own_index + offsets
    own_positive = jnp.where(forward < end_valid, forward, own_index - offsets)
    earlier = []
    later = []
    for step in range(1, reach_hops + 1):
        length = lengths[step - 1]
        earlier.append(from_behind(embeddings[row_count - length :], ("tm", "sub"), step))
        later.append(from_behind(embeddings[:length], ("tm", "sub"), -step))
    window = jnp.concatenate(earlier[::-1] + [embeddings] + later, axis=0)
    scores = scale_factor * jnp.einsum(
        "td,ud->tu", embeddings, window, preferred_element_type=jnp.float32
    )
    in_band = pair_mask(own_index, win_index, own_valid, win_valid)
    masked = jnp.where(in_band, scores, -jnp.inf)
    row_max = jnp.where(own_valid, jnp.max(masked, axis=1), 0.0)
    totals = jnp.sum(jnp.exp(masked - row_max[:, None]), axis=1) + jnp.where(own_valid, 0.0, 1.0)
    log_sum = row_max + jnp.log(totals)
    weights = jnp.exp(masked - log_sum[:, None])
    hits = ((win_index[None, :] == own_positive[:, None]) & own_valid[:, None]).astype(jnp.float32)
    coefficient = (weights - hits).astype(jnp.bfloat16)
    query_grad = scale_factor * jnp.einsum(
        "tu,ud->td", coefficient, window, preferred_element_type=jnp.float32
    )
    key_grad = scale_factor * jnp.einsum(
        "tu,td->ud", coefficient, embeddings, preferred_element_type=jnp.float32
    )
    result = query_grad + key_grad[BAND : BAND + row_count]
    offset_low = BAND
    offset_high = BAND + row_count
    for step in range(1, reach_hops + 1):
        length = lengths[step - 1]
        offset_low = offset_low - length
        incoming = from_behind(key_grad[offset_low : offset_low + length], ("tm", "sub"), -step)
        result = result.at[row_count - length :].add(incoming)
        incoming_late = from_behind(
            key_grad[offset_high : offset_high + length], ("tm", "sub"), step
        )
        result = result.at[:length].add(incoming_late)
        offset_high = offset_high + length
    return result


def solution(mesh):
    return jax.shard_map(
        per_device,
        mesh=mesh,
        in_specs=(P(("videos", "tm", "sub"), None), P(("videos", "tm", "sub")), P("videos")),
        out_specs=P(("videos", "tm", "sub"), None),
        check_vma=False,
    )
```

profile of v0, /device:TPU:1, one launch (start us, length us, event | category | flops | bytes accessed | tf_op | source)
XLA Modules:
  0.0 223.5 jit_solution(3356767811751826879)
XLA Ops:
  0.0 0.0 copy-start
  0.0 5.0 %collective-permute-start.1 = (bf16[384,1024]{1,0:T(8,128)(2,1)}, bf16[384,1024]{1,0:T(8,128)(2,1)}, u32[]{:S(2)}, u32[]{:S(2)}) collective-permute-start(bf16[384,1024]{1,0:T(8,128)(2,1)} %param.23), channel_id=1, source_target_pairs={{0,2},{1,3},{2,4},{3,5},{4,6},{5,7},{6,8},{7,9},{8,10},{9,11},{10,... | collective-permute-start | bytes 2359304 | tf_op jit(solution)/shard_map/ppermute | solution.py:15
  5.0 3.1 %collective-permute-start.2 = (bf16[384,1024]{1,0:T(8,128)(2,1)}, bf16[384,1024]{1,0:T(8,128)(2,1)S(1)}, u32[]{:S(2)}, u32[]{:S(2)}) collective-permute-start(bf16[384,1024]{1,0:T(8,128)(2,1)} %param.23), channel_id=1, source_target_pairs={{0,1},{1,2},{2,3},{3,4},{4,5},{5,6},{6,7},{7,8},{8,9},{9,10},{10,1... | collective-permute-start | bytes 2359304 | tf_op jit(solution)/shard_map/ppermute | solution.py:15
  8.1 1.9 collective-permute-start.3
  10.0 1.3 collective-permute-start.4
  11.3 2.2 %fusion.17 = (bf16[256,1024]{1,0:T(8,128)(2,1)}, bf16[256,1024]{1,0:T(8,128)(2,1)}) fusion(bf16[384,1024]{1,0:T(8,128)(2,1)} %param.23), kind=kLoop, calls=%fused_computation.39 | loop fusion | bytes 2097152 | tf_op jit(solution)/shard_map/slice | solution.py:43
  13.6 6.5 %collective-permute-start = (bf16[256,1024]{1,0:T(8,128)(2,1)}, bf16[256,1024]{1,0:T(8,128)(2,1)}, u32[]{:S(2)}, u32[]{:S(2)}) collective-permute-start(bf16[256,1024]{1,0:T(8,128)(2,1)} %get-tuple-element.116), channel_id=1, source_target_pairs={{0,3},{1,4},{2,5},{3,6},{4,7},{5,8},{6,9},{7,10},{8,11},{9,12},{10... | collective-permute-start | bytes 1572872 | tf_op jit(solution)/shard_map/ppermute | solution.py:15
  20.1 1.3 fusion.18
  22.1 0.7 compare_select_fusion
  22.8 0.6 compare_and_fusion
  23.3 0.6 fusion.14
  23.9 1.8 collective-permute-done
  25.7 1.3 collective-permute-start.5
  27.0 1.1 constant_dynamic-update-slice_fusion.6
  28.1 23.4 %collective-permute-done.1 = bf16[384,1024]{1,0:T(8,128)(2,1)} collective-permute-done((bf16[384,1024]{1,0:T(8,128)(2,1)}, bf16[384,1024]{1,0:T(8,128)(2,1)}, u32[]{:S(2)}, u32[]{:S(2)}) %collective-permute-start.1) | collective-permute-done | bytes 786464 | tf_op jit(solution)/shard_map/ppermute | solution.py:15
  51.5 1.2 constant_dynamic-update-slice_fusion.5
  52.7 14.0 %collective-permute-done.2 = bf16[384,1024]{1,0:T(8,128)(2,1)S(1)} collective-permute-done((bf16[384,1024]{1,0:T(8,128)(2,1)}, bf16[384,1024]{1,0:T(8,128)(2,1)S(1)}, u32[]{:S(2)}, u32[]{:S(2)}) %collective-permute-start.2) | collective-permute-done | bytes 786464 | tf_op jit(solution)/shard_map/ppermute | solution.py:15
  66.7 0.1 constant_dynamic-update-slice_fusion.4
  66.7 0.0 copy-done
  66.7 0.1 constant_dynamic-update-slice_fusion.3
  66.8 0.0 collective-permute-done.3
  66.8 0.1 constant_dynamic-update-slice_fusion.2
  66.9 0.0 collective-permute-done.4
  66.9 0.1 constant_dynamic-update-slice_fusion.1
  66.9 8.9 %collective-permute-done.5 = bf16[256,1024]{1,0:T(8,128)(2,1)S(1)} collective-permute-done((bf16[256,1024]{1,0:T(8,128)(2,1)}, bf16[256,1024]{1,0:T(8,128)(2,1)S(1)}, u32[]{:S(2)}, u32[]{:S(2)}) %collective-permute-start.5) | collective-permute-done | bytes 524320 | tf_op jit(solution)/shard_map/ppermute | solution.py:15
  75.9 4.0 %fusion.19 = (f32[384]{0:T(512)S(1)}, f32[384,2432]{0,1:T(8,128)S(1)}) fusion(bf16[2432,1024]{1,0:T(8,128)(2,1)S(1)} %constant_dynamic-update-slice_fusion, bf16[384,1024]{1,0:T(8,128)(2,1)S(1)} %copy-done, pred[2432]{0:T(1024)(128)(4,1)S(1)} %compare_and_fusion, pred[384]{0:T(512)(128)(4,1)S(1)} %fusion.14, s32[2432]{0:T(1024)S(1)} %iota_add_fusion, ...), kind=kOutput, calls=%fused_computation.41 | convolution fusion | flops 1921941120 | bytes 9518336 | tf_op jit(solution)/shard_map/td,ud->tu/dot_general | solution.py:45
  79.9 0.6 broadcast_select_fusion
  80.5 0.6 exponential_reduce_fusion
  81.1 0.6 log_add_fusion
  81.7 3.2 %convolution_multiply_fusion = f32[2432,1024]{1,0:T(8,128)S(1)} fusion(bf16[384,1024]{1,0:T(8,128)(2,1)S(1)} %copy-done, f32[384,2432]{0,1:T(8,128)S(1)} %get-tuple-element.120, s32[384]{0:T(512)S(1)} %get-tuple-element.121, f32[384]{0:T(512)S(1)} %log_add_fusion, s32[2432]{0:T(1024)S(1)} %iota_add_fusion, pred[384]{0:T(512)(128)(4,1)S(1)} %fusion.14), kind=kOutput, calls=%fused_computation | convolution fusion | flops 1920696320 | bytes 14496640 | tf_op jit(solution)/shard_map/tu,td->ud/dot_general | solution.py:59
  84.9 1.1 fusion.16
  86.0 2.5 %collective-permute-start.6 = (f32[384,1024]{1,0:T(8,128)S(1)}, f32[384,1024]{1,0:T(8,128)S(1)}, u32[]{:S(2)}, u32[]{:S(2)}) collective-permute-start(f32[384,1024]{1,0:T(8,128)S(1)} %get-tuple-element.111), channel_id=1, source_target_pairs={{1,0},{2,1},{3,2},{4,3},{5,4},{6,5},{7,6},{8,7},{9,8},{10,9},{11,1... | collective-permute-start | bytes 4718600 | tf_op jit(solution)/shard_map/ppermute | solution.py:15
  88.5 3.1 %collective-permute-start.7 = (f32[384,1024]{1,0:T(8,128)S(1)}, f32[384,1024]{1,0:T(8,128)S(1)}, u32[]{:S(2)}, u32[]{:S(2)}) collective-permute-start(f32[384,1024]{1,0:T(8,128)S(1)} %get-tuple-element.114), channel_id=1, source_target_pairs={{0,1},{1,2},{2,3},{3,4},{4,5},{5,6},{6,7},{7,8},{8,9},{9,10},{10,1... | collective-permute-start | bytes 4718600 | tf_op jit(solution)/shard_map/ppermute | solution.py:15
  91.6 1.3 collective-permute-start.8
  92.9 6.6 %collective-permute-start.9 = (f32[384,1024]{1,0:T(8,128)S(1)}, f32[384,1024]{1,0:T(8,128)}, u32[]{:S(2)}, u32[]{:S(2)}) collective-permute-start(f32[384,1024]{1,0:T(8,128)S(1)} %get-tuple-element.112), channel_id=1, source_target_pairs={{0,2},{1,3},{2,4},{3,5},{4,6},{5,7},{6,8},{7,9},{8,10},{9,11},{10,... | collective-permute-start | bytes 4718600 | tf_op jit(solution)/shard_map/ppermute | solution.py:15
  99.4 0.2 fusion.15
  99.7 1.3 collective-permute-start.10
  101.0 17.1 %collective-permute-done.6 = f32[384,1024]{1,0:T(8,128)S(1)} collective-permute-done((f32[384,1024]{1,0:T(8,128)S(1)}, f32[384,1024]{1,0:T(8,128)S(1)}, u32[]{:S(2)}, u32[]{:S(2)}) %collective-permute-start.6) | collective-permute-done | bytes 1572896 | tf_op jit(solution)/shard_map/ppermute | solution.py:15
  118.1 4.2 %collective-permute-start.11 = (f32[256,1024]{1,0:T(8,128)S(1)}, f32[256,1024]{1,0:T(8,128)S(1)}, u32[]{:S(2)}, u32[]{:S(2)}) collective-permute-start(f32[256,1024]{1,0:T(8,128)S(1)} %get-tuple-element.109), channel_id=1, source_target_pairs={{0,3},{1,4},{2,5},{3,6},{4,7},{5,8},{6,9},{7,10},{8,11},{9,12},{10... | collective-permute-start | bytes 3145736 | tf_op jit(solution)/shard_map/ppermute | solution.py:15
  122.3 64.9 %collective-permute-done.7 = f32[384,1024]{1,0:T(8,128)S(1)} collective-permute-done((f32[384,1024]{1,0:T(8,128)S(1)}, f32[384,1024]{1,0:T(8,128)S(1)}, u32[]{:S(2)}, u32[]{:S(2)}) %collective-permute-start.7) | collective-permute-done | bytes 1572896 | tf_op jit(solution)/shard_map/ppermute | solution.py:15
  187.2 0.0 collective-permute-done.8
  187.2 28.2 %collective-permute-done.9 = f32[384,1024]{1,0:T(8,128)} collective-permute-done((f32[384,1024]{1,0:T(8,128)S(1)}, f32[384,1024]{1,0:T(8,128)}, u32[]{:S(2)}, u32[]{:S(2)}) %collective-permute-start.9) | collective-permute-done | bytes 1572896 | tf_op jit(solution)/shard_map/ppermute | solution.py:15
  215.4 4.2 %fusion.9 = f32[384,1024]{1,0:T(8,128)S(1)} fusion(f32[384,1024]{1,0:T(8,128)} %collective-permute-done.9, f32[384,1024]{1,0:T(8,128)S(1)} %collective-permute-done.8, f32[384,1024]{1,0:T(8,128)S(1)} %collective-permute-done.7, f32[384,1024]{1,0:T(8,128)S(1)} %collective-permute-done.6, f32[2432,1024]{1,0:T(8,128)S(1)} %convolution_multiply_fusion, ...), kind=kOutput, calls=%fused_computation.16 | convolution fusion | flops 1920565248 | bytes 18166656 | tf_op jit(solution)/shard_map/tu,ud->td/dot_general | solution.py:56
  219.6 0.0 collective-permute-done.10
  219.6 0.3 fusion.11
  219.9 0.0 copy-start.1
  219.9 0.0 collective-permute-done.11
  219.9 1.1 copy-done.1
  221.1 2.4 %fusion.10 = f32[384,1024]{1,0:T(8,128)} fusion(f32[384,1024]{1,0:T(8,128)} %copy-done.1, f32[256,1024]{1,0:T(8,128)S(1)} %collective-permute-done.11), kind=kLoop, calls=%fused_computation.18 | loop fusion | flops 262144 | bytes 3145728 | tf_op jit(solution)/shard_map/scatter-add | solution.py:73
  (2 shorter events, 0.0 us)
Async XLA Ops:
  0.0 66.7 %copy-start = (bf16[384,1024]{1,0:T(8,128)(2,1)S(1)}, bf16[384,1024]{1,0:T(8,128)(2,1)}, u32[]{:S(2)}) copy-start(bf16[384,1024]{1,0:T(8,128)(2,1)} %param.23) | copy-start | bytes 2359300
  0.0 51.5 %collective-permute-start.1 = (bf16[384,1024]{1,0:T(8,128)(2,1)}, bf16[384,1024]{1,0:T(8,128)(2,1)}, u32[]{:S(2)}, u32[]{:S(2)}) collective-permute-start(bf16[384,1024]{1,0:T(8,128)(2,1)} %param.23), channel_id=1, source_target_pairs={{0,2},{1,3},{2,4},{3,5},{4,6},{5,7},{6,8},{7,9},{8,10},{9,11},{10,... | collective-permute-start | bytes 2359304 | tf_op jit(solution)/shard_map/ppermute | solution.py:15
  5.0 61.7 %collective-permute-start.2 = (bf16[384,1024]{1,0:T(8,128)(2,1)}, bf16[384,1024]{1,0:T(8,128)(2,1)S(1)}, u32[]{:S(2)}, u32[]{:S(2)}) collective-permute-start(bf16[384,1024]{1,0:T(8,128)(2,1)} %param.23), channel_id=1, source_target_pairs={{0,1},{1,2},{2,3},{3,4},{4,5},{5,6},{6,7},{7,8},{8,9},{9,10},{10,1... | collective-permute-start | bytes 2359304 | tf_op jit(solution)/shard_map/ppermute | solution.py:15
  8.1 58.7 %collective-permute-start.3 = (bf16[384,1024]{1,0:T(8,128)(2,1)}, bf16[384,1024]{1,0:T(8,128)(2,1)S(1)}, u32[]{:S(2)}, u32[]{:S(2)}) collective-permute-start(bf16[384,1024]{1,0:T(8,128)(2,1)} %param.23), channel_id=1, source_target_pairs={{1,0},{2,1},{3,2},{4,3},{5,4},{6,5},{7,6},{8,7},{9,8},{10,9},{11,1... | collective-permute-start | bytes 2359304 | tf_op jit(solution)/shard_map/ppermute | solution.py:15
  10.0 56.8 %collective-permute-start.4 = (bf16[384,1024]{1,0:T(8,128)(2,1)}, bf16[384,1024]{1,0:T(8,128)(2,1)S(1)}, u32[]{:S(2)}, u32[]{:S(2)}) collective-permute-start(bf16[384,1024]{1,0:T(8,128)(2,1)} %param.23), channel_id=1, source_target_pairs={{2,0},{3,1},{4,2},{5,3},{6,4},{7,5},{8,6},{9,7},{10,8},{11,9},{12,... | collective-permute-start | bytes 2359304 | tf_op jit(solution)/shard_map/ppermute | solution.py:15
  13.6 12.1 %collective-permute-start = (bf16[256,1024]{1,0:T(8,128)(2,1)}, bf16[256,1024]{1,0:T(8,128)(2,1)}, u32[]{:S(2)}, u32[]{:S(2)}) collective-permute-start(bf16[256,1024]{1,0:T(8,128)(2,1)} %get-tuple-element.116), channel_id=1, source_target_pairs={{0,3},{1,4},{2,5},{3,6},{4,7},{5,8},{6,9},{7,10},{8,11},{9,12},{10... | collective-permute-start | bytes 1572872 | tf_op jit(solution)/shard_map/ppermute | solution.py:15
  25.7 50.1 %collective-permute-start.5 = (bf16[256,1024]{1,0:T(8,128)(2,1)}, bf16[256,1024]{1,0:T(8,128)(2,1)S(1)}, u32[]{:S(2)}, u32[]{:S(2)}) collective-permute-start(bf16[256,1024]{1,0:T(8,128)(2,1)} %get-tuple-element.115), channel_id=1, source_target_pairs={{3,0},{4,1},{5,2},{6,3},{7,4},{8,5},{9,6},{10,7},{11,8},{12,9},{13... | collective-permute-start | bytes 1572872 | tf_op jit(solution)/shard_map/ppermute | solution.py:15
  86.0 32.1 %collective-permute-start.6 = (f32[384,1024]{1,0:T(8,128)S(1)}, f32[384,1024]{1,0:T(8,128)S(1)}, u32[]{:S(2)}, u32[]{:S(2)}) collective-permute-start(f32[384,1024]{1,0:T(8,128)S(1)} %get-tuple-element.111), channel_id=1, source_target_pairs={{1,0},{2,1},{3,2},{4,3},{5,4},{6,5},{7,6},{8,7},{9,8},{10,9},{11,1... | collective-permute-start | bytes 4718600 | tf_op jit(solution)/shard_map/ppermute | solution.py:15
  88.5 98.7 %collective-permute-start.7 = (f32[384,1024]{1,0:T(8,128)S(1)}, f32[384,1024]{1,0:T(8,128)S(1)}, u32[]{:S(2)}, u32[]{:S(2)}) collective-permute-start(f32[384,1024]{1,0:T(8,128)S(1)} %get-tuple-element.114), channel_id=1, source_target_pairs={{0,1},{1,2},{2,3},{3,4},{4,5},{5,6},{6,7},{7,8},{8,9},{9,10},{10,1... | collective-permute-start | bytes 4718600 | tf_op jit(solution)/shard_map/ppermute | solution.py:15
  91.6 95.6 %collective-permute-start.8 = (f32[384,1024]{1,0:T(8,128)S(1)}, f32[384,1024]{1,0:T(8,128)S(1)}, u32[]{:S(2)}, u32[]{:S(2)}) collective-permute-start(f32[384,1024]{1,0:T(8,128)S(1)} %get-tuple-element.113), channel_id=1, source_target_pairs={{2,0},{3,1},{4,2},{5,3},{6,4},{7,5},{8,6},{9,7},{10,8},{11,9},{12,... | collective-permute-start | bytes 4718600 | tf_op jit(solution)/shard_map/ppermute | solution.py:15
  92.9 122.5 %collective-permute-start.9 = (f32[384,1024]{1,0:T(8,128)S(1)}, f32[384,1024]{1,0:T(8,128)}, u32[]{:S(2)}, u32[]{:S(2)}) collective-permute-start(f32[384,1024]{1,0:T(8,128)S(1)} %get-tuple-element.112), channel_id=1, source_target_pairs={{0,2},{1,3},{2,4},{3,5},{4,6},{5,7},{6,8},{7,9},{8,10},{9,11},{10,... | collective-permute-start | bytes 4718600 | tf_op jit(solution)/shard_map/ppermute | solution.py:15
  99.7 120.0 %collective-permute-start.10 = (f32[256,1024]{1,0:T(8,128)S(1)}, f32[256,1024]{1,0:T(8,128)S(1)}, u32[]{:S(2)}, u32[]{:S(2)}) collective-permute-start(f32[256,1024]{1,0:T(8,128)S(1)} %get-tuple-element.110), channel_id=1, source_target_pairs={{3,0},{4,1},{5,2},{6,3},{7,4},{8,5},{9,6},{10,7},{11,8},{12,9},{13... | collective-permute-start | bytes 3145736 | tf_op jit(solution)/shard_map/ppermute | solution.py:15
  118.1 101.8 %collective-permute-start.11 = (f32[256,1024]{1,0:T(8,128)S(1)}, f32[256,1024]{1,0:T(8,128)S(1)}, u32[]{:S(2)}, u32[]{:S(2)}) collective-permute-start(f32[256,1024]{1,0:T(8,128)S(1)} %get-tuple-element.109), channel_id=1, source_target_pairs={{0,3},{1,4},{2,5},{3,6},{4,7},{5,8},{6,9},{7,10},{8,11},{9,12},{10... | collective-permute-start | bytes 3145736 | tf_op jit(solution)/shard_map/ppermute | solution.py:15
  219.9 1.1 copy-start.1
where the time goes:
time: 224 us; the launch traced here: 223 us
  waiting for transfers between devices  158 us (71%)
  starting transfers between devices  38 us (17%)
  matrix products  11.4 us (5%)
  local copies, waits for them, and re-layouts  8.58 us (4%)
  other arithmetic  6.25 us (3%)
    ppermute x12, waiting for transfers between devices, from_behind(): return lax.ppermute(x, axis, pairs)  158 us
    ppermute x12, starting transfers between devices, from_behind(): return lax.ppermute(x, axis, pairs)  38 us
  transfers between devices with their start and end apart: 12, of which 7 were waited for; matrix products, arithmetic and copies ran while one was open for 6% of the time, Pallas kernels for 0%

commit v1 on v0

v1 whole, which is shorter than its diff:
```python
import jax
import jax.numpy as jnp
from jax import lax
from jax.sharding import PartitionSpec as P

BAND = 1024
SCALE = 16.0
AXES = ("tm", "sub")


def shift(x, count, target):
    pairs = [(i, target(i)) for i in range(count) if 0 <= target(i) < count]
    return lax.ppermute(x, AXES, pairs)


def to_core(i):
    return i ^ 1


def to_pair(i):
    return i ^ 2


def to_cross(i):
    return i + 2 if i & 2 else i - 2


def to_far(i):
    return i + 3 if i & 1 else i - 3


def to_side(i):
    return i - 2 if i & 1 else i + 2


def per_device(embeddings, offsets, limits):
    rows = embeddings.shape[0]
    count = lax.axis_size(AXES)
    assert count % 4 == 0 and lax.axis_size("sub") % 2 == 0
    tail = BAND - 2 * rows
    assert 0 < tail <= rows
    device = lax.axis_index(AXES)
    core = device % 2
    chip = (device // 2) % 2
    frames = rows * count
    start_valid = limits[0]
    end_valid = frames - limits[1]
    arange = jnp.arange(rows, dtype=jnp.int32)
    own_index = device * rows + arange
    own_valid = (own_index >= start_valid) & (own_index < end_valid)
    forward = own_index + offsets
    positive = jnp.where(forward < end_valid, forward, own_index - offsets)

    pair = shift(embeddings, count, to_pair)
    cross = shift(embeddings, count, to_cross)
    far = shift(
        jnp.where(core == 1, embeddings[rows - tail :], embeddings[:tail]), count, to_far
    )
    mate = shift(embeddings, count, to_core)
    pair_mate = shift(pair, count, to_core)
    cross_mate = shift(cross, count, to_core)

    cross_step = jnp.where(chip == 1, 2, -2)
    mate_device = device ^ 1
    blocks = [
        (embeddings, device * rows),
        (mate, mate_device * rows),
        (pair, (device ^ 2) * rows),
        (pair_mate, (mate_device ^ 2) * rows),
        (far, jnp.where(core == 1, (device + 3) * rows, (device - 2) * rows - tail)),
        (cross, (device + cross_step) * rows),
        (cross_mate, (mate_device + cross_step) * rows),
    ]
    masked = []
    indices = []
    for block, base in blocks:
        index = base + jnp.arange(block.shape[0], dtype=jnp.int32)
        valid = (index >= start_valid) & (index < end_valid)
        spacing = own_index[:, None] - index[None, :]
        inside = (jnp.abs(spacing) <= BAND) & (spacing != 0)
        inside = inside & own_valid[:, None] & valid[None, :]
        scores = SCALE * jnp.einsum(
            "td,ud->tu", embeddings, block, preferred_element_type=jnp.float32
        )
        masked.append(jnp.where(inside, scores, -jnp.inf))
        indices.append(index)
    row_max = masked[0].max(axis=1)
    for part in masked[1:]:
        row_max = jnp.maximum(row_max, part.max(axis=1))
    row_max = jnp.where(own_valid, row_max, 0.0)
    totals = jnp.where(own_valid, 0.0, 1.0)
    for part in masked:
        totals = totals + jnp.sum(jnp.exp(part - row_max[:, None]), axis=1)
    log_sum = row_max + jnp.log(totals)

    own_positive = jnp.where(own_valid, positive, -1)
    note = jnp.stack([log_sum, own_positive.astype(jnp.float32)])
    mate_note = shift(note, count, to_core)
    side = shift(jnp.stack([note, mate_note]), count, to_side)
    far_note = shift(note, count, to_far)
    side, far_note = lax.optimization_barrier((side, far_note))
    other = shift(side, count, to_core)
    far_note = jnp.where(core == 1, far_note[:, :tail], far_note[:, rows - tail :])
    swap = core == chip
    pair_note = jnp.where(swap, other[1], side[0])
    pair_mate_note = jnp.where(swap, other[0], side[1])
    cross_note = jnp.where(swap, side[0], other[1])
    cross_mate_note = jnp.where(swap, side[1], other[0])
    notes = [note, mate_note, pair_note, pair_mate_note, far_note, cross_note, cross_mate_note]

    result = jnp.zeros(embeddings.shape, jnp.float32)
    for (block, _), part, index, their in zip(blocks, masked, indices, notes):
        hits = (index[None, :] == own_positive[:, None]).astype(jnp.float32)
        out_weight = (jnp.exp(part - log_sum[:, None]) - hits).astype(jnp.bfloat16)
        result = result + jnp.einsum(
            "tu,ud->td", out_weight, block, preferred_element_type=jnp.float32
        )
    for (block, _), part, index, their in zip(blocks, masked, indices, notes):
        back_hits = (their[1].astype(jnp.int32)[None, :] == own_index[:, None]).astype(jnp.float32)
        back_weight = (jnp.exp(part - their[0][None, :]) - back_hits).astype(jnp.bfloat16)
        result = result + jnp.einsum(
            "tu,ud->td", back_weight, block, preferred_element_type=jnp.float32
        )
    return SCALE * result


def solution(mesh):
    return jax.shard_map(
        per_device,
        mesh=mesh,
        in_specs=(P(("videos", "tm", "sub"), None), P(("videos", "tm", "sub")), P("videos")),
        out_specs=P(("videos", "tm", "sub"), None),
        check_vma=False,
    )
```

time: 224 us -> 68.4 us (0.31)
  waiting for transfers between devices: 158 us -> 21.1 us
  starting transfers between devices: 38 us -> 16.7 us
  local copies, waits for them, and re-layouts: 8.58 us -> 0.71 us
  matrix products: 11.4 us -> 19.1 us
    ppermute x12 -> x10, waiting for transfers between devices: 158 us -> 21.1 us  [shift(): return lax.ppermute(x, AXES, pairs)]
    ppermute x12 -> x10, starting transfers between devices: 38 us -> 16.7 us  [shift(): return lax.ppermute(x, AXES, pairs)]
    dot_general x3 -> x21, matrix products: 11.4 us -> 19.1 us  [the longest x7 7.78 us: per_device(): jnp.einsum('tu,ud->td', back_weight, block, preferred_element_type=jnp.fl...]
    unnamed x10 -> x6, local copies, waits for them, and re-layouts: 3.6 us -> 0.01 us
    slice x3 -> x5, local copies, waits for them, and re-layouts: 3.6 us -> 0.1 us  [per_device(): their[0][None, :]]
    and x2 -> x6, other arithmetic: 1.13 us -> 4.17 us  [per_device(): valid = (index >= start_valid) & (index < end_valid)]
    scatter-add x2 -> x0, other arithmetic: 2.65 us -> none  [the longest x1 2.38 us: per_device(): result = result.at[:length].add(incoming_late)]
  transfers between devices with their start and end apart: 12 -> 10, of which waited for: 7 -> 3; matrix products, arithmetic and copies ran while one was open for 6% -> 32% of each run, Pallas kernels for 0% -> 0%
where the time goes in v1:
time: 68.4 us; the launch traced here: 67.1 us
  waiting for transfers between devices  21.1 us (31%)
  matrix products  19.1 us (28%)
  starting transfers between devices  16.7 us (24%)
  other arithmetic  8.41 us (12%)
  between operations  1 us (1%)
  local copies, waits for them, and re-layouts  0.71 us (1%)
    ppermute x10, waiting for transfers between devices, shift(): return lax.ppermute(x, AXES, pairs)  21.1 us
    ppermute x10, starting transfers between devices, shift(): return lax.ppermute(x, AXES, pairs)  16.7 us
    dot_general x7, matrix products, per_device(): jnp.einsum('tu,ud->td', back_weight, block, preferred_element_type=jnp.fl...  7.78 us
    dot_general x7, matrix products, per_device(): jnp.einsum('tu,ud->td', out_weight, block, preferred_element_type=jnp.flo...  5.72 us
    dot_general x7, matrix products, per_device(): jnp.einsum('td,ud->tu', embeddings, block, preferred_element_type=jnp.flo...  5.56 us
    and x6, other arithmetic, per_device(): valid = (index >= start_valid) & (index < end_valid)  4.17 us
    select_n x1, other arithmetic, per_device(): jnp.where(core == 1, embeddings[rows - tail:], embeddings[:tail])  2.05 us
  transfers between devices with their start and end apart: 10, of which 3 were waited for; matrix products, arithmetic and copies ran while one was open for 32% of the time, Pallas kernels for 0%

profile of v1, /device:TPU:1, one launch (start us, length us, event | category | flops | bytes accessed | tf_op | source)
XLA Modules:
  0.0 67.1 jit_solution(6290796963123704363)
XLA Ops:
  0.0 0.0 copy-start
  0.0 0.0 copy-start.2
  0.0 0.0 copy-start.1
  0.0 0.8 %collective-permute-start.4 = (bf16[384,1024]{1,0:T(8,128)(2,1)}, bf16[384,1024]{1,0:T(8,128)(2,1)S(1)}, u32[]{:S(2)}, u32[]{:S(2)}) collective-permute-start(bf16[384,1024]{1,0:T(8,128)(2,1)} %param.3), channel_id=1, source_target_pairs={{2,4},{3,5},{4,2},{5,3},{6,8},{7,9},{8,6},{9,7},{10,12},{11,13},{1... | collective-permute-start | bytes 2359304 | tf_op jit(solution)/shard_map/ppermute | solution.py:13
  0.9 4.6 %collective-permute-start.1 = (bf16[384,1024]{1,0:T(8,128)(2,1)}, bf16[384,1024]{1,0:T(8,128)(2,1)S(1)}, u32[]{:S(2)}, u32[]{:S(2)}) collective-permute-start(bf16[384,1024]{1,0:T(8,128)(2,1)} %param.3), channel_id=1, source_target_pairs={{0,2},{1,3},{2,0},{3,1},{4,6},{5,7},{6,4},{7,5},{8,10},{9,11},{10,... | collective-permute-start | bytes 2359304 | tf_op jit(solution)/shard_map/ppermute | solution.py:13
  5.4 1.2 %collective-permute-start = (bf16[384,1024]{1,0:T(8,128)(2,1)}, bf16[384,1024]{1,0:T(8,128)(2,1)S(1)}, u32[]{:S(2)}, u32[]{:S(2)}) collective-permute-start(bf16[384,1024]{1,0:T(8,128)(2,1)} %param.3), channel_id=1, source_target_pairs={{0,1},{1,0},{2,3},{3,2},{4,5},{5,4},{6,7},{7,6},{8,9},{9,8},{10,11... | collective-permute-start | bytes 2359304 | tf_op jit(solution)/shard_map/ppermute | solution.py:13
  6.7 2.0 %slice_select_fusion = bf16[256,1024]{1,0:T(8,128)(2,1)} fusion(bf16[384,1024]{1,0:T(8,128)(2,1)} %param.3, pred[]{:T(512)S(6)} %eq.67), kind=kLoop, calls=%fused_computation.72 | loop fusion | flops 262144 | bytes 1572865 | tf_op jit(solution)/shard_map/jit(_where)/select_n | solution.py:57
  8.7 3.1 %collective-permute-start.3 = (bf16[256,1024]{1,0:T(8,128)(2,1)}, bf16[256,1024]{1,0:T(8,128)(2,1)}, u32[]{:S(2)}, u32[]{:S(2)}) collective-permute-start(bf16[256,1024]{1,0:T(8,128)(2,1)} %slice_select_fusion), channel_id=1, source_target_pairs={{1,4},{3,6},{4,1},{5,8},{6,3},{7,10},{8,5},{9,12},{10,7},{11,14},{... | collective-permute-start | bytes 1572872 | tf_op jit(solution)/shard_map/ppermute | solution.py:13
  11.9 0.0 copy-done.2
  11.9 0.6 fusion.104
  13.1 0.7 %compare_and_fusion.3 = pred[256]{0:T(512)(128)(4,1)S(1)} fusion(s32[]{:T(128)} %bitcast.1, s32[]{:T(128)} %bitcast, s32[]{:T(128)S(6)} %select_n.137), kind=kLoop, calls=%fused_computation.158 | loop fusion | flops 1024 | bytes 268 | tf_op jit(solution)/shard_map/and | solution.py:78
  13.8 0.7 %compare_and_fusion.1 = pred[384]{0:T(512)(128)(4,1)S(1)} fusion(s32[]{:T(128)} %bitcast.1, s32[]{:T(128)} %bitcast, s32[]{:T(128)S(6)} %mul.77), kind=kLoop, calls=%fused_computation.156 | loop fusion | flops 1536 | bytes 396 | tf_op jit(solution)/shard_map/and | solution.py:78
  14.5 0.7 %compare_and_fusion.2 = pred[384]{0:T(512)(128)(4,1)S(1)} fusion(s32[]{:T(128)} %bitcast.1, s32[]{:T(128)} %bitcast, s32[]{:T(128)S(6)} %mul.75), kind=kLoop, calls=%fused_computation.157 | loop fusion | flops 1536 | bytes 396 | tf_op jit(solution)/shard_map/and | solution.py:78
  15.2 0.7 %compare_and_fusion.4 = pred[384]{0:T(512)(128)(4,1)S(1)} fusion(s32[]{:T(128)} %bitcast.1, s32[]{:T(128)} %bitcast, s32[]{:T(128)S(6)} %mul.68), kind=kLoop, calls=%fused_computation.159 | loop fusion | flops 1536 | bytes 396 | tf_op jit(solution)/shard_map/and | solution.py:78
  15.9 0.7 %compare_and_fusion.6 = pred[384]{0:T(512)(128)(4,1)S(1)} fusion(s32[]{:T(128)} %bitcast.1, s32[]{:T(128)} %bitcast, s32[]{:T(128)S(6)} %mul.64), kind=kLoop, calls=%fused_computation.161 | loop fusion | flops 1536 | bytes 396 | tf_op jit(solution)/shard_map/and | solution.py:78
  16.6 0.0 copy-done.1
  16.6 0.7 %convert_convert_fusion = (s32[384]{0:T(512)S(1)}, s32[384]{0:T(512)S(1)}, pred[384]{0:T(512)(128)(4,1)S(1)}, s32[384]{0:T(512)S(1)}) fusion(s32[384]{0:T(512)S(1)} %copy-done.1, s32[]{:T(128)} %bitcast.1, s32[]{:T(128)S(6)} %mul.62, s32[]{:T(128)} %bitcast), kind=kLoop, calls=%fused_computation.182 | loop fusion | flops 4224 | bytes 6540 | tf_op jit(solution)/shard_map/convert_element_type | solution.py:119
  17.3 0.7 %compare_and_fusion.5 = pred[384]{0:T(512)(128)(4,1)S(1)} fusion(s32[]{:T(128)} %bitcast.1, s32[]{:T(128)} %bitcast, s32[]{:T(128)S(6)} %mul.66), kind=kLoop, calls=%fused_computation.160 | loop fusion | flops 1536 | bytes 396 | tf_op jit(solution)/shard_map/and | solution.py:78
  18.1 0.0 copy-done
  18.1 0.7 fusion.110
  18.8 10.3 %collective-permute-done.3 = bf16[256,1024]{1,0:T(8,128)(2,1)} collective-permute-done((bf16[256,1024]{1,0:T(8,128)(2,1)}, bf16[256,1024]{1,0:T(8,128)(2,1)}, u32[]{:S(2)}, u32[]{:S(2)}) %collective-permute-start.3) | collective-permute-done | bytes 524320 | tf_op jit(solution)/shard_map/ppermute | solution.py:13
  29.0 1.5 %fusion.107 = (f32[384]{0:T(512)S(1)}, f32[384,256]{0,1:T(8,128)S(1)}) fusion(bf16[256,1024]{1,0:T(8,128)(2,1)} %collective-permute-done.3, bf16[384,1024]{1,0:T(8,128)(2,1)S(1)} %copy-done, pred[256]{0:T(512)(128)(4,1)S(1)} %compare_and_fusion.3, pred[384]{0:T(512)(128)(4,1)S(1)} %get-tuple-element.17, s32[256]{0:T(256)S(1)} %iota_add_fusion.6, ...), kind=kOutput, calls=%fused_computation.187 | convolution fusion | flops 202309248 | bytes 1708672 | tf_op jit(solution)/shard_map/td,ud->tu/dot_general | solution.py:82
  30.6 0.0 collective-permute-done.4
  30.6 0.1 collective-permute-start.5
  30.6 8.8 %collective-permute-done.1 = bf16[384,1024]{1,0:T(8,128)(2,1)S(1)} collective-permute-done((bf16[384,1024]{1,0:T(8,128)(2,1)}, bf16[384,1024]{1,0:T(8,128)(2,1)S(1)}, u32[]{:S(2)}, u32[]{:S(2)}) %collective-permute-start.1) | collective-permute-done | bytes 786464 | tf_op jit(solution)/shard_map/ppermute | solution.py:13
  39.4 0.5 collective-permute-start.2
  39.9 0.7 fusion.106
  40.6 0.7 %fusion.109 = (f32[384]{0:T(512)S(1)}, f32[384,384]{0,1:T(8,128)S(1)}) fusion(bf16[384,1024]{1,0:T(8,128)(2,1)S(1)} %copy-done, bf16[384,1024]{1,0:T(8,128)(2,1)S(1)} %collective-permute-done.1, pred[384]{0:T(512)(128)(4,1)S(1)} %compare_and_fusion.5, pred[384]{0:T(512)(128)(4,1)S(1)} %get-tuple-element.17, s32[384]{0:T(512)S(1)} %iota_add_fusion.3, ...), kind=kOutput, calls=%fused_computation.189 | convolution fusion | flops 303464064 | bytes 2168064 | tf_op jit(solution)/shard_map/td,ud->tu/dot_general | solution.py:82
  41.2 0.0 collective-permute-done
  41.3 0.7 %fusion.111 = (f32[384]{0:T(512)S(1)}, f32[384,384]{0,1:T(8,128)S(1)}) fusion(bf16[384,1024]{1,0:T(8,128)(2,1)S(1)} %copy-done, bf16[384,1024]{1,0:T(8,128)(2,1)S(1)} %collective-permute-done, pred[384]{0:T(512)(128)(4,1)S(1)} %compare_and_fusion.6, pred[384]{0:T(512)(128)(4,1)S(1)} %get-tuple-element.17, s32[384]{0:T(512)S(1)} %iota_add_fusion.4, ...), kind=kOutput, calls=%fused_computation.191 | convolution fusion | flops 303464064 | bytes 2168064 | tf_op jit(solution)/shard_map/td,ud->tu/dot_general | solution.py:82
  41.9 0.0 collective-permute-done.5
  41.9 0.7 %fusion.105 = (f32[384]{0:T(512)S(1)}, f32[384,384]{0,1:T(8,128)S(1)}) fusion(bf16[384,1024]{1,0:T(8,128)(2,1)S(1)} %copy-done, bf16[384,1024]{1,0:T(8,128)(2,1)S(1)} %collective-permute-done.5, pred[384]{0:T(512)(128)(4,1)S(1)} %compare_and_fusion.1, pred[384]{0:T(512)(128)(4,1)S(1)} %get-tuple-element.17, s32[384]{0:T(512)S(1)} %iota_add_fusion, ...), kind=kOutput, calls=%fused_computation.185 | convolution fusion | flops 303464064 | bytes 2168064 | tf_op jit(solution)/shard_map/td,ud->tu/dot_general | solution.py:82
  42.6 0.0 collective-permute-done.2
  42.6 0.7 %fusion.108 = (f32[384]{0:T(512)S(1)}, f32[384,384]{0,1:T(8,128)S(1)}) fusion(bf16[384,1024]{1,0:T(8,128)(2,1)S(1)} %copy-done, bf16[384,1024]{1,0:T(8,128)(2,1)S(1)} %collective-permute-done.2, pred[384]{0:T(512)(128)(4,1)S(1)} %compare_and_fusion.4, pred[384]{0:T(512)(128)(4,1)S(1)} %get-tuple-element.17, s32[384]{0:T(512)S(1)} %iota_add_fusion.2, ...), kind=kOutput, calls=%fused_computation.188 | convolution fusion | flops 303464064 | bytes 2168064 | tf_op jit(solution)/shard_map/td,ud->tu/dot_general | solution.py:82
  43.3 0.1 exponential_reduce_fusion.6
  43.4 0.5 exponential_reduce_fusion.5
  43.9 0.7 %fusion.100 = f32[1,384]{1,0:T(1,128)S(1)} fusion(f32[384]{0:T(512)S(1)} %get-tuple-element.19, f32[384]{0:T(512)S(1)} %get-tuple-element.13, f32[384]{0:T(512)S(1)} %get-tuple-element.12, f32[384]{0:T(512)S(1)} %exponential_reduce_fusion.6, f32[384]{0:T(512)S(1)} %get-tuple-element.11, f32[384]{0:T(512)S(1)} %get-tuple-element.10, ...), kind=kLoop, calls=%fused_computation.178 | loop fusion | flops 5376 | bytes 13836 | tf_op jit(solution)/shard_map/add | solution.py:94
  44.7 4.0 %collective-permute-start.8 = (f32[2,384]{1,0:T(2,128)S(1)}, f32[2,384]{1,0:T(2,128)S(1)}, u32[]{:S(2)}, u32[]{:S(2)}) collective-permute-start(f32[2,384]{1,0:T(2,128)S(1)} %get-tuple-element.25), channel_id=1, source_target_pairs={{1,4},{3,6},{4,1},{5,8},{6,3},{7,10},{8,5},{9,12},{10,7},{11,14},{... | collective-permute-start | bytes 9224 | tf_op jit(solution)/shard_map/ppermute | solution.py:13
  48.7 0.1 collective-permute-start.6
  48.8 0.7 %fusion.36 = f32[384,1024]{1,0:T(8,128)S(1)} fusion(bf16[384,1024]{1,0:T(8,128)(2,1)S(1)} %copy-done, f32[384,384]{0,1:T(8,128)S(1)} %get-tuple-element.41, s32[384]{0:T(512)S(1)} %get-tuple-element.16, f32[384]{0:T(512)S(1)} %log_add_fusion, s32[384]{0:T(512)S(1)} %get-tuple-element.44), kind=kOutput, calls=%fused_computation.80 | convolution fusion | flops 302727168 | bytes 2953728 | tf_op jit(solution)/shard_map/tu,ud->td/dot_general | solution.py:115
  49.5 0.7 %fusion.42 = f32[384,1024]{1,0:T(8,128)S(1)} fusion(bf16[384,1024]{1,0:T(8,128)(2,1)S(1)} %copy-done, f32[384,384]{0,1:T(8,128)S(1)} %get-tuple-element.41, f32[384]{0:T(512)S(1)} %log_add_fusion, s32[384]{0:T(512)S(1)} %get-tuple-element.44, s32[384]{0:T(512)S(1)} %get-tuple-element.15), kind=kOutput, calls=%fused_computation.86 | convolution fusion | flops 302727168 | bytes 2953728 | tf_op jit(solution)/shard_map/tu,ud->td/dot_general | solution.py:121
  50.2 0.7 %fusion.38 = f32[384,1024]{1,0:T(8,128)S(1)} fusion(bf16[384,1024]{1,0:T(8,128)(2,1)S(1)} %collective-permute-done.1, f32[384,384]{0,1:T(8,128)S(1)} %get-tuple-element.39, s32[384]{0:T(512)S(1)} %get-tuple-element.16, f32[384]{0:T(512)S(1)} %log_add_fusion, s32[384]{0:T(512)S(1)} %iota_add_fusion.3), kind=kOutput, calls=%fused_computation.82 | convolution fusion | flops 302727168 | bytes 2953728 | tf_op jit(solution)/shard_map/tu,ud->td/dot_general | solution.py:115
  50.9 0.7 %fusion.40 = f32[384,1024]{1,0:T(8,128)S(1)} fusion(bf16[384,1024]{1,0:T(8,128)(2,1)S(1)} %collective-permute-done.4, f32[384,384]{0,1:T(8,128)S(1)} %get-tuple-element.33, s32[384]{0:T(512)S(1)} %get-tuple-element.16, f32[384]{0:T(512)S(1)} %log_add_fusion, s32[384]{0:T(512)S(1)} %iota_add_fusion.1), kind=kOutput, calls=%fused_computation.84 | convolution fusion | flops 302727168 | bytes 2953728 | tf_op jit(solution)/shard_map/tu,ud->td/dot_general | solution.py:115
  51.6 0.7 %fusion.39 = f32[384,1024]{1,0:T(8,128)S(1)} fusion(bf16[384,1024]{1,0:T(8,128)(2,1)S(1)} %collective-permute-done.2, f32[384,384]{0,1:T(8,128)S(1)} %get-tuple-element.37, s32[384]{0:T(512)S(1)} %get-tuple-element.16, f32[384]{0:T(512)S(1)} %log_add_fusion, s32[384]{0:T(512)S(1)} %iota_add_fusion.2), kind=kOutput, calls=%fused_computation.83 | convolution fusion | flops 302727168 | bytes 2953728 | tf_op jit(solution)/shard_map/tu,ud->td/dot_general | solution.py:115
  52.3 0.7 %fusion.37 = f32[384,1024]{1,0:T(8,128)S(1)} fusion(bf16[384,1024]{1,0:T(8,128)(2,1)S(1)} %collective-permute-done, f32[384,384]{0,1:T(8,128)S(1)} %get-tuple-element.43, s32[384]{0:T(512)S(1)} %get-tuple-element.16, f32[384]{0:T(512)S(1)} %log_add_fusion, s32[384]{0:T(512)S(1)} %iota_add_fusion.4), kind=kOutput, calls=%fused_computation.81 | convolution fusion | flops 302727168 | bytes 2953728 | tf_op jit(solution)/shard_map/tu,ud->td/dot_general | solution.py:115
  53.0 0.7 %fusion.41 = f32[384,1024]{1,0:T(8,128)S(1)} fusion(bf16[384,1024]{1,0:T(8,128)(2,1)S(1)} %collective-permute-done.5, f32[384,384]{0,1:T(8,128)S(1)} %get-tuple-element.31, s32[384]{0:T(512)S(1)} %get-tuple-element.16, f32[384]{0:T(512)S(1)} %log_add_fusion, s32[384]{0:T(512)S(1)} %iota_add_fusion), kind=kOutput, calls=%fused_computation.85 | convolution fusion | flops 302727168 | bytes 2953728 | tf_op jit(solution)/shard_map/tu,ud->td/dot_general | solution.py:115
  53.7 1.5 %fusion.83 = f32[384,1024]{1,0:T(8,128)S(1)} fusion(bf16[256,1024]{1,0:T(8,128)(2,1)} %collective-permute-done.3, f32[384,256]{0,1:T(8,128)S(1)} %get-tuple-element.35, s32[384]{0:T(512)S(1)} %get-tuple-element.16, f32[384]{0:T(512)S(1)} %log_add_fusion, s32[256]{0:T(256)S(1)} %iota_add_fusion.6), kind=kOutput, calls=%fused_computation.127 | convolution fusion | flops 201818112 | bytes 2494464 | tf_op jit(solution)/shard_map/tu,ud->td/dot_general | solution.py:115
  55.2 0.0 collective-permute-done.6
  55.3 1.5 %collective-permute-start.7 = (f32[2,2,384]{2,1,0:T(2,128)S(1)}, f32[2,2,384]{2,1,0:T(2,128)S(1)}, u32[]{:S(2)}, u32[]{:S(2)}) collective-permute-start(f32[2,2,384]{2,1,0:T(2,128)S(1)} %pad_maximum_fusion), channel_id=1, source_target_pairs={{0,2},{2,4},{3,1},{4,6},{5,3},{6,8},{7,5},{8,10},{9,7},{10,12},{11... | collective-permute-start | bytes 18440 | tf_op jit(solution)/shard_map/ppermute | solution.py:13
  56.8 0.7 %fusion.43 = f32[384,1024]{1,0:T(8,128)S(1)} fusion(bf16[384,1024]{1,0:T(8,128)(2,1)S(1)} %collective-permute-done, f32[384,384]{0,1:T(8,128)S(1)} %get-tuple-element.43, f32[384]{0:T(512)S(1)} %slice_reduce_fusion.4, s32[384]{0:T(512)S(1)} %get-tuple-element.44, s32[384]{0:T(512)S(1)} %fusion.99), kind=kOutput, calls=%fused_computation.87 | convolution fusion | flops 302727168 | bytes 2953728 | tf_op jit(solution)/shard_map/tu,ud->td/dot_general | solution.py:121
  57.5 0.0 collective-permute-done.8
  57.5 2.1 %collective-permute-done.7 = f32[2,2,384]{2,1,0:T(2,128)S(1)} collective-permute-done((f32[2,2,384]{2,1,0:T(2,128)S(1)}, f32[2,2,384]{2,1,0:T(2,128)S(1)}, u32[]{:S(2)}, u32[]{:S(2)}) %collective-permute-start.7) | collective-permute-done | bytes 6176 | tf_op jit(solution)/shard_map/ppermute | solution.py:13
  59.7 0.9 %collective-permute-start.9 = (f32[2,2,384]{2,1,0:T(2,128)S(1)}, f32[2,2,384]{2,1,0:T(2,128)S(1)}, u32[]{:S(2)}, u32[]{:S(2)}) collective-permute-start(f32[2,2,384]{2,1,0:T(2,128)S(1)} %collective-permute-done.7), channel_id=1, source_target_pairs={{0,1},{1,0},{2,3},{3,2},{4,5},{5,4},{6,7},{7,6},{8,9},{9,8},{10,11... | collective-permute-start | bytes 18440 | tf_op jit(solution)/shard_map/ppermute | solution.py:13
  60.6 1.6 %fusion.84 = f32[384,1024]{1,0:T(8,128)S(1)} fusion(bf16[256,1024]{1,0:T(8,128)(2,1)} %collective-permute-done.3, f32[384,256]{0,1:T(8,128)S(1)} %get-tuple-element.35, f32[256]{0:T(256)S(1)} %bitcast.41, s32[384]{0:T(512)S(1)} %get-tuple-element.44, s32[256]{0:T(256)S(1)} %bitcast.40), kind=kOutput, calls=%fused_computation.128 | convolution fusion | flops 201818112 | bytes 2493952 | tf_op jit(solution)/shard_map/tu,ud->td/dot_general | solution.py:121
  62.1 0.0 collective-permute-done.9
  62.3 0.7 %fusion.44 = f32[384,1024]{1,0:T(8,128)S(1)} fusion(bf16[384,1024]{1,0:T(8,128)(2,1)S(1)} %collective-permute-done.1, f32[384,384]{0,1:T(8,128)S(1)} %get-tuple-element.39, f32[384]{0:T(512)S(1)} %slice_reduce_fusion.3, s32[384]{0:T(512)S(1)} %get-tuple-element.44, s32[384]{0:T(512)S(1)} %fusion.98), kind=kOutput, calls=%fused_computation.88 | convolution fusion | flops 302727168 | bytes 2953728 | tf_op jit(solution)/shard_map/tu,ud->td/dot_general | solution.py:121
  63.1 0.7 %fusion.46 = f32[384,1024]{1,0:T(8,128)S(1)} fusion(bf16[384,1024]{1,0:T(8,128)(2,1)S(1)} %collective-permute-done.4, f32[384,384]{0,1:T(8,128)S(1)} %get-tuple-element.33, f32[384]{0:T(512)S(1)} %slice_reduce_fusion.1, s32[384]{0:T(512)S(1)} %get-tuple-element.44, s32[384]{0:T(512)S(1)} %fusion.96), kind=kOutput, calls=%fused_computation.90 | convolution fusion | flops 302727168 | bytes 2953728 | tf_op jit(solution)/shard_map/tu,ud->td/dot_general | solution.py:121
  63.8 0.7 %fusion.45 = f32[384,1024]{1,0:T(8,128)S(1)} fusion(bf16[384,1024]{1,0:T(8,128)(2,1)S(1)} %collective-permute-done.2, f32[384,384]{0,1:T(8,128)S(1)} %get-tuple-element.37, f32[384]{0:T(512)S(1)} %slice_reduce_fusion.2, s32[384]{0:T(512)S(1)} %get-tuple-element.44, s32[384]{0:T(512)S(1)} %fusion.97), kind=kOutput, calls=%fused_computation.89 | convolution fusion | flops 302727168 | bytes 2953728 | tf_op jit(solution)/shard_map/tu,ud->td/dot_general | solution.py:121
  64.5 2.5 %add_multiply_fusion = f32[384,1024]{1,0:T(8,128)} fusion(f32[384,1024]{1,0:T(8,128)S(1)} %fusion.46, f32[384,1024]{1,0:T(8,128)S(1)} %fusion.84, f32[384,1024]{1,0:T(8,128)S(1)} %fusion.45, f32[384,1024]{1,0:T(8,128)S(1)} %fusion.44, f32[384,1024]{1,0:T(8,128)S(1)} %fusion.43, f32[384,1024]{1,0:T(8,128)S(1)} %fusion.42, f32[384,1024]{1,0:T(8,128)S(1)} %fusion.41, ...), kind=kOutput, calls=%fused_computation | convolution fusion | flops 308232192 | bytes 23400960 | tf_op jit(solution)/shard_map/tu,ud->td/dot_general | solution.py:121
  (25 shorter events, 0.3 us)
Async XLA Ops:
  0.0 18.1 %copy-start = (bf16[384,1024]{1,0:T(8,128)(2,1)S(1)}, bf16[384,1024]{1,0:T(8,128)(2,1)}, u32[]{:S(2)}) copy-start(bf16[384,1024]{1,0:T(8,128)(2,1)} %param.3) | copy-start | bytes 2359300
  0.0 11.9 %copy-start.2 = (s32[2]{0:T(128)S(1)}, s32[2]{0:T(128)}, u32[]{:S(2)}) copy-start(s32[2]{0:T(128)} %param.5) | copy-start | bytes 28
  0.0 16.6 %copy-start.1 = (s32[384]{0:T(512)S(1)}, s32[384]{0:T(512)}, u32[]{:S(2)}) copy-start(s32[384]{0:T(512)} %param.4) | copy-start | bytes 4612
  0.0 30.5 %collective-permute-start.4 = (bf16[384,1024]{1,0:T(8,128)(2,1)}, bf16[384,1024]{1,0:T(8,128)(2,1)S(1)}, u32[]{:S(2)}, u32[]{:S(2)}) collective-permute-start(bf16[384,1024]{1,0:T(8,128)(2,1)} %param.3), channel_id=1, source_target_pairs={{2,4},{3,5},{4,2},{5,3},{6,8},{7,9},{8,6},{9,7},{10,12},{11,13},{1... | collective-permute-start | bytes 2359304 | tf_op jit(solution)/shard_map/ppermute | solution.py:13
  0.9 38.5 %collective-permute-start.1 = (bf16[384,1024]{1,0:T(8,128)(2,1)}, bf16[384,1024]{1,0:T(8,128)(2,1)S(1)}, u32[]{:S(2)}, u32[]{:S(2)}) collective-permute-start(bf16[384,1024]{1,0:T(8,128)(2,1)} %param.3), channel_id=1, source_target_pairs={{0,2},{1,3},{2,0},{3,1},{4,6},{5,7},{6,4},{7,5},{8,10},{9,11},{10,... | collective-permute-start | bytes 2359304 | tf_op jit(solution)/shard_map/ppermute | solution.py:13
  5.4 35.8 %collective-permute-start = (bf16[384,1024]{1,0:T(8,128)(2,1)}, bf16[384,1024]{1,0:T(8,128)(2,1)S(1)}, u32[]{:S(2)}, u32[]{:S(2)}) collective-permute-start(bf16[384,1024]{1,0:T(8,128)(2,1)} %param.3), channel_id=1, source_target_pairs={{0,1},{1,0},{2,3},{3,2},{4,5},{5,4},{6,7},{7,6},{8,9},{9,8},{10,11... | collective-permute-start | bytes 2359304 | tf_op jit(solution)/shard_map/ppermute | solution.py:13
  8.7 20.3 %collective-permute-start.3 = (bf16[256,1024]{1,0:T(8,128)(2,1)}, bf16[256,1024]{1,0:T(8,128)(2,1)}, u32[]{:S(2)}, u32[]{:S(2)}) collective-permute-start(bf16[256,1024]{1,0:T(8,128)(2,1)} %slice_select_fusion), channel_id=1, source_target_pairs={{1,4},{3,6},{4,1},{5,8},{6,3},{7,10},{8,5},{9,12},{10,7},{11,14},{... | collective-permute-start | bytes 1572872 | tf_op jit(solution)/shard_map/ppermute | solution.py:13
  30.6 11.4 %collective-permute-start.5 = (bf16[384,1024]{1,0:T(8,128)(2,1)S(1)}, bf16[384,1024]{1,0:T(8,128)(2,1)S(1)}, u32[]{:S(2)}, u32[]{:S(2)}) collective-permute-start(bf16[384,1024]{1,0:T(8,128)(2,1)S(1)} %collective-permute-done.4), channel_id=1, source_target_pairs={{0,1},{1,0},{2,3},{3,2},{4,5},{5,4},{6,7},{7,6},{8,9},{9,8},{10,11... | collective-permute-start | bytes 2359304 | tf_op jit(solution)/shard_map/ppermute | solution.py:13
  39.4 3.2 %collective-permute-start.2 = (bf16[384,1024]{1,0:T(8,128)(2,1)S(1)}, bf16[384,1024]{1,0:T(8,128)(2,1)S(1)}, u32[]{:S(2)}, u32[]{:S(2)}) collective-permute-start(bf16[384,1024]{1,0:T(8,128)(2,1)S(1)} %collective-permute-done.1), channel_id=1, source_target_pairs={{0,1},{1,0},{2,3},{3,2},{4,5},{5,4},{6,7},{7,6},{8,9},{9,8},{10,11... | collective-permute-start | bytes 2359304 | tf_op jit(solution)/shard_map/ppermute | solution.py:13
  44.7 12.9 %collective-permute-start.8 = (f32[2,384]{1,0:T(2,128)S(1)}, f32[2,384]{1,0:T(2,128)S(1)}, u32[]{:S(2)}, u32[]{:S(2)}) collective-permute-start(f32[2,384]{1,0:T(2,128)S(1)} %get-tuple-element.25), channel_id=1, source_target_pairs={{1,4},{3,6},{4,1},{5,8},{6,3},{7,10},{8,5},{9,12},{10,7},{11,14},{... | collective-permute-start | bytes 9224 | tf_op jit(solution)/shard_map/ppermute | solution.py:13
  48.7 6.6 %collective-permute-start.6 = (f32[2,384]{1,0:T(2,128)S(1)}, f32[2,384]{1,0:T(2,128)S(1)}, u32[]{:S(2)}, u32[]{:S(2)}) collective-permute-start(f32[2,384]{1,0:T(2,128)S(1)} %get-tuple-element.25), channel_id=1, source_target_pairs={{0,1},{1,0},{2,3},{3,2},{4,5},{5,4},{6,7},{7,6},{8,9},{9,8},{10,11... | collective-permute-start | bytes 9224 | tf_op jit(solution)/shard_map/ppermute | solution.py:13
  55.3 4.4 %collective-permute-start.7 = (f32[2,2,384]{2,1,0:T(2,128)S(1)}, f32[2,2,384]{2,1,0:T(2,128)S(1)}, u32[]{:S(2)}, u32[]{:S(2)}) collective-permute-start(f32[2,2,384]{2,1,0:T(2,128)S(1)} %pad_maximum_fusion), channel_id=1, source_target_pairs={{0,2},{2,4},{3,1},{4,6},{5,3},{6,8},{7,5},{8,10},{9,7},{10,12},{11... | collective-permute-start | bytes 18440 | tf_op jit(solution)/shard_map/ppermute | solution.py:13
  59.7 2.5 %collective-permute-start.9 = (f32[2,2,384]{2,1,0:T(2,128)S(1)}, f32[2,2,384]{2,1,0:T(2,128)S(1)}, u32[]{:S(2)}, u32[]{:S(2)}) collective-permute-start(f32[2,2,384]{2,1,0:T(2,128)S(1)} %collective-permute-done.7), channel_id=1, source_target_pairs={{0,1},{1,0},{2,3},{3,2},{4,5},{5,4},{6,7},{7,6},{8,9},{9,8},{10,11... | collective-permute-start | bytes 18440 | tf_op jit(solution)/shard_map/ppermute | solution.py:13

commit v2 on v1

v2 whole, which is shorter than its diff:
```python
import functools

import jax
import jax.numpy as jnp
from jax import lax
from jax.experimental import pallas as pl
from jax.experimental.pallas import tpu as pltpu
from jax.sharding import PartitionSpec as P

BAND = 1024
SCALE = 16.0
AXES = ("tm", "sub")
NOWHERE = 1 << 29
LANES = 128
COST = 0
VMEM = pl.BlockSpec(memory_space=pltpu.VMEM)
PARAMS = pltpu.CompilerParams(vmem_limit_bytes=16 << 20)


def shift(x, count, target):
    pairs = [(i, target(i)) for i in range(count) if 0 <= target(i) < count]
    return lax.ppermute(x, AXES, pairs)


def after(x, *others):
    return lax.optimization_barrier((x, *others))[0]


def to_core(i):
    return i ^ 1


def to_pair(i):
    return i ^ 2


def to_cross(i):
    return i + 2 if i & 2 else i - 2


def to_next(i):
    return i - 4 if i & 2 else i + 4


def to_far(i):
    return i + 3 if i & 1 else i - 3


def to_side(i):
    return i - 2 if i & 1 else i + 2


def is_second(axis_index, bit):
    return lax.rem(axis_index // bit, 2)


def parts_kernel(own_ref, head_ref, rest_ref, tail_ref, sems):
    split, tail = head_ref.shape[0], tail_ref.shape[0]
    core = is_second(lax.axis_index("sub"), 1)
    first = pl.multiple_of(core * (own_ref.shape[0] - tail), 16)
    copies = [
        pltpu.make_async_copy(own_ref.at[pl.ds(0, split)], head_ref, sems.at[0]),
        pltpu.make_async_copy(own_ref.at[pl.ds(split, own_ref.shape[0] - split)], rest_ref, sems.at[1]),
        pltpu.make_async_copy(own_ref.at[pl.ds(first, tail)], tail_ref, sems.at[2]),
    ]
    for copy in copies:
        copy.start()
    for copy in copies:
        copy.wait()


def parts_of(own, split, tail):
    rows, depth = own.shape
    return pl.pallas_call(
        parts_kernel,
        out_shape=[pltpu.VMEM((size, depth), own.dtype) for size in (split, rows - split, tail)],
        in_specs=[pl.BlockSpec(memory_space=pl.ANY)],
        out_specs=[VMEM] * 3,
        scratch_shapes=[pltpu.SemaphoreType.DMA((3,))],
        compiler_params=PARAMS,
        name="parts",
    )(pltpu.with_memory_space_constraint(own, pltpu.HBM))


def score_kernel(sizes, low, first, last, *refs):
    blocks = refs[: len(sizes)]
    column_ref, row_ref = refs[len(sizes) : len(sizes) + 2]
    refs = refs[len(sizes) + 2 :]
    if first:
        own = blocks[0][...]
    else:
        own = refs[0][...]
        old_peak, old_total = refs[1][:, :1], refs[2][:, :1]
        refs = refs[3:]
    window_ref, score_ref = refs[:2]
    rows = column_ref.shape[0]
    high = low + sum(sizes)
    block = jnp.concatenate([ref[...] for ref in blocks], axis=0)
    scores = SCALE * lax.dot_general(
        own, block, (((1,), (1,)), ((), ())), preferred_element_type=jnp.float32
    )
    spacing = column_ref[...] - row_ref[:, low:high]
    inside = jnp.abs(spacing) <= BAND
    if first:
        inside = inside & (spacing != 0)
    masked = jnp.where(inside, scores, -jnp.inf)
    score_ref[...] = masked
    peak = jnp.max(masked, axis=1, keepdims=True)
    if first:
        own_valid = column_ref[...] >= 0
        peak = jnp.where(own_valid, peak, 0.0)
    else:
        peak = jnp.maximum(peak, old_peak)
    total = jnp.sum(jnp.exp(score_ref[...] - peak), axis=1, keepdims=True)
    if first:
        total = total + jnp.where(own_valid, 0.0, 1.0)
    else:
        total = total + old_total * jnp.exp(old_peak - peak)
    window_ref[...] = block
    if last:
        log_ref, note_ref = refs[2:]
        log_sum = jnp.broadcast_to(peak + jnp.log(total), (rows, LANES))
        log_ref[...] = log_sum
        note_ref[...] = log_sum.T[:1]
    else:
        peak_ref, total_ref = refs[2:]
        peak_ref[...] = jnp.broadcast_to(peak, (rows, LANES))
        total_ref[...] = jnp.broadcast_to(total, (rows, LANES))


def scores_of(low, blocks, own, column, row, state, last):
    rows, depth = own.shape
    sizes = tuple(block.shape[0] for block in blocks)
    width = sum(sizes)
    first = state is None
    wide = jax.ShapeDtypeStruct((rows, LANES), jnp.float32)
    shapes = [
        jax.ShapeDtypeStruct((width, depth), jnp.bfloat16),
        jax.ShapeDtypeStruct((rows, width), jnp.float32),
        wide,
        jax.ShapeDtypeStruct((1, rows), jnp.float32) if last else wide,
    ]
    operands = (*blocks, column, row)
    if not first:
        operands = (*operands, own, *state)
    window, scores, *state = pl.pallas_call(
        functools.partial(score_kernel, sizes, low, first, last),
        out_shape=shapes,
        in_specs=[VMEM] * len(operands),
        out_specs=[VMEM] * len(shapes),
        compiler_params=PARAMS,
        cost_estimate=pl.CostEstimate(
            flops=COST * 2 * rows * width * depth // 100, bytes_accessed=COST * width * 40, transcendentals=0
        ),
        name="scores_last" if last else ("scores_first" if first else "scores_next"),
    )(*operands)
    return window, scores, state


def product_kernel(count, split, tail, *refs):
    windows, scores = refs[:count], refs[count : 2 * count]
    column_ref, positive_ref, log_ref, row_ref, own_note, mate_note, far_note, side_ref, other_ref, out_ref = refs[2 * count :]
    rows = column_ref.shape[0]
    core = is_second(lax.axis_index("sub"), 1)
    swap = core == is_second(lax.axis_index("sub"), 2)
    pair = jnp.where(swap, other_ref[1], side_ref[0])
    pair_mate = jnp.where(swap, other_ref[0], side_ref[1])
    cross = jnp.where(swap, side_ref[0], other_ref[1])
    cross_mate = jnp.where(swap, side_ref[1], other_ref[0])
    far = jnp.where(core == 1, far_note[:, :tail], far_note[:, rows - tail :])
    notes = jnp.concatenate(
        [
            own_note[...], mate_note[...], far, pair[:, :split], pair_mate[:, :split],
            pair[:, split:], pair_mate[:, split:], cross[:, split:], cross_mate[:, split:],
            cross[:, :split], cross_mate[:, :split],
        ],
        axis=1,
    )
    log_sum, positive = log_ref[:, :1], positive_ref[...]
    frame = column_ref[...].astype(jnp.float32)
    weights = []
    low = 0
    for ref in scores:
        high = low + ref.shape[1]
        score = ref[...]
        hit = jnp.where(row_ref[:, low:high] == positive, 1.0, 0.0)
        back_hit = jnp.where(notes[1:, low:high] == frame, 1.0, 0.0)
        weight = (jnp.exp(score - log_sum) - hit) + (jnp.exp(score - notes[:1, low:high]) - back_hit)
        weights.append(weight.astype(jnp.bfloat16))
        low = high
    weights = jnp.concatenate(weights, axis=1)
    step = 256
    for low in range(0, out_ref.shape[1], step):
        block = jnp.concatenate([ref[:, low : low + step] for ref in windows], axis=0)
        out_ref[:, low : low + step] = SCALE * jnp.dot(weights, block, preferred_element_type=jnp.float32)


def product_of(windows, scores, split, tail, *extra):
    rows, depth = scores[0].shape[0], windows[0].shape[1]
    operands = (*windows, *scores, *extra)
    return pl.pallas_call(
        functools.partial(product_kernel, len(windows), split, tail),
        out_shape=jax.ShapeDtypeStruct((rows, depth), jnp.float32),
        in_specs=[VMEM] * len(operands),
        out_specs=VMEM,
        compiler_params=PARAMS,
        name="product",
    )(*operands)


def per_device(embeddings, offsets, limits):
    rows, depth = embeddings.shape
    count = lax.axis_size(AXES)
    assert count % 4 == 0 and lax.axis_size("sub") % 2 == 0
    tail = BAND - 2 * rows
    split = 2 * rows // 3
    assert 0 < tail <= rows and split % 16 == 0
    device = lax.axis_index(AXES)
    core = device % 2
    chip = (device // 2) % 2
    frames = rows * count
    start_valid = limits[0]
    end_valid = frames - limits[1]

    head, rest, tail_rows = parts_of(embeddings, split, tail)
    mate = shift(embeddings, count, to_core)
    pair_head = shift(head, count, to_pair)
    far = shift(after(tail_rows, mate), count, to_far)
    pair_rest = shift(after(rest, mate), count, to_pair)
    cross_rest = shift(after(rest, mate), count, to_cross)

    mate_device = device ^ 1
    cross = (device + jnp.where(chip == 1, 2, -2)) * rows
    cross_mate = (mate_device + jnp.where(chip == 1, 2, -2)) * rows
    far_base = jnp.where(core == 1, (device + 3) * rows, (device - 2) * rows - tail)
    pair, pair_mate = (device ^ 2) * rows, (mate_device ^ 2) * rows
    places = [
        (device * rows, rows), (mate_device * rows, rows), (far_base, tail),
        (pair, split), (pair_mate, split), (pair + split, rows - split), (pair_mate + split, rows - split),
        (cross + split, rows - split), (cross_mate + split, rows - split), (cross, split), (cross_mate, split),
    ]
    row = jnp.concatenate([base + jnp.arange(size, dtype=jnp.int32) for base, size in places])[None]
    row = jnp.where((row >= start_valid) & (row < end_valid), row, NOWHERE)
    own_index = device * rows + jnp.arange(rows, dtype=jnp.int32)
    own_valid = (own_index >= start_valid) & (own_index < end_valid)
    column = jnp.where(own_valid, own_index, -NOWHERE)[:, None]
    forward = own_index + offsets
    positive = jnp.where(forward < end_valid, forward, own_index - offsets)
    positive = jnp.where(own_valid, positive, -1)

    windows, scores = [], []

    def score(blocks, state, last=False):
        low = sum(window.shape[0] for window in windows)
        window, score, state = scores_of(low, blocks, embeddings, column, row, state, last)
        windows.append(window)
        scores.append(score)
        return state

    state = score([embeddings, mate], None)
    cross_head = shift(after(pair_head, far), count, to_next)
    pair_mate_head = shift(after(pair_head, far), count, to_core)
    state = score([far, pair_head, pair_mate_head], state)
    pair_mate_rest = shift(after(pair_rest, state[0]), count, to_core)
    cross_mate_rest = shift(cross_rest, count, to_core)
    state = score([pair_rest, pair_mate_rest, cross_rest, cross_mate_rest], state)
    cross_mate_head = shift(after(cross_head, state[0]), count, to_core)
    log_sum, log_row = score([cross_head, cross_mate_head], state, True)

    note = jnp.concatenate([log_row, positive.astype(jnp.float32)[None]])
    mate_note = shift(note, count, to_core)
    side = shift(jnp.stack([note, mate_note]), count, to_side)
    far_note = shift(note, count, to_far)
    side, far_note = lax.optimization_barrier((side, far_note))
    other = shift(side, count, to_core)
    return product_of(
        windows, scores, split, tail,
        column, positive[:, None], log_sum, row, note, mate_note, far_note, side, other,
    )


def solution(mesh):
    return jax.shard_map(
        per_device,
        mesh=mesh,
        in_specs=(P(("videos", "tm", "sub"), None), P(("videos", "tm", "sub")), P("videos")),
        out_specs=P(("videos", "tm", "sub"), None),
        check_vma=False,
    )
```

time: 68.4 us -> 53.4 us (0.78)
  the two profiles are of different devices: /device:TPU:1 before, /device:TPU:19 now
where the time goes in v2:
time: 53.4 us; the launch traced here: 53.1 us
  starting transfers between devices  22.5 us (42%)
  waiting for transfers between devices  14.3 us (27%)
  Pallas kernels  11.2 us (21%)
  other arithmetic  2.79 us (5%)
  local copies, waits for them, and re-layouts  1.51 us (3%)
  between operations  0.84 us (2%)
    ppermute x14, starting transfers between devices, shift(): return lax.ppermute(x, AXES, pairs)  22.5 us
    ppermute x14, waiting for transfers between devices, shift(): return lax.ppermute(x, AXES, pairs)  14.3 us
    pallas_call x4, Pallas kernels, scores_of(): pl.pallas_call(functools.partial(score_kernel, sizes, low, first, last),...  5.61 us
    pallas_call x1, Pallas kernels, product_of(): pl.pallas_call(functools.partial(product_kernel, len(windows), split, tai...  4.31 us
    slice x1, local copies, waits for them, and re-layouts, per_device(): start_valid = limits[0]  1.35 us
    convert_element_type x1, other arithmetic, per_device(): note = jnp.concatenate([log_row, positive.astype(jnp.float32)[None]])  1.34 us
    pallas_call x1, Pallas kernels, parts_of(): pl.pallas_call(parts_kernel, out_shape=[pltpu.VMEM((size, depth), own.dty...  1.33 us
  transfers between devices with their start and end apart: 14, of which 9 were waited for; matrix products, arithmetic and copies ran while one was open for 8% of the time, Pallas kernels for 11%

profile of v2, /device:TPU:19, one launch (start us, length us, event | category | flops | bytes accessed | tf_op | source)
XLA Modules:
  0.0 53.1 jit_solution(355770726890309104)
XLA Ops:
  0.0 0.0 copy-start
  0.0 0.7 %collective-permute-start = (bf16[384,1024]{1,0:T(8,128)(2,1)}, bf16[384,1024]{1,0:T(8,128)(2,1)S(1)}, u32[]{:S(2)}, u32[]{:S(2)}) collective-permute-start(bf16[384,1024]{1,0:T(8,128)(2,1)} %refs_4_.1), channel_id=1, source_target_pairs={{0,1},{1,0},{2,3},{3,2},{4,5},{5,4},{6,7},{7,6},{8,9},{9,8},{10,11... | collective-permute-start | bytes 2359304 | tf_op jit(solution)/shard_map/ppermute | solution.py:22
  0.7 1.3 %parts.1 = (bf16[256,1024]{1,0:T(8,128)(2,1)S(1)}, bf16[128,1024]{1,0:T(8,128)(2,1)S(1)}, bf16[256,1024]{1,0:T(8,128)(2,1)S(1)}) custom-call(bf16[384,1024]{1,0:T(8,128)(2,1)} %refs_4_.1), custom_call_target="tpu_custom_call" | custom-call | tf_op jit(solution)/shard_map/parts/pallas_call | solution.py:74
  2.0 0.3 collective-permute-start.2
  2.4 1.3 %fusion.11 = (s32[1]{0:T(128)}, s32[1]{0:T(128)}) fusion(s32[2]{0:T(128)} %param.5), kind=kLoop, calls=%fused_computation.33 | loop fusion | bytes 16 | tf_op jit(solution)/shard_map/slice | solution.py:222
  4.3 1.3 %fusion.9 = (f32[384]{0:T(512)S(1)}, s32[384]{0:T(512)S(1)}, s32[384]{0:T(512)S(1)}) fusion(s32[384]{0:T(512)} %param.4, s32[]{:T(128)} %bitcast.1, s32[]{:T(128)} %bitcast, s32[]{:T(128)S(6)} %mul.29), kind=kLoop, calls=%fused_computation.32 | loop fusion | flops 3840 | bytes 6156 | tf_op jit(solution)/shard_map/convert_element_type | solution.py:270
  5.8 0.0 collective-permute-done.refs_1_
  5.8 3.4 %collective-permute-start.1 = (bf16[256,1024]{1,0:T(8,128)(2,1)S(1)}, bf16[256,1024]{1,0:T(8,128)(2,1)S(1)}, u32[]{:S(2)}, u32[]{:S(2)}) collective-permute-start(bf16[256,1024]{1,0:T(8,128)(2,1)S(1)} %get-tuple-element.33), channel_id=1, source_target_pairs={{1,4},{3,6},{4,1},{5,8},{6,3},{7,10},{8,5},{9,12},{10,7},{11,14},{... | collective-permute-start | bytes 1572872 | tf_op jit(solution)/shard_map/ppermute | solution.py:22
  9.3 1.9 %collective-permute-start.6 = (bf16[128,1024]{1,0:T(8,128)(2,1)S(1)}, bf16[128,1024]{1,0:T(8,128)(2,1)S(1)}, u32[]{:S(2)}, u32[]{:S(2)}) collective-permute-start(bf16[128,1024]{1,0:T(8,128)(2,1)S(1)} %get-tuple-element.40), channel_id=1, source_target_pairs={{2,4},{3,5},{4,2},{5,3},{6,8},{7,9},{8,6},{9,7},{10,12},{11,13},{1... | collective-permute-start | bytes 786440 | tf_op jit(solution)/shard_map/ppermute | solution.py:22
  11.3 1.4 %collective-permute-start.4 = (bf16[128,1024]{1,0:T(8,128)(2,1)S(1)}, bf16[128,1024]{1,0:T(8,128)(2,1)S(1)}, u32[]{:S(2)}, u32[]{:S(2)}) collective-permute-start(bf16[128,1024]{1,0:T(8,128)(2,1)S(1)} %get-tuple-element.40), channel_id=1, source_target_pairs={{0,2},{1,3},{2,0},{3,1},{4,6},{5,7},{6,4},{7,5},{8,10},{9,11},{10,... | collective-permute-start | bytes 786440 | tf_op jit(solution)/shard_map/ppermute | solution.py:22
  12.7 3.6 %collective-permute-done.2.refs_1_ = bf16[256,1024]{1,0:T(8,128)(2,1)S(1)} collective-permute-done((bf16[256,1024]{1,0:T(8,128)(2,1)S(1)}, bf16[256,1024]{1,0:T(8,128)(2,1)S(1)}, u32[]{:S(2)}, u32[]{:S(2)}) %collective-permute-start.2) | collective-permute-done | bytes 524320 | tf_op jit(solution)/shard_map/ppermute | solution.py:22
  16.2 1.0 %collective-permute-done.1.refs_0_ = bf16[256,1024]{1,0:T(8,128)(2,1)S(1)} collective-permute-done((bf16[256,1024]{1,0:T(8,128)(2,1)S(1)}, bf16[256,1024]{1,0:T(8,128)(2,1)S(1)}, u32[]{:S(2)}, u32[]{:S(2)}) %collective-permute-start.1) | collective-permute-done | bytes 524320 | tf_op jit(solution)/shard_map/ppermute | solution.py:22
  17.2 2.1 %collective-permute-start.8 = (bf16[256,1024]{1,0:T(8,128)(2,1)S(1)}, bf16[256,1024]{1,0:T(8,128)(2,1)S(1)}, u32[]{:S(2)}, u32[]{:S(2)}) collective-permute-start(bf16[256,1024]{1,0:T(8,128)(2,1)S(1)} %collective-permute-done.2.refs_1_), channel_id=1, source_target_pairs={{0,4},{1,5},{4,8},{5,9},{6,2},{7,3},{8,12},{9,13},{10,6},{11,7},{1... | collective-permute-start | bytes 1572872 | tf_op jit(solution)/shard_map/ppermute | solution.py:22
  19.3 1.6 %collective-permute-start.3 = (bf16[256,1024]{1,0:T(8,128)(2,1)S(1)}, bf16[256,1024]{1,0:T(8,128)(2,1)S(1)}, u32[]{:S(2)}, u32[]{:S(2)}) collective-permute-start(bf16[256,1024]{1,0:T(8,128)(2,1)S(1)} %collective-permute-done.2.refs_1_), channel_id=1, source_target_pairs={{0,1},{1,0},{2,3},{3,2},{4,5},{5,4},{6,7},{7,6},{8,9},{9,8},{10,11... | collective-permute-start | bytes 1572872 | tf_op jit(solution)/shard_map/ppermute | solution.py:22
  21.0 0.7 %and_select_fusion.refs_3_.refs_4_.refs_5_.refs_11_ = s32[1,2560]{1,0:T(1,128)S(1)} fusion(s32[1,2560]{1,0:T(1,128)S(1)} %constant_dynamic-update-slice_fusion, s32[]{:T(128)} %bitcast.1, s32[]{:T(128)} %bitcast), kind=kLoop, calls=%fused_computation.5 | loop fusion | flops 10240 | bytes 20488 | tf_op jit(solution)/shard_map/jit(_where)/select_n | solution.py:243
  21.6 0.7 %fusion.refs_2_.refs_3_.refs_4_.refs_8_ = s32[384,1]{1,0:T(8,128)S(1)} fusion(s32[]{:T(128)} %bitcast.1, s32[]{:T(128)} %bitcast, s32[]{:T(128)S(6)} %mul.29), kind=kLoop, calls=%fused_computation.1 | loop fusion | flops 1920 | bytes 1548 | tf_op jit(solution)/shard_map/jit(_where)/select_n | solution.py:246
  22.3 0.0 copy-done
  22.3 1.6 %scores_first.1 = (bf16[768,1024]{1,0:T(8,128)(2,1)S(1)}, f32[384,768]{1,0:T(8,128)S(1)}, f32[384,128]{1,0:T(8,128)S(1)}, f32[384,128]{1,0:T(8,128)S(1)}) custom-call(bf16[384,1024]{1,0:T(8,128)(2,1)S(1)} %copy-done, bf16[384,1024]{1,0:T(8,128)(2,1)S(1)} %collective-permute-done.refs_1_, s32[384,1]{1,0:T(8,128)S(1)} %fusion.refs_2_.refs_3_.refs_4_.refs_8_, ...), custom_call_target="tpu_custom_call" | custom-call | tf_op jit(solution)/shard_map/scores_first/pallas_call | solution.py:146
  23.9 0.0 collective-permute-done.6.refs_2_
  23.9 0.1 collective-permute-start.7
  24.0 0.0 collective-permute-done.3.refs_2_
  24.0 1.5 %scores_next.2 = (bf16[768,1024]{1,0:T(8,128)(2,1)S(1)}, f32[384,768]{1,0:T(8,128)S(1)}, f32[384,128]{1,0:T(8,128)S(1)}, f32[384,128]{1,0:T(8,128)S(1)}) custom-call(bf16[256,1024]{1,0:T(8,128)(2,1)S(1)} %collective-permute-done.1.refs_0_, bf16[256,1024]{1,0:T(8,128)(2,1)S(1)} %collective-permute-done.2.refs_1_, ...), custom_call_target="tpu_custom_call" | custom-call | tf_op jit(solution)/shard_map/scores_next/pallas_call | solution.py:146
  25.5 1.3 %collective-permute-done.4.refs_0_ = bf16[128,1024]{1,0:T(8,128)(2,1)S(1)} collective-permute-done((bf16[128,1024]{1,0:T(8,128)(2,1)S(1)}, bf16[128,1024]{1,0:T(8,128)(2,1)S(1)}, u32[]{:S(2)}, u32[]{:S(2)}) %collective-permute-start.4) | collective-permute-done | bytes 262176 | tf_op jit(solution)/shard_map/ppermute | solution.py:22
  26.8 0.9 %collective-permute-start.5 = (bf16[128,1024]{1,0:T(8,128)(2,1)S(1)}, bf16[128,1024]{1,0:T(8,128)(2,1)S(1)}, u32[]{:S(2)}, u32[]{:S(2)}) collective-permute-start(bf16[128,1024]{1,0:T(8,128)(2,1)S(1)} %collective-permute-done.4.refs_0_), channel_id=1, source_target_pairs={{0,1},{1,0},{2,3},{3,2},{4,5},{5,4},{6,7},{7,6},{8,9},{9,8},{10,11... | collective-permute-start | bytes 786440 | tf_op jit(solution)/shard_map/ppermute | solution.py:22
  27.7 0.0 collective-permute-done.7.refs_3_
  27.7 1.2 %collective-permute-done.5.refs_1_ = bf16[128,1024]{1,0:T(8,128)(2,1)S(1)} collective-permute-done((bf16[128,1024]{1,0:T(8,128)(2,1)S(1)}, bf16[128,1024]{1,0:T(8,128)(2,1)S(1)}, u32[]{:S(2)}, u32[]{:S(2)}) %collective-permute-start.5) | collective-permute-done | bytes 262176 | tf_op jit(solution)/shard_map/ppermute | solution.py:22
  28.8 1.3 %scores_next.3 = (bf16[512,1024]{1,0:T(8,128)(2,1)S(1)}, f32[384,512]{1,0:T(8,128)S(1)}, f32[384,128]{1,0:T(8,128)S(1)}, f32[384,128]{1,0:T(8,128)S(1)}) custom-call(bf16[128,1024]{1,0:T(8,128)(2,1)S(1)} %collective-permute-done.4.refs_0_, bf16[128,1024]{1,0:T(8,128)(2,1)S(1)} %collective-permute-done.5.refs_1_, ...), custom_call_target="tpu_custom_call" | custom-call | tf_op jit(solution)/shard_map/scores_next/pallas_call | solution.py:146
  30.1 1.1 %collective-permute-done.8.refs_0_ = bf16[256,1024]{1,0:T(8,128)(2,1)S(1)} collective-permute-done((bf16[256,1024]{1,0:T(8,128)(2,1)S(1)}, bf16[256,1024]{1,0:T(8,128)(2,1)S(1)}, u32[]{:S(2)}, u32[]{:S(2)}) %collective-permute-start.8) | collective-permute-done | bytes 524320 | tf_op jit(solution)/shard_map/ppermute | solution.py:22
  31.2 2.2 %collective-permute-start.9 = (bf16[256,1024]{1,0:T(8,128)(2,1)S(1)}, bf16[256,1024]{1,0:T(8,128)(2,1)S(1)}, u32[]{:S(2)}, u32[]{:S(2)}) collective-permute-start(bf16[256,1024]{1,0:T(8,128)(2,1)S(1)} %collective-permute-done.8.refs_0_), channel_id=1, source_target_pairs={{0,1},{1,0},{2,3},{3,2},{4,5},{5,4},{6,7},{7,6},{8,9},{9,8},{10,11... | collective-permute-start | bytes 1572872 | tf_op jit(solution)/shard_map/ppermute | solution.py:22
  33.5 1.5 %collective-permute-done.9.refs_1_ = bf16[256,1024]{1,0:T(8,128)(2,1)S(1)} collective-permute-done((bf16[256,1024]{1,0:T(8,128)(2,1)S(1)}, bf16[256,1024]{1,0:T(8,128)(2,1)S(1)}, u32[]{:S(2)}, u32[]{:S(2)}) %collective-permute-start.9) | collective-permute-done | bytes 524320 | tf_op jit(solution)/shard_map/ppermute | solution.py:22
  35.0 1.3 %scores_last.1 = (bf16[512,1024]{1,0:T(8,128)(2,1)S(1)}, f32[384,512]{1,0:T(8,128)S(1)}, f32[384,128]{1,0:T(8,128)S(1)}, f32[1,384]{1,0:T(1,128)S(1)}) custom-call(bf16[256,1024]{1,0:T(8,128)(2,1)S(1)} %collective-permute-done.8.refs_0_, bf16[256,1024]{1,0:T(8,128)(2,1)S(1)} %collective-permute-done.9.refs_1_, ...), custom_call_target="tpu_custom_call" | custom-call | tf_op jit(solution)/shard_map/scores_last/pallas_call | solution.py:146
  36.3 0.4 collective-permute-start.10
  36.8 0.8 %collective-permute-done.10.refs_13_ = f32[2,384]{1,0:T(2,128)S(1)} collective-permute-done((f32[2,384]{1,0:T(2,128)S(1)}, f32[2,384]{1,0:T(2,128)S(1)}, u32[]{:S(2)}, u32[]{:S(2)}) %collective-permute-start.10) | collective-permute-done | bytes 3104 | tf_op jit(solution)/shard_map/ppermute | solution.py:22
  37.6 3.6 %collective-permute-start.11 = (f32[2,2,384]{2,1,0:T(2,128)S(1)}, f32[2,2,384]{2,1,0:T(2,128)S(1)}, u32[]{:S(2)}, u32[]{:S(2)}) collective-permute-start(f32[2,2,384]{2,1,0:T(2,128)S(1)} %pad_maximum_fusion), channel_id=1, source_target_pairs={{0,2},{2,4},{3,1},{4,6},{5,3},{6,8},{7,5},{8,10},{9,7},{10,12},{11... | collective-permute-start | bytes 18440 | tf_op jit(solution)/shard_map/ppermute | solution.py:22
  41.2 1.9 %collective-permute-start.12 = (f32[2,384]{1,0:T(2,128)S(1)}, f32[2,384]{1,0:T(2,128)S(1)}, u32[]{:S(2)}, u32[]{:S(2)}) collective-permute-start(f32[2,384]{1,0:T(2,128)S(1)} %get-tuple-element.60.refs_12_), channel_id=1, source_target_pairs={{1,4},{3,6},{4,1},{5,8},{6,3},{7,10},{8,5},{9,12},{10,7},{11,14},{... | collective-permute-start | bytes 9224 | tf_op jit(solution)/shard_map/ppermute | solution.py:22
  43.1 3.0 %collective-permute-done.12.refs_14_ = f32[2,384]{1,0:T(2,128)S(1)} collective-permute-done((f32[2,384]{1,0:T(2,128)S(1)}, f32[2,384]{1,0:T(2,128)S(1)}, u32[]{:S(2)}, u32[]{:S(2)}) %collective-permute-start.12) | collective-permute-done | bytes 3104 | tf_op jit(solution)/shard_map/ppermute | solution.py:22
  46.1 0.0 collective-permute-done.11.refs_15_
  46.1 1.9 %collective-permute-start.13 = (f32[2,2,384]{2,1,0:T(2,128)S(1)}, f32[2,2,384]{2,1,0:T(2,128)S(1)}, u32[]{:S(2)}, u32[]{:S(2)}) collective-permute-start(f32[2,2,384]{2,1,0:T(2,128)S(1)} %collective-permute-done.11.refs_15_), channel_id=1, source_target_pairs={{0,1},{1,0},{2,3},{3,2},{4,5},{5,4},{6,7},{7,6},{8,9},{9,8},{10,11... | collective-permute-start | bytes 18440 | tf_op jit(solution)/shard_map/ppermute | solution.py:22
  48.0 0.1 broadcast_in_dim.24.refs_9_
  48.1 0.7 %collective-permute-done.13.refs_16_ = f32[2,2,384]{2,1,0:T(2,128)S(1)} collective-permute-done((f32[2,2,384]{2,1,0:T(2,128)S(1)}, f32[2,2,384]{2,1,0:T(2,128)S(1)}, u32[]{:S(2)}, u32[]{:S(2)}) %collective-permute-start.13) | collective-permute-done | bytes 6176 | tf_op jit(solution)/shard_map/ppermute | solution.py:22
  48.8 4.3 %product.1 = f32[384,1024]{1,0:T(8,128)} custom-call(bf16[768,1024]{1,0:T(8,128)(2,1)S(1)} %get-tuple-element.31.refs_0_, bf16[768,1024]{1,0:T(8,128)(2,1)S(1)} %get-tuple-element.38.refs_1_, bf16[512,1024]{1,0:T(8,128)(2,1)S(1)} %get-tuple-element.44.refs_2_, bf16[512,1024]{1,0:T(8,128)(2,1)S(1)} %get-tuple-element.48.refs_3_, ...), custom_call_target="tpu_custom_call" | custom-call | tf_op jit(solution)/shard_map/product/pallas_call | solution.py:201
  (20 shorter events, 0.2 us)
Async XLA Ops:
  0.0 22.3 %copy-start = (bf16[384,1024]{1,0:T(8,128)(2,1)S(1)}, bf16[384,1024]{1,0:T(8,128)(2,1)}, u32[]{:S(2)}) copy-start(bf16[384,1024]{1,0:T(8,128)(2,1)} %refs_4_.1) | copy-start | bytes 2359300
  0.0 5.8 %collective-permute-start = (bf16[384,1024]{1,0:T(8,128)(2,1)}, bf16[384,1024]{1,0:T(8,128)(2,1)S(1)}, u32[]{:S(2)}, u32[]{:S(2)}) collective-permute-start(bf16[384,1024]{1,0:T(8,128)(2,1)} %refs_4_.1), channel_id=1, source_target_pairs={{0,1},{1,0},{2,3},{3,2},{4,5},{5,4},{6,7},{7,6},{8,9},{9,8},{10,11... | collective-permute-start | bytes 2359304 | tf_op jit(solution)/shard_map/ppermute | solution.py:22
  2.0 14.2 %collective-permute-start.2 = (bf16[256,1024]{1,0:T(8,128)(2,1)S(1)}, bf16[256,1024]{1,0:T(8,128)(2,1)S(1)}, u32[]{:S(2)}, u32[]{:S(2)}) collective-permute-start(bf16[256,1024]{1,0:T(8,128)(2,1)S(1)} %get-tuple-element.34), channel_id=1, source_target_pairs={{0,2},{1,3},{2,0},{3,1},{4,6},{5,7},{6,4},{7,5},{8,10},{9,11},{10,... | collective-permute-start | bytes 1572872 | tf_op jit(solution)/shard_map/ppermute | solution.py:22
  5.8 11.4 %collective-permute-start.1 = (bf16[256,1024]{1,0:T(8,128)(2,1)S(1)}, bf16[256,1024]{1,0:T(8,128)(2,1)S(1)}, u32[]{:S(2)}, u32[]{:S(2)}) collective-permute-start(bf16[256,1024]{1,0:T(8,128)(2,1)S(1)} %get-tuple-element.33), channel_id=1, source_target_pairs={{1,4},{3,6},{4,1},{5,8},{6,3},{7,10},{8,5},{9,12},{10,7},{11,14},{... | collective-permute-start | bytes 1572872 | tf_op jit(solution)/shard_map/ppermute | solution.py:22
  9.3 14.6 %collective-permute-start.6 = (bf16[128,1024]{1,0:T(8,128)(2,1)S(1)}, bf16[128,1024]{1,0:T(8,128)(2,1)S(1)}, u32[]{:S(2)}, u32[]{:S(2)}) collective-permute-start(bf16[128,1024]{1,0:T(8,128)(2,1)S(1)} %get-tuple-element.40), channel_id=1, source_target_pairs={{2,4},{3,5},{4,2},{5,3},{6,8},{7,9},{8,6},{9,7},{10,12},{11,13},{1... | collective-permute-start | bytes 786440 | tf_op jit(solution)/shard_map/ppermute | solution.py:22
  11.3 15.5 %collective-permute-start.4 = (bf16[128,1024]{1,0:T(8,128)(2,1)S(1)}, bf16[128,1024]{1,0:T(8,128)(2,1)S(1)}, u32[]{:S(2)}, u32[]{:S(2)}) collective-permute-start(bf16[128,1024]{1,0:T(8,128)(2,1)S(1)} %get-tuple-element.40), channel_id=1, source_target_pairs={{0,2},{1,3},{2,0},{3,1},{4,6},{5,7},{6,4},{7,5},{8,10},{9,11},{10,... | collective-permute-start | bytes 786440 | tf_op jit(solution)/shard_map/ppermute | solution.py:22
  17.2 14.0 %collective-permute-start.8 = (bf16[256,1024]{1,0:T(8,128)(2,1)S(1)}, bf16[256,1024]{1,0:T(8,128)(2,1)S(1)}, u32[]{:S(2)}, u32[]{:S(2)}) collective-permute-start(bf16[256,1024]{1,0:T(8,128)(2,1)S(1)} %collective-permute-done.2.refs_1_), channel_id=1, source_target_pairs={{0,4},{1,5},{4,8},{5,9},{6,2},{7,3},{8,12},{9,13},{10,6},{11,7},{1... | collective-permute-start | bytes 1572872 | tf_op jit(solution)/shard_map/ppermute | solution.py:22
  19.3 4.7 %collective-permute-start.3 = (bf16[256,1024]{1,0:T(8,128)(2,1)S(1)}, bf16[256,1024]{1,0:T(8,128)(2,1)S(1)}, u32[]{:S(2)}, u32[]{:S(2)}) collective-permute-start(bf16[256,1024]{1,0:T(8,128)(2,1)S(1)} %collective-permute-done.2.refs_1_), channel_id=1, source_target_pairs={{0,1},{1,0},{2,3},{3,2},{4,5},{5,4},{6,7},{7,6},{8,9},{9,8},{10,11... | collective-permute-start | bytes 1572872 | tf_op jit(solution)/shard_map/ppermute | solution.py:22
  23.9 3.8 %collective-permute-start.7 = (bf16[128,1024]{1,0:T(8,128)(2,1)S(1)}, bf16[128,1024]{1,0:T(8,128)(2,1)S(1)}, u32[]{:S(2)}, u32[]{:S(2)}) collective-permute-start(bf16[128,1024]{1,0:T(8,128)(2,1)S(1)} %collective-permute-done.6.refs_2_), channel_id=1, source_target_pairs={{0,1},{1,0},{2,3},{3,2},{4,5},{5,4},{6,7},{7,6},{8,9},{9,8},{10,11... | collective-permute-start | bytes 786440 | tf_op jit(solution)/shard_map/ppermute | solution.py:22
  26.8 2.0 %collective-permute-start.5 = (bf16[128,1024]{1,0:T(8,128)(2,1)S(1)}, bf16[128,1024]{1,0:T(8,128)(2,1)S(1)}, u32[]{:S(2)}, u32[]{:S(2)}) collective-permute-start(bf16[128,1024]{1,0:T(8,128)(2,1)S(1)} %collective-permute-done.4.refs_0_), channel_id=1, source_target_pairs={{0,1},{1,0},{2,3},{3,2},{4,5},{5,4},{6,7},{7,6},{8,9},{9,8},{10,11... | collective-permute-start | bytes 786440 | tf_op jit(solution)/shard_map/ppermute | solution.py:22
  31.2 3.8 %collective-permute-start.9 = (bf16[256,1024]{1,0:T(8,128)(2,1)S(1)}, bf16[256,1024]{1,0:T(8,128)(2,1)S(1)}, u32[]{:S(2)}, u32[]{:S(2)}) collective-permute-start(bf16[256,1024]{1,0:T(8,128)(2,1)S(1)} %collective-permute-done.8.refs_0_), channel_id=1, source_target_pairs={{0,1},{1,0},{2,3},{3,2},{4,5},{5,4},{6,7},{7,6},{8,9},{9,8},{10,11... | collective-permute-start | bytes 1572872 | tf_op jit(solution)/shard_map/ppermute | solution.py:22
  36.3 1.3 %collective-permute-start.10 = (f32[2,384]{1,0:T(2,128)S(1)}, f32[2,384]{1,0:T(2,128)S(1)}, u32[]{:S(2)}, u32[]{:S(2)}) collective-permute-start(f32[2,384]{1,0:T(2,128)S(1)} %get-tuple-element.60.refs_12_), channel_id=1, source_target_pairs={{0,1},{1,0},{2,3},{3,2},{4,5},{5,4},{6,7},{7,6},{8,9},{9,8},{10,11... | collective-permute-start | bytes 9224 | tf_op jit(solution)/shard_map/ppermute | solution.py:22
  37.6 8.5 %collective-permute-start.11 = (f32[2,2,384]{2,1,0:T(2,128)S(1)}, f32[2,2,384]{2,1,0:T(2,128)S(1)}, u32[]{:S(2)}, u32[]{:S(2)}) collective-permute-start(f32[2,2,384]{2,1,0:T(2,128)S(1)} %pad_maximum_fusion), channel_id=1, source_target_pairs={{0,2},{2,4},{3,1},{4,6},{5,3},{6,8},{7,5},{8,10},{9,7},{10,12},{11... | collective-permute-start | bytes 18440 | tf_op jit(solution)/shard_map/ppermute | solution.py:22
  41.2 4.9 %collective-permute-start.12 = (f32[2,384]{1,0:T(2,128)S(1)}, f32[2,384]{1,0:T(2,128)S(1)}, u32[]{:S(2)}, u32[]{:S(2)}) collective-permute-start(f32[2,384]{1,0:T(2,128)S(1)} %get-tuple-element.60.refs_12_), channel_id=1, source_target_pairs={{1,4},{3,6},{4,1},{5,8},{6,3},{7,10},{8,5},{9,12},{10,7},{11,14},{... | collective-permute-start | bytes 9224 | tf_op jit(solution)/shard_map/ppermute | solution.py:22
  46.1 2.7 %collective-permute-start.13 = (f32[2,2,384]{2,1,0:T(2,128)S(1)}, f32[2,2,384]{2,1,0:T(2,128)S(1)}, u32[]{:S(2)}, u32[]{:S(2)}) collective-permute-start(f32[2,2,384]{2,1,0:T(2,128)S(1)} %collective-permute-done.11.refs_15_), channel_id=1, source_target_pairs={{0,1},{1,0},{2,3},{3,2},{4,5},{5,4},{6,7},{7,6},{8,9},{9,8},{10,11... | collective-permute-start | bytes 18440 | tf_op jit(solution)/shard_map/ppermute | solution.py:22

commit v3 on v2

v3 whole, which is shorter than its diff:
```python
import functools

import jax
import jax.numpy as jnp
from jax import lax
from jax.experimental import pallas as pl
from jax.experimental.pallas import tpu as pltpu
from jax.sharding import PartitionSpec as P

BAND = 1024
SCALE = 16.0
AXES = ("tm", "sub")
NOWHERE = 1 << 29
LANES = 128
STEP = 256
VMEM = pl.BlockSpec(memory_space=pltpu.VMEM)
COST = pl.CostEstimate(flops=0, bytes_accessed=0, transcendentals=0)
PARAMS = pltpu.CompilerParams(vmem_limit_bytes=16 << 20)


def shift(x, count, target):
    pairs = [(i, target(i)) for i in range(count) if 0 <= target(i) < count]
    return lax.ppermute(x, AXES, pairs)


def after(x, *others):
    return lax.optimization_barrier((x, *others))[0]


def to_core(i):
    return i ^ 1


def to_pair(i):
    return i ^ 2


def to_cross(i):
    return i + 2 if i & 2 else i - 2


def to_next(i):
    return i - 4 if i & 2 else i + 4


def to_far(i):
    return i + 3 if i & 1 else i - 3


def to_side(i):
    return i - 2 if i & 1 else i + 2


def is_second(axis_index, bit):
    return lax.rem(axis_index // bit, 2)


def parts_kernel(own_ref, head_ref, rest_ref, tail_ref, sems):
    split, tail = head_ref.shape[0], tail_ref.shape[0]
    core = is_second(lax.axis_index("sub"), 1)
    first = pl.multiple_of(core * (own_ref.shape[0] - tail), 16)
    copies = [
        pltpu.make_async_copy(own_ref.at[pl.ds(0, split)], head_ref, sems.at[0]),
        pltpu.make_async_copy(own_ref.at[pl.ds(split, own_ref.shape[0] - split)], rest_ref, sems.at[1]),
        pltpu.make_async_copy(own_ref.at[pl.ds(first, tail)], tail_ref, sems.at[2]),
    ]
    for copy in copies:
        copy.start()
    for copy in copies:
        copy.wait()


def parts_of(own, split, tail):
    rows, depth = own.shape
    return pl.pallas_call(
        parts_kernel,
        out_shape=[pltpu.VMEM((size, depth), own.dtype) for size in (split, rows - split, tail)],
        in_specs=[pl.BlockSpec(memory_space=pl.ANY)],
        out_specs=[VMEM] * 3,
        scratch_shapes=[pltpu.SemaphoreType.DMA((3,))],
        compiler_params=PARAMS,
        cost_estimate=COST,
        name="parts",
    )(pltpu.with_memory_space_constraint(own, pltpu.HBM))


def index_kernel(split, tail, limits_ref, offset_ref, row_ref, column_ref, positive_ref, positive_row_ref):
    rows = offset_ref.shape[1]
    device = lax.axis_index("tm") * lax.axis_size("sub") + lax.axis_index("sub")
    core, chip = is_second(device, 1), is_second(device, 2)
    start, end = limits_ref[0], lax.axis_size(AXES) * rows - limits_ref[1]
    mate = device + 1 - 2 * core
    across, step = 2 - 4 * chip, 4 * chip - 2
    far = jnp.where(core == 1, (device + 3) * rows, (device - 2) * rows - tail)
    pair, pair_mate = (device + across) * rows, (mate + across) * rows
    cross, cross_mate = (device + step) * rows, (mate + step) * rows
    places = [
        (device * rows, rows), (mate * rows, rows), (far, tail),
        (pair, split), (pair_mate, split), (pair + split, rows - split), (pair_mate + split, rows - split),
        (cross + split, rows - split), (cross_mate + split, rows - split), (cross, split), (cross_mate, split),
    ]
    low = 0
    for base, size in places:
        index = base + lax.broadcasted_iota(jnp.int32, (1, size), 1)
        index = jnp.where((index >= start) & (index < end), index, NOWHERE)
        row_ref[:, low : low + size] = index.astype(jnp.float32)
        low += size
    index = device * rows + lax.broadcasted_iota(jnp.int32, (rows, 1), 0)
    index = jnp.where((index >= start) & (index < end), index, -NOWHERE)
    column_ref[...] = index.astype(jnp.float32)
    index = device * rows + lax.broadcasted_iota(jnp.int32, (1, rows), 1)
    forward = index + offset_ref[...]
    positive = jnp.where(forward < end, forward, index - offset_ref[...])
    positive = jnp.where((index >= start) & (index < end), positive, -1).astype(jnp.float32)
    positive_row_ref[...] = positive
    positive_ref[...] = jnp.broadcast_to(positive, (LANES, rows)).T[:, :1]


def index_of(limits, offsets, split, tail, width):
    rows = offsets.shape[1]
    shapes = [(1, width), (rows, 1), (rows, 1), (1, rows)]
    return pl.pallas_call(
        functools.partial(index_kernel, split, tail),
        out_shape=[jax.ShapeDtypeStruct(shape, jnp.float32) for shape in shapes],
        in_specs=[pl.BlockSpec(memory_space=pltpu.SMEM), VMEM],
        out_specs=[VMEM] * 4,
        compiler_params=PARAMS,
        cost_estimate=COST,
        name="index",
    )(limits, offsets)


def score_kernel(sizes, low, first, last, *refs):
    blocks = refs[: len(sizes)]
    column_ref, row_ref, positive_row_ref = refs[len(sizes) : len(sizes) + 3]
    refs = refs[len(sizes) + 3 :]
    if first:
        own = blocks[0][...]
    else:
        own = refs[0][...]
        old_peak, old_total = refs[1][:, :1], refs[2][:, :1]
        refs = refs[3:]
    window_ref, score_ref = refs[:2]
    rows = column_ref.shape[0]
    high = low + sum(sizes)
    block = jnp.concatenate([ref[...] for ref in blocks], axis=0)
    scores = SCALE * lax.dot_general(
        own, block, (((1,), (1,)), ((), ())), preferred_element_type=jnp.float32
    )
    spacing = column_ref[...] - row_ref[:, low:high]
    inside = jnp.abs(spacing) <= BAND
    if first:
        inside = inside & (spacing != 0.0)
    masked = jnp.where(inside, scores, -jnp.inf)
    score_ref[...] = masked
    peak = jnp.max(masked, axis=1, keepdims=True)
    if first:
        own_valid = column_ref[...] >= 0.0
        peak = jnp.where(own_valid, peak, 0.0)
    else:
        peak = jnp.maximum(peak, old_peak)
    total = jnp.sum(jnp.exp(score_ref[...] - peak), axis=1, keepdims=True)
    if first:
        total = total + jnp.where(own_valid, 0.0, 1.0)
    else:
        total = total + old_total * jnp.exp(old_peak - peak)
    window_ref[...] = block
    if last:
        log_ref, note_ref = refs[2:]
        log_sum = jnp.broadcast_to(peak + jnp.log(total), (rows, LANES))
        log_ref[...] = log_sum
        note_ref[:1] = log_sum.T[:1]
        note_ref[1:] = positive_row_ref[...]
    else:
        peak_ref, total_ref = refs[2:]
        peak_ref[...] = jnp.broadcast_to(peak, (rows, LANES))
        total_ref[...] = jnp.broadcast_to(total, (rows, LANES))


def scores_of(low, blocks, own, column, row, positive_row, state, last):
    rows, depth = own.shape
    sizes = tuple(block.shape[0] for block in blocks)
    width = sum(sizes)
    first = state is None
    wide = jax.ShapeDtypeStruct((rows, LANES), jnp.float32)
    shapes = [
        jax.ShapeDtypeStruct((width, depth), jnp.bfloat16),
        jax.ShapeDtypeStruct((rows, width), jnp.float32),
        wide,
        jax.ShapeDtypeStruct((2, rows), jnp.float32) if last else wide,
    ]
    operands = (*blocks, column, row, positive_row)
    if not first:
        operands = (*operands, own, *state)
    window, scores, *state = pl.pallas_call(
        functools.partial(score_kernel, sizes, low, first, last),
        out_shape=shapes,
        in_specs=[VMEM] * len(operands),
        out_specs=[VMEM] * len(shapes),
        compiler_params=PARAMS,
        cost_estimate=COST,
        name="scores_last" if last else ("scores_first" if first else "scores_next"),
    )(*operands)
    return window, scores, state


def weight_of(score, log_sum, index, wanted):
    weight = jnp.exp(score - log_sum) - jnp.where(index == wanted, 1.0, 0.0)
    return weight.astype(jnp.bfloat16)


def product_out_kernel(count, *refs):
    windows, scores = refs[:count], refs[count : 2 * count]
    column_ref, positive_ref, log_ref, row_ref, own_note, mate_note, out_ref = refs[2 * count :]
    log_sum, positive = log_ref[:, :1], positive_ref[...]
    weights = []
    low = 0
    for ref in scores:
        high = low + ref.shape[1]
        weights.append(weight_of(ref[...], log_sum, row_ref[:, low:high], positive))
        low = high
    notes = jnp.concatenate([own_note[...], mate_note[...]], axis=1)
    weights.append(weight_of(scores[0][...], notes[:1], notes[1:], column_ref[...]))
    weights = jnp.concatenate(weights, axis=1)
    for low in range(0, out_ref.shape[1], STEP):
        block = jnp.concatenate([ref[:, low : low + STEP] for ref in (*windows, windows[0])], axis=0)
        out_ref[:, low : low + STEP] = jnp.dot(weights, block, preferred_element_type=jnp.float32)


def product_back_kernel(count, split, tail, *refs):
    windows, scores = refs[:count], refs[count : 2 * count]
    column_ref, far_note, side_ref, other_ref, base_ref, out_ref, held_ref, sems = refs[2 * count :]
    rows = column_ref.shape[0]
    core = is_second(lax.axis_index("sub"), 1)
    swap = core == is_second(lax.axis_index("sub"), 2)
    pair = jnp.where(swap, other_ref[1], side_ref[0])
    pair_mate = jnp.where(swap, other_ref[0], side_ref[1])
    cross = jnp.where(swap, side_ref[0], other_ref[1])
    cross_mate = jnp.where(swap, side_ref[1], other_ref[0])
    far = jnp.where(core == 1, far_note[:, :tail], far_note[:, rows - tail :])
    notes = jnp.concatenate(
        [
            far, pair[:, :split], pair_mate[:, :split], pair[:, split:], pair_mate[:, split:],
            cross[:, split:], cross_mate[:, split:], cross[:, :split], cross_mate[:, :split],
        ],
        axis=1,
    )
    weights = []
    low = 0
    for ref in scores:
        high = low + ref.shape[1]
        weights.append(weight_of(ref[...], notes[:1, low:high], notes[1:, low:high], column_ref[...]))
        low = high
    weights = jnp.concatenate(weights, axis=1)
    copies = []
    for number, low in enumerate(range(0, out_ref.shape[1], STEP)):
        place = pl.ds(low, STEP)
        block = jnp.concatenate([ref[:, low : low + STEP] for ref in windows], axis=0)
        part = jnp.dot(weights, block, preferred_element_type=jnp.float32)
        held_ref[:, low : low + STEP] = SCALE * (part + base_ref[:, low : low + STEP])
        copies.append(pltpu.make_async_copy(held_ref.at[:, place], out_ref.at[:, place], sems.at[number]))
        copies[-1].start()
    for copy in copies:
        copy.wait()


def product_of(kernel, operands, scratch, place, name):
    rows, depth = operands[-1].shape if scratch else (operands[-1].shape[1], operands[0].shape[1])
    return pl.pallas_call(
        kernel,
        out_shape=jax.ShapeDtypeStruct((rows, depth), jnp.float32),
        in_specs=[VMEM] * len(operands),
        out_specs=place,
        scratch_shapes=scratch,
        compiler_params=PARAMS,
        cost_estimate=COST,
        name=name,
    )(*operands)


def per_device(embeddings, offsets, limits):
    rows, depth = embeddings.shape
    count = lax.axis_size(AXES)
    assert count % 4 == 0 and lax.axis_size("sub") % 4 == 0
    tail = BAND - 2 * rows
    split = 2 * rows // 3
    assert 0 < tail <= rows and split % 16 == 0

    head, rest, tail_rows = parts_of(embeddings, split, tail)
    mate = shift(embeddings, count, to_core)
    pair_head = shift(head, count, to_pair)
    far = shift(after(tail_rows, mate), count, to_far)
    row, column, positive, positive_row = index_of(
        limits, offsets[None], split, tail, 6 * rows + tail
    )

    windows, scores = [], []

    def score(blocks, state, last=False):
        low = sum(window.shape[0] for window in windows)
        window, score, state = scores_of(low, blocks, embeddings, column, row, positive_row, state, last)
        windows.append(window)
        scores.append(score)
        return state

    state = score([embeddings, mate], None)
    pair_rest = shift(after(rest, state[0]), count, to_pair)
    pair_mate_head = shift(after(pair_head, far, state[0]), count, to_core)
    cross_rest = shift(after(rest, pair_head, far), count, to_cross)
    cross_head = shift(after(pair_head, far, state[0]), count, to_next)
    pair_mate_rest = shift(pair_rest, count, to_core)
    state = score([far, pair_head, pair_mate_head, pair_rest, pair_mate_rest], state)
    cross_mate_rest = shift(cross_rest, count, to_core)
    cross_mate_head = shift(after(cross_head, state[0]), count, to_core)
    log_sum, note = score([cross_rest, cross_mate_rest, cross_head, cross_mate_head], state, True)

    mate_note = shift(note, count, to_core)
    side = shift(jnp.stack([note, mate_note]), count, to_side)
    far_note = shift(note, count, to_far)
    base = product_of(
        functools.partial(product_out_kernel, len(windows)),
        (*windows, *scores, column, positive, log_sum, row, note, mate_note),
        [], VMEM, "product_out",
    )
    side, far_note, base = lax.optimization_barrier((side, far_note, base))
    other = shift(side, count, to_core)
    return product_of(
        functools.partial(product_back_kernel, len(windows) - 1, split, tail),
        (*windows[1:], *scores[1:], column, far_note, side, other, base),
        [pltpu.VMEM((rows, depth), jnp.float32), pltpu.SemaphoreType.DMA((depth // STEP,))],
        pl.BlockSpec(memory_space=pl.ANY), "product_back",
    )


def solution(mesh):
    return jax.shard_map(
        per_device,
        mesh=mesh,
        in_specs=(P(("videos", "tm", "sub"), None), P(("videos", "tm", "sub")), P("videos")),
        out_specs=P(("videos", "tm", "sub"), None),
        check_vma=False,
    )
```

time: 53.4 us -> 52.6 us (0.985)
  the two profiles are of different devices: /device:TPU:19 before, /device:TPU:1 now
where the time goes in v3:
time: 52.6 us; the launch traced here: 52.2 us
  starting transfers between devices  21.8 us (41%)
  waiting for transfers between devices  15.5 us (29%)
  Pallas kernels  12.4 us (24%)
  local copies, waits for them, and re-layouts  2.47 us (5%)
    ppermute x14, starting transfers between devices, shift(): return lax.ppermute(x, AXES, pairs)  21.8 us
    ppermute x14, waiting for transfers between devices, shift(): return lax.ppermute(x, AXES, pairs)  15.5 us
    pallas_call x2, Pallas kernels, product_of(): pl.pallas_call(kernel, out_shape=jax.ShapeDtypeStruct((rows, depth), jnp....  5.55 us
    pallas_call x3, Pallas kernels, scores_of(): pl.pallas_call(functools.partial(score_kernel, sizes, low, first, last),...  4.76 us
    unnamed x4, local copies, waits for them, and re-layouts  1.78 us
    pallas_call x1, Pallas kernels, parts_of(): pl.pallas_call(parts_kernel, out_shape=[pltpu.VMEM((size, depth), own.dty...  1.33 us
  transfers between devices with their start and end apart: 14, of which 7 were waited for; matrix products, arithmetic and copies ran while one was open for 1% of the time, Pallas kernels for 16%

profile of v3, /device:TPU:1, one launch (start us, length us, event | category | flops | bytes accessed | tf_op | source)
XLA Modules:
  0.0 52.2 jit_solution(1151527835556467021)
XLA Ops:
  0.0 0.1 collective-permute-start
  0.1 1.3 %parts.1 = (bf16[256,1024]{1,0:T(8,128)(2,1)S(1)}, bf16[128,1024]{1,0:T(8,128)(2,1)S(1)}, bf16[256,1024]{1,0:T(8,128)(2,1)S(1)}) custom-call(bf16[384,1024]{1,0:T(8,128)(2,1)} %refs_7_.1), custom_call_target="tpu_custom_call" | custom-call | tf_op jit(solution)/shard_map/parts/pallas_call | solution.py:75
  1.4 2.7 %collective-permute-start.2 = (bf16[256,1024]{1,0:T(8,128)(2,1)S(1)}, bf16[256,1024]{1,0:T(8,128)(2,1)S(1)}, u32[]{:S(2)}, u32[]{:S(2)}) collective-permute-start(bf16[256,1024]{1,0:T(8,128)(2,1)S(1)} %get-tuple-element.34), channel_id=1, source_target_pairs={{0,2},{1,3},{2,0},{3,1},{4,6},{5,7},{6,4},{7,5},{8,10},{9,11},{10,... | collective-permute-start | bytes 1572872 | tf_op jit(solution)/shard_map/ppermute | solution.py:23
  4.1 0.0 collective-permute-done.refs_1_
  4.1 3.4 %collective-permute-start.1 = (bf16[256,1024]{1,0:T(8,128)(2,1)S(1)}, bf16[256,1024]{1,0:T(8,128)(2,1)S(1)}, u32[]{:S(2)}, u32[]{:S(2)}) collective-permute-start(bf16[256,1024]{1,0:T(8,128)(2,1)S(1)} %get-tuple-element.33), channel_id=1, source_target_pairs={{1,4},{3,6},{4,1},{5,8},{6,3},{7,10},{8,5},{9,12},{10,7},{11,14},{... | collective-permute-start | bytes 1572872 | tf_op jit(solution)/shard_map/ppermute | solution.py:23
  7.5 0.7 %broadcast_in_dim.3.offset_ref = s32[1,384]{1,0:T(1,128)S(1)} reshape(s32[384]{0:T(512)} %param.4) | data formatting | bytes 3072 | tf_op jit(solution)/shard_map/broadcast_in_dim | solution.py:294
  8.2 0.0 copy-start.1
  8.2 0.7 %copy-done.1 = s32[2]{0:T(128)S(1)} copy-done((s32[2]{0:T(128)S(1)}, s32[2]{0:T(128)}, u32[]{:S(2)}) %copy-start.1) | copy-done | bytes 32
  8.9 0.7 %index.1 = (f32[1,2560]{1,0:T(1,128)S(1)}, f32[384,1]{1,0:T(8,128)S(1)}, f32[384,1]{1,0:T(8,128)S(1)}, f32[1,384]{1,0:T(1,128)S(1)}) custom-call(s32[2]{0:T(128)S(1)} %copy-done.1, s32[1,384]{1,0:T(1,128)S(1)} %broadcast_in_dim.3.offset_ref), custom_call_target="tpu_custom_call" | custom-call | tf_op jit(solution)/shard_map/index/pallas_call | solution.py:122
  9.6 0.0 copy-start
  9.6 1.1 %copy-done = bf16[384,1024]{1,0:T(8,128)(2,1)S(1)} copy-done((bf16[384,1024]{1,0:T(8,128)(2,1)S(1)}, bf16[384,1024]{1,0:T(8,128)(2,1)}, u32[]{:S(2)}) %copy-start) | copy-done | bytes 786456
  10.7 1.5 %scores_first.1 = (bf16[768,1024]{1,0:T(8,128)(2,1)S(1)}, f32[384,768]{1,0:T(8,128)S(1)}, f32[384,128]{1,0:T(8,128)S(1)}, f32[384,128]{1,0:T(8,128)S(1)}) custom-call(bf16[384,1024]{1,0:T(8,128)(2,1)S(1)} %copy-done, bf16[384,1024]{1,0:T(8,128)(2,1)S(1)} %collective-permute-done.refs_1_, f32[384,1]{1,0:T(8,128)S(1)} %get-tuple-element.35.refs_2_.refs_5_.refs_4_.refs_6_, ...), custom_call_target="tpu_custom_call" | custom-call | tf_op jit(solution)/shard_map/scores_first/pallas_call | solution.py:195
  12.3 0.8 %collective-permute-start.4 = (bf16[128,1024]{1,0:T(8,128)(2,1)S(1)}, bf16[128,1024]{1,0:T(8,128)(2,1)S(1)}, u32[]{:S(2)}, u32[]{:S(2)}) collective-permute-start(bf16[128,1024]{1,0:T(8,128)(2,1)S(1)} %get-tuple-element.44), channel_id=1, source_target_pairs={{0,2},{1,3},{2,0},{3,1},{4,6},{5,7},{6,4},{7,5},{8,10},{9,11},{10,... | collective-permute-start | bytes 786440 | tf_op jit(solution)/shard_map/ppermute | solution.py:23
  13.1 3.3 %collective-permute-done.2.refs_1_ = bf16[256,1024]{1,0:T(8,128)(2,1)S(1)} collective-permute-done((bf16[256,1024]{1,0:T(8,128)(2,1)S(1)}, bf16[256,1024]{1,0:T(8,128)(2,1)S(1)}, u32[]{:S(2)}, u32[]{:S(2)}) %collective-permute-start.2) | collective-permute-done | bytes 524320 | tf_op jit(solution)/shard_map/ppermute | solution.py:23
  16.4 0.0 collective-permute-done.1.refs_0_
  16.4 0.8 %collective-permute-start.3 = (bf16[256,1024]{1,0:T(8,128)(2,1)S(1)}, bf16[256,1024]{1,0:T(8,128)(2,1)S(1)}, u32[]{:S(2)}, u32[]{:S(2)}) collective-permute-start(bf16[256,1024]{1,0:T(8,128)(2,1)S(1)} %collective-permute-done.2.refs_1_), channel_id=1, source_target_pairs={{0,1},{1,0},{2,3},{3,2},{4,5},{5,4},{6,7},{7,6},{8,9},{9,8},{10,11... | collective-permute-start | bytes 1572872 | tf_op jit(solution)/shard_map/ppermute | solution.py:23
  17.2 3.7 %collective-permute-start.8 = (bf16[256,1024]{1,0:T(8,128)(2,1)S(1)}, bf16[256,1024]{1,0:T(8,128)(2,1)S(1)}, u32[]{:S(2)}, u32[]{:S(2)}) collective-permute-start(bf16[256,1024]{1,0:T(8,128)(2,1)S(1)} %collective-permute-done.2.refs_1_), channel_id=1, source_target_pairs={{0,4},{1,5},{4,8},{5,9},{6,2},{7,3},{8,12},{9,13},{10,6},{11,7},{1... | collective-permute-start | bytes 1572872 | tf_op jit(solution)/shard_map/ppermute | solution.py:23
  20.9 1.1 %collective-permute-done.4.refs_3_ = bf16[128,1024]{1,0:T(8,128)(2,1)S(1)} collective-permute-done((bf16[128,1024]{1,0:T(8,128)(2,1)S(1)}, bf16[128,1024]{1,0:T(8,128)(2,1)S(1)}, u32[]{:S(2)}, u32[]{:S(2)}) %collective-permute-start.4) | collective-permute-done | bytes 262176 | tf_op jit(solution)/shard_map/ppermute | solution.py:23
  22.0 0.6 %collective-permute-start.5 = (bf16[128,1024]{1,0:T(8,128)(2,1)S(1)}, bf16[128,1024]{1,0:T(8,128)(2,1)S(1)}, u32[]{:S(2)}, u32[]{:S(2)}) collective-permute-start(bf16[128,1024]{1,0:T(8,128)(2,1)S(1)} %collective-permute-done.4.refs_3_), channel_id=1, source_target_pairs={{0,1},{1,0},{2,3},{3,2},{4,5},{5,4},{6,7},{7,6},{8,9},{9,8},{10,11... | collective-permute-start | bytes 786440 | tf_op jit(solution)/shard_map/ppermute | solution.py:23
  22.6 0.7 %collective-permute-start.6 = (bf16[128,1024]{1,0:T(8,128)(2,1)S(1)}, bf16[128,1024]{1,0:T(8,128)(2,1)S(1)}, u32[]{:S(2)}, u32[]{:S(2)}) collective-permute-start(bf16[128,1024]{1,0:T(8,128)(2,1)S(1)} %get-tuple-element.44), channel_id=1, source_target_pairs={{2,4},{3,5},{4,2},{5,3},{6,8},{7,9},{8,6},{9,7},{10,12},{11,13},{1... | collective-permute-start | bytes 786440 | tf_op jit(solution)/shard_map/ppermute | solution.py:23
  23.3 0.5 collective-permute-done.5.refs_4_
  23.8 0.0 collective-permute-done.3.refs_2_
  23.8 1.7 %scores_next.1 = (bf16[1024,1024]{1,0:T(8,128)(2,1)S(1)}, f32[384,1024]{1,0:T(8,128)S(1)}, f32[384,128]{1,0:T(8,128)S(1)}, f32[384,128]{1,0:T(8,128)S(1)}) custom-call(bf16[256,1024]{1,0:T(8,128)(2,1)S(1)} %collective-permute-done.1.refs_0_, bf16[256,1024]{1,0:T(8,128)(2,1)S(1)} %collective-permute-done.2.refs_1_, ...), custom_call_target="tpu_custom_call" | custom-call | tf_op jit(solution)/shard_map/scores_next/pallas_call | solution.py:195
  25.5 6.7 %collective-permute-done.8.refs_2_ = bf16[256,1024]{1,0:T(8,128)(2,1)S(1)} collective-permute-done((bf16[256,1024]{1,0:T(8,128)(2,1)S(1)}, bf16[256,1024]{1,0:T(8,128)(2,1)S(1)}, u32[]{:S(2)}, u32[]{:S(2)}) %collective-permute-start.8) | collective-permute-done | bytes 524320 | tf_op jit(solution)/shard_map/ppermute | solution.py:23
  32.2 0.8 %collective-permute-start.9 = (bf16[256,1024]{1,0:T(8,128)(2,1)S(1)}, bf16[256,1024]{1,0:T(8,128)(2,1)S(1)}, u32[]{:S(2)}, u32[]{:S(2)}) collective-permute-start(bf16[256,1024]{1,0:T(8,128)(2,1)S(1)} %collective-permute-done.8.refs_2_), channel_id=1, source_target_pairs={{0,1},{1,0},{2,3},{3,2},{4,5},{5,4},{6,7},{7,6},{8,9},{9,8},{10,11... | collective-permute-start | bytes 1572872 | tf_op jit(solution)/shard_map/ppermute | solution.py:23
  33.0 0.0 collective-permute-done.6.refs_0_
  33.0 0.0 collective-permute-start.7
  33.0 1.9 %collective-permute-done.7.refs_1_ = bf16[128,1024]{1,0:T(8,128)(2,1)S(1)} collective-permute-done((bf16[128,1024]{1,0:T(8,128)(2,1)S(1)}, bf16[128,1024]{1,0:T(8,128)(2,1)S(1)}, u32[]{:S(2)}, u32[]{:S(2)}) %collective-permute-start.7) | collective-permute-done | bytes 262176 | tf_op jit(solution)/shard_map/ppermute | solution.py:23
  34.9 0.0 collective-permute-done.9.refs_3_
  34.9 1.5 %scores_last.1 = (bf16[768,1024]{1,0:T(8,128)(2,1)S(1)}, f32[384,768]{1,0:T(8,128)S(1)}, f32[384,128]{1,0:T(8,128)S(1)}, f32[2,384]{1,0:T(2,128)S(1)}) custom-call(bf16[128,1024]{1,0:T(8,128)(2,1)S(1)} %collective-permute-done.6.refs_0_, bf16[128,1024]{1,0:T(8,128)(2,1)S(1)} %collective-permute-done.7.refs_1_, ...), custom_call_target="tpu_custom_call" | custom-call | tf_op jit(solution)/shard_map/scores_last/pallas_call | solution.py:195
  36.4 0.4 collective-permute-start.10
  36.8 0.8 %collective-permute-done.10.refs_11_ = f32[2,384]{1,0:T(2,128)S(1)} collective-permute-done((f32[2,384]{1,0:T(2,128)S(1)}, f32[2,384]{1,0:T(2,128)S(1)}, u32[]{:S(2)}, u32[]{:S(2)}) %collective-permute-start.10) | collective-permute-done | bytes 3104 | tf_op jit(solution)/shard_map/ppermute | solution.py:23
  37.6 1.3 %collective-permute-start.11 = (f32[2,2,384]{2,1,0:T(2,128)S(1)}, f32[2,2,384]{2,1,0:T(2,128)S(1)}, u32[]{:S(2)}, u32[]{:S(2)}) collective-permute-start(f32[2,2,384]{2,1,0:T(2,128)S(1)} %pad_maximum_fusion), channel_id=1, source_target_pairs={{0,2},{2,4},{3,1},{4,6},{5,3},{6,8},{7,5},{8,10},{9,7},{10,12},{11... | collective-permute-start | bytes 18440 | tf_op jit(solution)/shard_map/ppermute | solution.py:23
  38.9 6.4 %collective-permute-start.12 = (f32[2,384]{1,0:T(2,128)S(1)}, f32[2,384]{1,0:T(2,128)S(1)}, u32[]{:S(2)}, u32[]{:S(2)}) collective-permute-start(f32[2,384]{1,0:T(2,128)S(1)} %get-tuple-element.51.refs_10_), channel_id=1, source_target_pairs={{1,4},{3,6},{4,1},{5,8},{6,3},{7,10},{8,5},{9,12},{10,7},{11,14},{... | collective-permute-start | bytes 9224 | tf_op jit(solution)/shard_map/ppermute | solution.py:23
  45.4 2.9 %product_out.1.refs_8_ = f32[384,1024]{1,0:T(8,128)S(1)} custom-call(bf16[768,1024]{1,0:T(8,128)(2,1)S(1)} %get-tuple-element.52.refs_0_, bf16[1024,1024]{1,0:T(8,128)(2,1)S(1)} %get-tuple-element.43.refs_1_.refs_0_, bf16[768,1024]{1,0:T(8,128)(2,1)S(1)} %get-tuple-element.48.refs_2_.refs_1_, f32[384,768]{1,0:T(8,128)S(1)} %get-tuple-element.53.refs_3_, ...), custom_call_target="tpu_custom_call" | custom-call | tf_op jit(solution)/shard_map/product_out/pallas_call | solution.py:269
  48.3 0.0 collective-permute-done.12.refs_5_
  48.3 0.0 collective-permute-done.11.refs_6_
  48.3 0.1 collective-permute-start.13
  48.4 1.2 %collective-permute-done.13.refs_7_ = f32[2,2,384]{2,1,0:T(2,128)S(1)} collective-permute-done((f32[2,2,384]{2,1,0:T(2,128)S(1)}, f32[2,2,384]{2,1,0:T(2,128)S(1)}, u32[]{:S(2)}, u32[]{:S(2)}) %collective-permute-start.13) | collective-permute-done | bytes 6176 | tf_op jit(solution)/shard_map/ppermute | solution.py:23
  49.6 2.6 %product_back.1 = f32[384,1024]{1,0:T(8,128)} custom-call(bf16[1024,1024]{1,0:T(8,128)(2,1)S(1)} %get-tuple-element.43.refs_1_.refs_0_, bf16[768,1024]{1,0:T(8,128)(2,1)S(1)} %get-tuple-element.48.refs_2_.refs_1_, f32[384,1024]{1,0:T(8,128)S(1)} %get-tuple-element.49.refs_4_.refs_2_, f32[384,768]{1,0:T(8,128)S(1)} %get-tuple-element.50.refs_5_.refs_3_, ...), custom_call_target="tpu_custom_call" | custom-call | tf_op jit(solution)/shard_map/product_back/pallas_call | solution.py:269
  (1 shorter events, 0.0 us)
Async XLA Ops:
  0.0 4.1 %collective-permute-start = (bf16[384,1024]{1,0:T(8,128)(2,1)}, bf16[384,1024]{1,0:T(8,128)(2,1)S(1)}, u32[]{:S(2)}, u32[]{:S(2)}) collective-permute-start(bf16[384,1024]{1,0:T(8,128)(2,1)} %refs_7_.1), channel_id=1, source_target_pairs={{0,1},{1,0},{2,3},{3,2},{4,5},{5,4},{6,7},{7,6},{8,9},{9,8},{10,11... | collective-permute-start | bytes 2359304 | tf_op jit(solution)/shard_map/ppermute | solution.py:23
  1.4 15.0 %collective-permute-start.2 = (bf16[256,1024]{1,0:T(8,128)(2,1)S(1)}, bf16[256,1024]{1,0:T(8,128)(2,1)S(1)}, u32[]{:S(2)}, u32[]{:S(2)}) collective-permute-start(bf16[256,1024]{1,0:T(8,128)(2,1)S(1)} %get-tuple-element.34), channel_id=1, source_target_pairs={{0,2},{1,3},{2,0},{3,1},{4,6},{5,7},{6,4},{7,5},{8,10},{9,11},{10,... | collective-permute-start | bytes 1572872 | tf_op jit(solution)/shard_map/ppermute | solution.py:23
  4.1 12.3 %collective-permute-start.1 = (bf16[256,1024]{1,0:T(8,128)(2,1)S(1)}, bf16[256,1024]{1,0:T(8,128)(2,1)S(1)}, u32[]{:S(2)}, u32[]{:S(2)}) collective-permute-start(bf16[256,1024]{1,0:T(8,128)(2,1)S(1)} %get-tuple-element.33), channel_id=1, source_target_pairs={{1,4},{3,6},{4,1},{5,8},{6,3},{7,10},{8,5},{9,12},{10,7},{11,14},{... | collective-permute-start | bytes 1572872 | tf_op jit(solution)/shard_map/ppermute | solution.py:23
  8.2 0.7 %copy-start.1 = (s32[2]{0:T(128)S(1)}, s32[2]{0:T(128)}, u32[]{:S(2)}) copy-start(s32[2]{0:T(128)} %limits_ref.1) | copy-start | bytes 28
  9.6 1.1 %copy-start = (bf16[384,1024]{1,0:T(8,128)(2,1)S(1)}, bf16[384,1024]{1,0:T(8,128)(2,1)}, u32[]{:S(2)}) copy-start(bf16[384,1024]{1,0:T(8,128)(2,1)} %refs_7_.1) | copy-start | bytes 2359300
  12.3 9.7 %collective-permute-start.4 = (bf16[128,1024]{1,0:T(8,128)(2,1)S(1)}, bf16[128,1024]{1,0:T(8,128)(2,1)S(1)}, u32[]{:S(2)}, u32[]{:S(2)}) collective-permute-start(bf16[128,1024]{1,0:T(8,128)(2,1)S(1)} %get-tuple-element.44), channel_id=1, source_target_pairs={{0,2},{1,3},{2,0},{3,1},{4,6},{5,7},{6,4},{7,5},{8,10},{9,11},{10,... | collective-permute-start | bytes 786440 | tf_op jit(solution)/shard_map/ppermute | solution.py:23
  16.4 7.4 %collective-permute-start.3 = (bf16[256,1024]{1,0:T(8,128)(2,1)S(1)}, bf16[256,1024]{1,0:T(8,128)(2,1)S(1)}, u32[]{:S(2)}, u32[]{:S(2)}) collective-permute-start(bf16[256,1024]{1,0:T(8,128)(2,1)S(1)} %collective-permute-done.2.refs_1_), channel_id=1, source_target_pairs={{0,1},{1,0},{2,3},{3,2},{4,5},{5,4},{6,7},{7,6},{8,9},{9,8},{10,11... | collective-permute-start | bytes 1572872 | tf_op jit(solution)/shard_map/ppermute | solution.py:23
  17.2 15.0 %collective-permute-start.8 = (bf16[256,1024]{1,0:T(8,128)(2,1)S(1)}, bf16[256,1024]{1,0:T(8,128)(2,1)S(1)}, u32[]{:S(2)}, u32[]{:S(2)}) collective-permute-start(bf16[256,1024]{1,0:T(8,128)(2,1)S(1)} %collective-permute-done.2.refs_1_), channel_id=1, source_target_pairs={{0,4},{1,5},{4,8},{5,9},{6,2},{7,3},{8,12},{9,13},{10,6},{11,7},{1... | collective-permute-start | bytes 1572872 | tf_op jit(solution)/shard_map/ppermute | solution.py:23
  22.0 1.8 %collective-permute-start.5 = (bf16[128,1024]{1,0:T(8,128)(2,1)S(1)}, bf16[128,1024]{1,0:T(8,128)(2,1)S(1)}, u32[]{:S(2)}, u32[]{:S(2)}) collective-permute-start(bf16[128,1024]{1,0:T(8,128)(2,1)S(1)} %collective-permute-done.4.refs_3_), channel_id=1, source_target_pairs={{0,1},{1,0},{2,3},{3,2},{4,5},{5,4},{6,7},{7,6},{8,9},{9,8},{10,11... | collective-permute-start | bytes 786440 | tf_op jit(solution)/shard_map/ppermute | solution.py:23
  22.6 10.4 %collective-permute-start.6 = (bf16[128,1024]{1,0:T(8,128)(2,1)S(1)}, bf16[128,1024]{1,0:T(8,128)(2,1)S(1)}, u32[]{:S(2)}, u32[]{:S(2)}) collective-permute-start(bf16[128,1024]{1,0:T(8,128)(2,1)S(1)} %get-tuple-element.44), channel_id=1, source_target_pairs={{2,4},{3,5},{4,2},{5,3},{6,8},{7,9},{8,6},{9,7},{10,12},{11,13},{1... | collective-permute-start | bytes 786440 | tf_op jit(solution)/shard_map/ppermute | solution.py:23
  32.2 2.7 %collective-permute-start.9 = (bf16[256,1024]{1,0:T(8,128)(2,1)S(1)}, bf16[256,1024]{1,0:T(8,128)(2,1)S(1)}, u32[]{:S(2)}, u32[]{:S(2)}) collective-permute-start(bf16[256,1024]{1,0:T(8,128)(2,1)S(1)} %collective-permute-done.8.refs_2_), channel_id=1, source_target_pairs={{0,1},{1,0},{2,3},{3,2},{4,5},{5,4},{6,7},{7,6},{8,9},{9,8},{10,11... | collective-permute-start | bytes 1572872 | tf_op jit(solution)/shard_map/ppermute | solution.py:23
  33.0 1.9 %collective-permute-start.7 = (bf16[128,1024]{1,0:T(8,128)(2,1)S(1)}, bf16[128,1024]{1,0:T(8,128)(2,1)S(1)}, u32[]{:S(2)}, u32[]{:S(2)}) collective-permute-start(bf16[128,1024]{1,0:T(8,128)(2,1)S(1)} %collective-permute-done.6.refs_0_), channel_id=1, source_target_pairs={{0,1},{1,0},{2,3},{3,2},{4,5},{5,4},{6,7},{7,6},{8,9},{9,8},{10,11... | collective-permute-start | bytes 786440 | tf_op jit(solution)/shard_map/ppermute | solution.py:23
  36.4 1.2 %collective-permute-start.10 = (f32[2,384]{1,0:T(2,128)S(1)}, f32[2,384]{1,0:T(2,128)S(1)}, u32[]{:S(2)}, u32[]{:S(2)}) collective-permute-start(f32[2,384]{1,0:T(2,128)S(1)} %get-tuple-element.51.refs_10_), channel_id=1, source_target_pairs={{0,1},{1,0},{2,3},{3,2},{4,5},{5,4},{6,7},{7,6},{8,9},{9,8},{10,11... | collective-permute-start | bytes 9224 | tf_op jit(solution)/shard_map/ppermute | solution.py:23
  37.6 10.7 %collective-permute-start.11 = (f32[2,2,384]{2,1,0:T(2,128)S(1)}, f32[2,2,384]{2,1,0:T(2,128)S(1)}, u32[]{:S(2)}, u32[]{:S(2)}) collective-permute-start(f32[2,2,384]{2,1,0:T(2,128)S(1)} %pad_maximum_fusion), channel_id=1, source_target_pairs={{0,2},{2,4},{3,1},{4,6},{5,3},{6,8},{7,5},{8,10},{9,7},{10,12},{11... | collective-permute-start | bytes 18440 | tf_op jit(solution)/shard_map/ppermute | solution.py:23
  38.9 9.4 %collective-permute-start.12 = (f32[2,384]{1,0:T(2,128)S(1)}, f32[2,384]{1,0:T(2,128)S(1)}, u32[]{:S(2)}, u32[]{:S(2)}) collective-permute-start(f32[2,384]{1,0:T(2,128)S(1)} %get-tuple-element.51.refs_10_), channel_id=1, source_target_pairs={{1,4},{3,6},{4,1},{5,8},{6,3},{7,10},{8,5},{9,12},{10,7},{11,14},{... | collective-permute-start | bytes 9224 | tf_op jit(solution)/shard_map/ppermute | solution.py:23
  48.3 1.2 %collective-permute-start.13 = (f32[2,2,384]{2,1,0:T(2,128)S(1)}, f32[2,2,384]{2,1,0:T(2,128)S(1)}, u32[]{:S(2)}, u32[]{:S(2)}) collective-permute-start(f32[2,2,384]{2,1,0:T(2,128)S(1)} %collective-permute-done.11.refs_6_), channel_id=1, source_target_pairs={{0,1},{1,0},{2,3},{3,2},{4,5},{5,4},{6,7},{7,6},{8,9},{9,8},{10,11... | collective-permute-start | bytes 18440 | tf_op jit(solution)/shard_map/ppermute | solution.py:23

commit v4 on v3

--- a/solution.py
+++ b/solution.py
@@ -45,10 +45,6 @@
 
 def to_far(i):
     return i + 3 if i & 1 else i - 3
-
-
-def to_side(i):
-    return i - 2 if i & 1 else i + 2
 
 
 def is_second(axis_index, bit):
@@ -229,14 +225,11 @@
 
 def product_back_kernel(count, split, tail, *refs):
     windows, scores = refs[:count], refs[count : 2 * count]
-    column_ref, far_note, side_ref, other_ref, base_ref, out_ref, held_ref, sems = refs[2 * count :]
+    column_ref, far_note, pair_ref, cross_ref, other_ref, base_ref, out_ref, held_ref, sems = refs[2 * count :]
     rows = column_ref.shape[0]
     core = is_second(lax.axis_index("sub"), 1)
-    swap = core == is_second(lax.axis_index("sub"), 2)
-    pair = jnp.where(swap, other_ref[1], side_ref[0])
-    pair_mate = jnp.where(swap, other_ref[0], side_ref[1])
-    cross = jnp.where(swap, side_ref[0], other_ref[1])
-    cross_mate = jnp.where(swap, side_ref[1], other_ref[0])
+    pair, cross = pair_ref[...], cross_ref[...]
+    pair_mate, cross_mate = other_ref[0], other_ref[1]
     far = jnp.where(core == 1, far_note[:, :tail], far_note[:, rows - tail :])
     notes = jnp.concatenate(
         [
@@ -315,18 +308,19 @@
     log_sum, note = score([cross_rest, cross_mate_rest, cross_head, cross_mate_head], state, True)
 
     mate_note = shift(note, count, to_core)
-    side = shift(jnp.stack([note, mate_note]), count, to_side)
+    pair_note = shift(note, count, to_pair)
     far_note = shift(note, count, to_far)
+    cross_note = shift(pair_note, count, to_next)
     base = product_of(
         functools.partial(product_out_kernel, len(windows)),
         (*windows, *scores, column, positive, log_sum, row, note, mate_note),
         [], VMEM, "product_out",
     )
-    side, far_note, base = lax.optimization_barrier((side, far_note, base))
-    other = shift(side, count, to_core)
+    cross_note, far_note, base = lax.optimization_barrier((cross_note, far_note, base))
+    other = shift(jnp.stack([pair_note, cross_note]), count, to_core)
     return product_of(
         functools.partial(product_back_kernel, len(windows) - 1, split, tail),
-        (*windows[1:], *scores[1:], column, far_note, side, other, base),
+        (*windows[1:], *scores[1:], column, far_note, pair_note, cross_note, other, base),
         [pltpu.VMEM((rows, depth), jnp.float32), pltpu.SemaphoreType.DMA((depth // STEP,))],
         pl.BlockSpec(memory_space=pl.ANY), "product_back",
     )

time: 52.6 us -> 52.7 us (level)
  starting transfers between devices: 21.8 us -> 22.7 us
  waiting for transfers between devices: 15.5 us -> 14.7 us
    ppermute x14 -> x15, starting transfers between devices: 21.8 us -> 22.7 us  [shift(): return lax.ppermute(x, AXES, pairs)]
    ppermute x14 -> x15, waiting for transfers between devices: 15.5 us -> 14.7 us  [shift(): return lax.ppermute(x, AXES, pairs)]
  transfers between devices with their start and end apart: 14 -> 15, of which waited for: 7 -> 6; matrix products, arithmetic and copies ran while one was open for 1% -> 1% of each run, Pallas kernels for 16% -> 16%
where the time goes in v4:
time: 52.7 us; the launch traced here: 52.3 us
  starting transfers between devices  22.7 us (43%)
  waiting for transfers between devices  14.7 us (28%)
  Pallas kernels  12.3 us (23%)
  local copies, waits for them, and re-layouts  2.47 us (5%)
    ppermute x15, starting transfers between devices, shift(): return lax.ppermute(x, AXES, pairs)  22.7 us
    ppermute x15, waiting for transfers between devices, shift(): return lax.ppermute(x, AXES, pairs)  14.7 us
    pallas_call x2, Pallas kernels, product_of(): pl.pallas_call(kernel, out_shape=jax.ShapeDtypeStruct((rows, depth), jnp....  5.53 us
    pallas_call x3, Pallas kernels, scores_of(): pl.pallas_call(functools.partial(score_kernel, sizes, low, first, last),...  4.76 us
    unnamed x4, local copies, waits for them, and re-layouts  1.78 us
    pallas_call x1, Pallas kernels, parts_of(): pl.pallas_call(parts_kernel, out_shape=[pltpu.VMEM((size, depth), own.dty...  1.33 us
  transfers between devices with their start and end apart: 15, of which 6 were waited for; matrix products, arithmetic and copies ran while one was open for 1% of the time, Pallas kernels for 16%

profile of v4, /device:TPU:1, one launch (start us, length us, event | category | flops | bytes accessed | tf_op | source)
XLA Modules:
  0.0 52.3 jit_solution(9201804288624556083)
XLA Ops:
  0.0 0.1 collective-permute-start
  0.1 1.3 %parts.1 = (bf16[256,1024]{1,0:T(8,128)(2,1)S(1)}, bf16[128,1024]{1,0:T(8,128)(2,1)S(1)}, bf16[256,1024]{1,0:T(8,128)(2,1)S(1)}) custom-call(bf16[384,1024]{1,0:T(8,128)(2,1)} %refs_7_.1), custom_call_target="tpu_custom_call" | custom-call | tf_op jit(solution)/shard_map/parts/pallas_call | solution.py:71
  1.4 2.7 %collective-permute-start.2 = (bf16[256,1024]{1,0:T(8,128)(2,1)S(1)}, bf16[256,1024]{1,0:T(8,128)(2,1)S(1)}, u32[]{:S(2)}, u32[]{:S(2)}) collective-permute-start(bf16[256,1024]{1,0:T(8,128)(2,1)S(1)} %get-tuple-element.34), channel_id=1, source_target_pairs={{0,2},{1,3},{2,0},{3,1},{4,6},{5,7},{6,4},{7,5},{8,10},{9,11},{10,... | collective-permute-start | bytes 1572872 | tf_op jit(solution)/shard_map/ppermute | solution.py:23
  4.1 0.0 collective-permute-done.refs_1_
  4.1 3.4 %collective-permute-start.1 = (bf16[256,1024]{1,0:T(8,128)(2,1)S(1)}, bf16[256,1024]{1,0:T(8,128)(2,1)S(1)}, u32[]{:S(2)}, u32[]{:S(2)}) collective-permute-start(bf16[256,1024]{1,0:T(8,128)(2,1)S(1)} %get-tuple-element.33), channel_id=1, source_target_pairs={{1,4},{3,6},{4,1},{5,8},{6,3},{7,10},{8,5},{9,12},{10,7},{11,14},{... | collective-permute-start | bytes 1572872 | tf_op jit(solution)/shard_map/ppermute | solution.py:23
  7.5 0.7 %broadcast_in_dim.3.offset_ref = s32[1,384]{1,0:T(1,128)S(1)} reshape(s32[384]{0:T(512)} %param.4) | data formatting | bytes 3072 | tf_op jit(solution)/shard_map/broadcast_in_dim | solution.py:287
  8.2 0.0 copy-start.1
  8.2 0.7 %copy-done.1 = s32[2]{0:T(128)S(1)} copy-done((s32[2]{0:T(128)S(1)}, s32[2]{0:T(128)}, u32[]{:S(2)}) %copy-start.1) | copy-done | bytes 32
  8.9 0.7 %index.1 = (f32[1,2560]{1,0:T(1,128)S(1)}, f32[384,1]{1,0:T(8,128)S(1)}, f32[384,1]{1,0:T(8,128)S(1)}, f32[1,384]{1,0:T(1,128)S(1)}) custom-call(s32[2]{0:T(128)S(1)} %copy-done.1, s32[1,384]{1,0:T(1,128)S(1)} %broadcast_in_dim.3.offset_ref), custom_call_target="tpu_custom_call" | custom-call | tf_op jit(solution)/shard_map/index/pallas_call | solution.py:118
  9.6 0.0 copy-start
  9.6 1.1 %copy-done = bf16[384,1024]{1,0:T(8,128)(2,1)S(1)} copy-done((bf16[384,1024]{1,0:T(8,128)(2,1)S(1)}, bf16[384,1024]{1,0:T(8,128)(2,1)}, u32[]{:S(2)}) %copy-start) | copy-done | bytes 786456
  10.7 1.5 %scores_first.1 = (bf16[768,1024]{1,0:T(8,128)(2,1)S(1)}, f32[384,768]{1,0:T(8,128)S(1)}, f32[384,128]{1,0:T(8,128)S(1)}, f32[384,128]{1,0:T(8,128)S(1)}) custom-call(bf16[384,1024]{1,0:T(8,128)(2,1)S(1)} %copy-done, bf16[384,1024]{1,0:T(8,128)(2,1)S(1)} %collective-permute-done.refs_1_, f32[384,1]{1,0:T(8,128)S(1)} %get-tuple-element.35.refs_2_.refs_5_.refs_4_.refs_6_, ...), custom_call_target="tpu_custom_call" | custom-call | tf_op jit(solution)/shard_map/scores_first/pallas_call | solution.py:191
  12.3 0.8 %collective-permute-start.4 = (bf16[128,1024]{1,0:T(8,128)(2,1)S(1)}, bf16[128,1024]{1,0:T(8,128)(2,1)S(1)}, u32[]{:S(2)}, u32[]{:S(2)}) collective-permute-start(bf16[128,1024]{1,0:T(8,128)(2,1)S(1)} %get-tuple-element.44), channel_id=1, source_target_pairs={{0,2},{1,3},{2,0},{3,1},{4,6},{5,7},{6,4},{7,5},{8,10},{9,11},{10,... | collective-permute-start | bytes 786440 | tf_op jit(solution)/shard_map/ppermute | solution.py:23
  13.1 3.3 %collective-permute-done.2.refs_1_ = bf16[256,1024]{1,0:T(8,128)(2,1)S(1)} collective-permute-done((bf16[256,1024]{1,0:T(8,128)(2,1)S(1)}, bf16[256,1024]{1,0:T(8,128)(2,1)S(1)}, u32[]{:S(2)}, u32[]{:S(2)}) %collective-permute-start.2) | collective-permute-done | bytes 524320 | tf_op jit(solution)/shard_map/ppermute | solution.py:23
  16.4 0.0 collective-permute-done.1.refs_0_
  16.4 0.8 %collective-permute-start.3 = (bf16[256,1024]{1,0:T(8,128)(2,1)S(1)}, bf16[256,1024]{1,0:T(8,128)(2,1)S(1)}, u32[]{:S(2)}, u32[]{:S(2)}) collective-permute-start(bf16[256,1024]{1,0:T(8,128)(2,1)S(1)} %collective-permute-done.2.refs_1_), channel_id=1, source_target_pairs={{0,1},{1,0},{2,3},{3,2},{4,5},{5,4},{6,7},{7,6},{8,9},{9,8},{10,11... | collective-permute-start | bytes 1572872 | tf_op jit(solution)/shard_map/ppermute | solution.py:23
  17.2 3.7 %collective-permute-start.8 = (bf16[256,1024]{1,0:T(8,128)(2,1)S(1)}, bf16[256,1024]{1,0:T(8,128)(2,1)S(1)}, u32[]{:S(2)}, u32[]{:S(2)}) collective-permute-start(bf16[256,1024]{1,0:T(8,128)(2,1)S(1)} %collective-permute-done.2.refs_1_), channel_id=1, source_target_pairs={{0,4},{1,5},{4,8},{5,9},{6,2},{7,3},{8,12},{9,13},{10,6},{11,7},{1... | collective-permute-start | bytes 1572872 | tf_op jit(solution)/shard_map/ppermute | solution.py:23
  20.9 1.1 %collective-permute-done.4.refs_3_ = bf16[128,1024]{1,0:T(8,128)(2,1)S(1)} collective-permute-done((bf16[128,1024]{1,0:T(8,128)(2,1)S(1)}, bf16[128,1024]{1,0:T(8,128)(2,1)S(1)}, u32[]{:S(2)}, u32[]{:S(2)}) %collective-permute-start.4) | collective-permute-done | bytes 262176 | tf_op jit(solution)/shard_map/ppermute | solution.py:23
  22.0 0.6 %collective-permute-start.5 = (bf16[128,1024]{1,0:T(8,128)(2,1)S(1)}, bf16[128,1024]{1,0:T(8,128)(2,1)S(1)}, u32[]{:S(2)}, u32[]{:S(2)}) collective-permute-start(bf16[128,1024]{1,0:T(8,128)(2,1)S(1)} %collective-permute-done.4.refs_3_), channel_id=1, source_target_pairs={{0,1},{1,0},{2,3},{3,2},{4,5},{5,4},{6,7},{7,6},{8,9},{9,8},{10,11... | collective-permute-start | bytes 786440 | tf_op jit(solution)/shard_map/ppermute | solution.py:23
  22.6 0.7 %collective-permute-start.6 = (bf16[128,1024]{1,0:T(8,128)(2,1)S(1)}, bf16[128,1024]{1,0:T(8,128)(2,1)S(1)}, u32[]{:S(2)}, u32[]{:S(2)}) collective-permute-start(bf16[128,1024]{1,0:T(8,128)(2,1)S(1)} %get-tuple-element.44), channel_id=1, source_target_pairs={{2,4},{3,5},{4,2},{5,3},{6,8},{7,9},{8,6},{9,7},{10,12},{11,13},{1... | collective-permute-start | bytes 786440 | tf_op jit(solution)/shard_map/ppermute | solution.py:23
  23.3 0.5 collective-permute-done.5.refs_4_
  23.8 0.0 collective-permute-done.3.refs_2_
  23.8 1.7 %scores_next.1 = (bf16[1024,1024]{1,0:T(8,128)(2,1)S(1)}, f32[384,1024]{1,0:T(8,128)S(1)}, f32[384,128]{1,0:T(8,128)S(1)}, f32[384,128]{1,0:T(8,128)S(1)}) custom-call(bf16[256,1024]{1,0:T(8,128)(2,1)S(1)} %collective-permute-done.1.refs_0_, bf16[256,1024]{1,0:T(8,128)(2,1)S(1)} %collective-permute-done.2.refs_1_, ...), custom_call_target="tpu_custom_call" | custom-call | tf_op jit(solution)/shard_map/scores_next/pallas_call | solution.py:191
  25.5 6.7 %collective-permute-done.8.refs_2_ = bf16[256,1024]{1,0:T(8,128)(2,1)S(1)} collective-permute-done((bf16[256,1024]{1,0:T(8,128)(2,1)S(1)}, bf16[256,1024]{1,0:T(8,128)(2,1)S(1)}, u32[]{:S(2)}, u32[]{:S(2)}) %collective-permute-start.8) | collective-permute-done | bytes 524320 | tf_op jit(solution)/shard_map/ppermute | solution.py:23
  32.2 0.8 %collective-permute-start.9 = (bf16[256,1024]{1,0:T(8,128)(2,1)S(1)}, bf16[256,1024]{1,0:T(8,128)(2,1)S(1)}, u32[]{:S(2)}, u32[]{:S(2)}) collective-permute-start(bf16[256,1024]{1,0:T(8,128)(2,1)S(1)} %collective-permute-done.8.refs_2_), channel_id=1, source_target_pairs={{0,1},{1,0},{2,3},{3,2},{4,5},{5,4},{6,7},{7,6},{8,9},{9,8},{10,11... | collective-permute-start | bytes 1572872 | tf_op jit(solution)/shard_map/ppermute | solution.py:23
  33.0 0.0 collective-permute-done.6.refs_0_
  33.0 0.0 collective-permute-start.7
  33.0 1.9 %collective-permute-done.7.refs_1_ = bf16[128,1024]{1,0:T(8,128)(2,1)S(1)} collective-permute-done((bf16[128,1024]{1,0:T(8,128)(2,1)S(1)}, bf16[128,1024]{1,0:T(8,128)(2,1)S(1)}, u32[]{:S(2)}, u32[]{:S(2)}) %collective-permute-start.7) | collective-permute-done | bytes 262176 | tf_op jit(solution)/shard_map/ppermute | solution.py:23
  34.9 0.0 collective-permute-done.9.refs_3_
  34.9 1.5 %scores_last.1 = (bf16[768,1024]{1,0:T(8,128)(2,1)S(1)}, f32[384,768]{1,0:T(8,128)S(1)}, f32[384,128]{1,0:T(8,128)S(1)}, f32[2,384]{1,0:T(2,128)S(1)}) custom-call(bf16[128,1024]{1,0:T(8,128)(2,1)S(1)} %collective-permute-done.6.refs_0_, bf16[128,1024]{1,0:T(8,128)(2,1)S(1)} %collective-permute-done.7.refs_1_, ...), custom_call_target="tpu_custom_call" | custom-call | tf_op jit(solution)/shard_map/scores_last/pallas_call | solution.py:191
  36.4 2.2 %collective-permute-start.10 = (f32[2,384]{1,0:T(2,128)S(1)}, f32[2,384]{1,0:T(2,128)S(1)}, u32[]{:S(2)}, u32[]{:S(2)}) collective-permute-start(f32[2,384]{1,0:T(2,128)S(1)} %get-tuple-element.51.refs_10_), channel_id=1, source_target_pairs={{0,2},{1,3},{2,0},{3,1},{4,6},{5,7},{6,4},{7,5},{8,10},{9,11},{10,... | collective-permute-start | bytes 9224 | tf_op jit(solution)/shard_map/ppermute | solution.py:23
  38.5 0.7 %collective-permute-start.13 = (f32[2,384]{1,0:T(2,128)S(1)}, f32[2,384]{1,0:T(2,128)S(1)}, u32[]{:S(2)}, u32[]{:S(2)}) collective-permute-start(f32[2,384]{1,0:T(2,128)S(1)} %get-tuple-element.51.refs_10_), channel_id=1, source_target_pairs={{0,1},{1,0},{2,3},{3,2},{4,5},{5,4},{6,7},{7,6},{8,9},{9,8},{10,11... | collective-permute-start | bytes 9224 | tf_op jit(solution)/shard_map/ppermute | solution.py:23
  39.2 3.1 %collective-permute-start.12 = (f32[2,384]{1,0:T(2,128)S(1)}, f32[2,384]{1,0:T(2,128)S(1)}, u32[]{:S(2)}, u32[]{:S(2)}) collective-permute-start(f32[2,384]{1,0:T(2,128)S(1)} %get-tuple-element.51.refs_10_), channel_id=1, source_target_pairs={{1,4},{3,6},{4,1},{5,8},{6,3},{7,10},{8,5},{9,12},{10,7},{11,14},{... | collective-permute-start | bytes 9224 | tf_op jit(solution)/shard_map/ppermute | solution.py:23
  42.3 0.0 collective-permute-done.10.refs_6_
  42.3 3.2 %collective-permute-start.11 = (f32[2,384]{1,0:T(2,128)S(1)}, f32[2,384]{1,0:T(2,128)S(1)}, u32[]{:S(2)}, u32[]{:S(2)}) collective-permute-start(f32[2,384]{1,0:T(2,128)S(1)} %collective-permute-done.10.refs_6_), channel_id=1, source_target_pairs={{0,4},{1,5},{4,8},{5,9},{6,2},{7,3},{8,12},{9,13},{10,6},{11,7},{1... | collective-permute-start | bytes 9224 | tf_op jit(solution)/shard_map/ppermute | solution.py:23
  45.5 0.0 collective-permute-done.13.refs_11_
  45.5 2.9 %product_out.1.refs_9_ = f32[384,1024]{1,0:T(8,128)S(1)} custom-call(bf16[768,1024]{1,0:T(8,128)(2,1)S(1)} %get-tuple-element.52.refs_0_, bf16[1024,1024]{1,0:T(8,128)(2,1)S(1)} %get-tuple-element.43.refs_1_.refs_0_, bf16[768,1024]{1,0:T(8,128)(2,1)S(1)} %get-tuple-element.48.refs_2_.refs_1_, f32[384,768]{1,0:T(8,128)S(1)} %get-tuple-element.53.refs_3_, ...), custom_call_target="tpu_custom_call" | custom-call | tf_op jit(solution)/shard_map/product_out/pallas_call | solution.py:262
  48.4 0.0 collective-permute-done.12.refs_5_
  48.4 0.0 collective-permute-done.11.refs_7_
  48.5 0.1 collective-permute-start.14
  48.6 1.2 %collective-permute-done.14.refs_8_ = f32[2,2,384]{2,1,0:T(2,128)S(1)} collective-permute-done((f32[2,2,384]{2,1,0:T(2,128)S(1)}, f32[2,2,384]{2,1,0:T(2,128)S(1)}, u32[]{:S(2)}, u32[]{:S(2)}) %collective-permute-start.14) | collective-permute-done | bytes 6176 | tf_op jit(solution)/shard_map/ppermute | solution.py:23
  49.7 2.6 %product_back.1 = f32[384,1024]{1,0:T(8,128)} custom-call(bf16[1024,1024]{1,0:T(8,128)(2,1)S(1)} %get-tuple-element.43.refs_1_.refs_0_, bf16[768,1024]{1,0:T(8,128)(2,1)S(1)} %get-tuple-element.48.refs_2_.refs_1_, f32[384,1024]{1,0:T(8,128)S(1)} %get-tuple-element.49.refs_4_.refs_2_, f32[384,768]{1,0:T(8,128)S(1)} %get-tuple-element.50.refs_5_.refs_3_, ...), custom_call_target="tpu_custom_call" | custom-call | tf_op jit(solution)/shard_map/product_back/pallas_call | solution.py:262
  (1 shorter events, 0.0 us)
Async XLA Ops:
  0.0 4.1 %collective-permute-start = (bf16[384,1024]{1,0:T(8,128)(2,1)}, bf16[384,1024]{1,0:T(8,128)(2,1)S(1)}, u32[]{:S(2)}, u32[]{:S(2)}) collective-permute-start(bf16[384,1024]{1,0:T(8,128)(2,1)} %refs_7_.1), channel_id=1, source_target_pairs={{0,1},{1,0},{2,3},{3,2},{4,5},{5,4},{6,7},{7,6},{8,9},{9,8},{10,11... | collective-permute-start | bytes 2359304 | tf_op jit(solution)/shard_map/ppermute | solution.py:23
  1.4 15.0 %collective-permute-start.2 = (bf16[256,1024]{1,0:T(8,128)(2,1)S(1)}, bf16[256,1024]{1,0:T(8,128)(2,1)S(1)}, u32[]{:S(2)}, u32[]{:S(2)}) collective-permute-start(bf16[256,1024]{1,0:T(8,128)(2,1)S(1)} %get-tuple-element.34), channel_id=1, source_target_pairs={{0,2},{1,3},{2,0},{3,1},{4,6},{5,7},{6,4},{7,5},{8,10},{9,11},{10,... | collective-permute-start | bytes 1572872 | tf_op jit(solution)/shard_map/ppermute | solution.py:23
  4.1 12.3 %collective-permute-start.1 = (bf16[256,1024]{1,0:T(8,128)(2,1)S(1)}, bf16[256,1024]{1,0:T(8,128)(2,1)S(1)}, u32[]{:S(2)}, u32[]{:S(2)}) collective-permute-start(bf16[256,1024]{1,0:T(8,128)(2,1)S(1)} %get-tuple-element.33), channel_id=1, source_target_pairs={{1,4},{3,6},{4,1},{5,8},{6,3},{7,10},{8,5},{9,12},{10,7},{11,14},{... | collective-permute-start | bytes 1572872 | tf_op jit(solution)/shard_map/ppermute | solution.py:23
  8.2 0.7 %copy-start.1 = (s32[2]{0:T(128)S(1)}, s32[2]{0:T(128)}, u32[]{:S(2)}) copy-start(s32[2]{0:T(128)} %limits_ref.1) | copy-start | bytes 28
  9.6 1.1 %copy-start = (bf16[384,1024]{1,0:T(8,128)(2,1)S(1)}, bf16[384,1024]{1,0:T(8,128)(2,1)}, u32[]{:S(2)}) copy-start(bf16[384,1024]{1,0:T(8,128)(2,1)} %refs_7_.1) | copy-start | bytes 2359300
  12.3 9.7 %collective-permute-start.4 = (bf16[128,1024]{1,0:T(8,128)(2,1)S(1)}, bf16[128,1024]{1,0:T(8,128)(2,1)S(1)}, u32[]{:S(2)}, u32[]{:S(2)}) collective-permute-start(bf16[128,1024]{1,0:T(8,128)(2,1)S(1)} %get-tuple-element.44), channel_id=1, source_target_pairs={{0,2},{1,3},{2,0},{3,1},{4,6},{5,7},{6,4},{7,5},{8,10},{9,11},{10,... | collective-permute-start | bytes 786440 | tf_op jit(solution)/shard_map/ppermute | solution.py:23
  16.4 7.4 %collective-permute-start.3 = (bf16[256,1024]{1,0:T(8,128)(2,1)S(1)}, bf16[256,1024]{1,0:T(8,128)(2,1)S(1)}, u32[]{:S(2)}, u32[]{:S(2)}) collective-permute-start(bf16[256,1024]{1,0:T(8,128)(2,1)S(1)} %collective-permute-done.2.refs_1_), channel_id=1, source_target_pairs={{0,1},{1,0},{2,3},{3,2},{4,5},{5,4},{6,7},{7,6},{8,9},{9,8},{10,11... | collective-permute-start | bytes 1572872 | tf_op jit(solution)/shard_map/ppermute | solution.py:23
  17.2 15.0 %collective-permute-start.8 = (bf16[256,1024]{1,0:T(8,128)(2,1)S(1)}, bf16[256,1024]{1,0:T(8,128)(2,1)S(1)}, u32[]{:S(2)}, u32[]{:S(2)}) collective-permute-start(bf16[256,1024]{1,0:T(8,128)(2,1)S(1)} %collective-permute-done.2.refs_1_), channel_id=1, source_target_pairs={{0,4},{1,5},{4,8},{5,9},{6,2},{7,3},{8,12},{9,13},{10,6},{11,7},{1... | collective-permute-start | bytes 1572872 | tf_op jit(solution)/shard_map/ppermute | solution.py:23
  22.0 1.8 %collective-permute-start.5 = (bf16[128,1024]{1,0:T(8,128)(2,1)S(1)}, bf16[128,1024]{1,0:T(8,128)(2,1)S(1)}, u32[]{:S(2)}, u32[]{:S(2)}) collective-permute-start(bf16[128,1024]{1,0:T(8,128)(2,1)S(1)} %collective-permute-done.4.refs_3_), channel_id=1, source_target_pairs={{0,1},{1,0},{2,3},{3,2},{4,5},{5,4},{6,7},{7,6},{8,9},{9,8},{10,11... | collective-permute-start | bytes 786440 | tf_op jit(solution)/shard_map/ppermute | solution.py:23
  22.6 10.4 %collective-permute-start.6 = (bf16[128,1024]{1,0:T(8,128)(2,1)S(1)}, bf16[128,1024]{1,0:T(8,128)(2,1)S(1)}, u32[]{:S(2)}, u32[]{:S(2)}) collective-permute-start(bf16[128,1024]{1,0:T(8,128)(2,1)S(1)} %get-tuple-element.44), channel_id=1, source_target_pairs={{2,4},{3,5},{4,2},{5,3},{6,8},{7,9},{8,6},{9,7},{10,12},{11,13},{1... | collective-permute-start | bytes 786440 | tf_op jit(solution)/shard_map/ppermute | solution.py:23
  32.2 2.7 %collective-permute-start.9 = (bf16[256,1024]{1,0:T(8,128)(2,1)S(1)}, bf16[256,1024]{1,0:T(8,128)(2,1)S(1)}, u32[]{:S(2)}, u32[]{:S(2)}) collective-permute-start(bf16[256,1024]{1,0:T(8,128)(2,1)S(1)} %collective-permute-done.8.refs_2_), channel_id=1, source_target_pairs={{0,1},{1,0},{2,3},{3,2},{4,5},{5,4},{6,7},{7,6},{8,9},{9,8},{10,11... | collective-permute-start | bytes 1572872 | tf_op jit(solution)/shard_map/ppermute | solution.py:23
  33.0 1.9 %collective-permute-start.7 = (bf16[128,1024]{1,0:T(8,128)(2,1)S(1)}, bf16[128,1024]{1,0:T(8,128)(2,1)S(1)}, u32[]{:S(2)}, u32[]{:S(2)}) collective-permute-start(bf16[128,1024]{1,0:T(8,128)(2,1)S(1)} %collective-permute-done.6.refs_0_), channel_id=1, source_target_pairs={{0,1},{1,0},{2,3},{3,2},{4,5},{5,4},{6,7},{7,6},{8,9},{9,8},{10,11... | collective-permute-start | bytes 786440 | tf_op jit(solution)/shard_map/ppermute | solution.py:23
  36.4 5.9 %collective-permute-start.10 = (f32[2,384]{1,0:T(2,128)S(1)}, f32[2,384]{1,0:T(2,128)S(1)}, u32[]{:S(2)}, u32[]{:S(2)}) collective-permute-start(f32[2,384]{1,0:T(2,128)S(1)} %get-tuple-element.51.refs_10_), channel_id=1, source_target_pairs={{0,2},{1,3},{2,0},{3,1},{4,6},{5,7},{6,4},{7,5},{8,10},{9,11},{10,... | collective-permute-start | bytes 9224 | tf_op jit(solution)/shard_map/ppermute | solution.py:23
  38.5 7.0 %collective-permute-start.13 = (f32[2,384]{1,0:T(2,128)S(1)}, f32[2,384]{1,0:T(2,128)S(1)}, u32[]{:S(2)}, u32[]{:S(2)}) collective-permute-start(f32[2,384]{1,0:T(2,128)S(1)} %get-tuple-element.51.refs_10_), channel_id=1, source_target_pairs={{0,1},{1,0},{2,3},{3,2},{4,5},{5,4},{6,7},{7,6},{8,9},{9,8},{10,11... | collective-permute-start | bytes 9224 | tf_op jit(solution)/shard_map/ppermute | solution.py:23
  39.2 9.2 %collective-permute-start.12 = (f32[2,384]{1,0:T(2,128)S(1)}, f32[2,384]{1,0:T(2,128)S(1)}, u32[]{:S(2)}, u32[]{:S(2)}) collective-permute-start(f32[2,384]{1,0:T(2,128)S(1)} %get-tuple-element.51.refs_10_), channel_id=1, source_target_pairs={{1,4},{3,6},{4,1},{5,8},{6,3},{7,10},{8,5},{9,12},{10,7},{11,14},{... | collective-permute-start | bytes 9224 | tf_op jit(solution)/shard_map/ppermute | solution.py:23
  42.3 6.2 %collective-permute-start.11 = (f32[2,384]{1,0:T(2,128)S(1)}, f32[2,384]{1,0:T(2,128)S(1)}, u32[]{:S(2)}, u32[]{:S(2)}) collective-permute-start(f32[2,384]{1,0:T(2,128)S(1)} %collective-permute-done.10.refs_6_), channel_id=1, source_target_pairs={{0,4},{1,5},{4,8},{5,9},{6,2},{7,3},{8,12},{9,13},{10,6},{11,7},{1... | collective-permute-start | bytes 9224 | tf_op jit(solution)/shard_map/ppermute | solution.py:23
  48.5 1.2 %collective-permute-start.14 = (f32[2,2,384]{2,1,0:T(2,128)S(1)}, f32[2,2,384]{2,1,0:T(2,128)S(1)}, u32[]{:S(2)}, u32[]{:S(2)}) collective-permute-start(f32[2,2,384]{2,1,0:T(2,128)S(1)} %pad_maximum_fusion), channel_id=1, source_target_pairs={{0,1},{1,0},{2,3},{3,2},{4,5},{5,4},{6,7},{7,6},{8,9},{9,8},{10,11... | collective-permute-start | bytes 18440 | tf_op jit(solution)/shard_map/ppermute | solution.py:23

commit v5 on v4

--- a/solution.py
+++ b/solution.py
@@ -51,14 +51,19 @@
     return lax.rem(axis_index // bit, 2)
 
 
-def parts_kernel(own_ref, head_ref, rest_ref, tail_ref, sems):
-    split, tail = head_ref.shape[0], tail_ref.shape[0]
+def head_kernel(own_ref, head_ref, sem):
+    copy = pltpu.make_async_copy(own_ref.at[pl.ds(0, head_ref.shape[0])], head_ref, sem)
+    copy.start()
+    copy.wait()
+
+
+def parts_kernel(own_ref, rest_ref, tail_ref, sems):
+    rest, tail = rest_ref.shape[0], tail_ref.shape[0]
     core = is_second(lax.axis_index("sub"), 1)
     first = pl.multiple_of(core * (own_ref.shape[0] - tail), 16)
     copies = [
-        pltpu.make_async_copy(own_ref.at[pl.ds(0, split)], head_ref, sems.at[0]),
-        pltpu.make_async_copy(own_ref.at[pl.ds(split, own_ref.shape[0] - split)], rest_ref, sems.at[1]),
-        pltpu.make_async_copy(own_ref.at[pl.ds(first, tail)], tail_ref, sems.at[2]),
+        pltpu.make_async_copy(own_ref.at[pl.ds(own_ref.shape[0] - rest, rest)], rest_ref, sems.at[0]),
+        pltpu.make_async_copy(own_ref.at[pl.ds(first, tail)], tail_ref, sems.at[1]),
     ]
     for copy in copies:
         copy.start()
@@ -66,17 +71,16 @@
         copy.wait()
 
 
-def parts_of(own, split, tail):
-    rows, depth = own.shape
+def copies_of(kernel, own, sizes, semaphores, name):
     return pl.pallas_call(
-        parts_kernel,
-        out_shape=[pltpu.VMEM((size, depth), own.dtype) for size in (split, rows - split, tail)],
+        kernel,
+        out_shape=[pltpu.VMEM((size, own.shape[1]), own.dtype) for size in sizes],
         in_specs=[pl.BlockSpec(memory_space=pl.ANY)],
-        out_specs=[VMEM] * 3,
-        scratch_shapes=[pltpu.SemaphoreType.DMA((3,))],
+        out_specs=[VMEM] * len(sizes),
+        scratch_shapes=[semaphores],
         compiler_params=PARAMS,
         cost_estimate=COST,
-        name="parts",
+        name=name,
     )(pltpu.with_memory_space_constraint(own, pltpu.HBM))
 
 
@@ -205,9 +209,9 @@
     return weight.astype(jnp.bfloat16)
 
 
-def product_out_kernel(count, *refs):
+def product_out_kernel(count, split, tail, *refs):
     windows, scores = refs[:count], refs[count : 2 * count]
-    column_ref, positive_ref, log_ref, row_ref, own_note, mate_note, out_ref = refs[2 * count :]
+    column_ref, positive_ref, log_ref, row_ref, own_note, mate_note, pair_note, out_ref = refs[2 * count :]
     log_sum, positive = log_ref[:, :1], positive_ref[...]
     weights = []
     low = 0
@@ -217,9 +221,14 @@
         low = high
     notes = jnp.concatenate([own_note[...], mate_note[...]], axis=1)
     weights.append(weight_of(scores[0][...], notes[:1], notes[1:], column_ref[...]))
+    weights.append(
+        weight_of(scores[1][:, tail : tail + split], pair_note[:1, :split], pair_note[1:, :split], column_ref[...])
+    )
     weights = jnp.concatenate(weights, axis=1)
     for low in range(0, out_ref.shape[1], STEP):
-        block = jnp.concatenate([ref[:, low : low + STEP] for ref in (*windows, windows[0])], axis=0)
+        place = slice(low, low + STEP)
+        blocks = [ref[:, place] for ref in (*windows, windows[0])] + [windows[1][tail : tail + split, place]]
+        block = jnp.concatenate(blocks, axis=0)
         out_ref[:, low : low + STEP] = jnp.dot(weights, block, preferred_element_type=jnp.float32)
 
 
@@ -233,22 +242,27 @@
     far = jnp.where(core == 1, far_note[:, :tail], far_note[:, rows - tail :])
     notes = jnp.concatenate(
         [
-            far, pair[:, :split], pair_mate[:, :split], pair[:, split:], pair_mate[:, split:],
+            far, pair_mate[:, :split], pair[:, split:], pair_mate[:, split:],
             cross[:, split:], cross_mate[:, split:], cross[:, :split], cross_mate[:, :split],
         ],
         axis=1,
     )
     weights = []
     low = 0
-    for ref in scores:
-        high = low + ref.shape[1]
-        weights.append(weight_of(ref[...], notes[:1, low:high], notes[1:, low:high], column_ref[...]))
+    for number, ref in enumerate(scores):
+        score = ref[...]
+        if number == 0:
+            score = jnp.concatenate([score[:, :tail], score[:, tail + split :]], axis=1)
+        high = low + score.shape[1]
+        weights.append(weight_of(score, notes[:1, low:high], notes[1:, low:high], column_ref[...]))
         low = high
     weights = jnp.concatenate(weights, axis=1)
     copies = []
     for number, low in enumerate(range(0, out_ref.shape[1], STEP)):
         place = pl.ds(low, STEP)
-        block = jnp.concatenate([ref[:, low : low + STEP] for ref in windows], axis=0)
+        first = windows[0][:, low : low + STEP]
+        blocks = [first[:tail], first[tail + split :]] + [ref[:, low : low + STEP] for ref in windows[1:]]
+        block = jnp.concatenate(blocks, axis=0)
         part = jnp.dot(weights, block, preferred_element_type=jnp.float32)
         held_ref[:, low : low + STEP] = SCALE * (part + base_ref[:, low : low + STEP])
         copies.append(pltpu.make_async_copy(held_ref.at[:, place], out_ref.at[:, place], sems.at[number]))
@@ -279,8 +293,11 @@
     split = 2 * rows // 3
     assert 0 < tail <= rows and split % 16 == 0
 
-    head, rest, tail_rows = parts_of(embeddings, split, tail)
+    head, = copies_of(head_kernel, embeddings, [split], pltpu.SemaphoreType.DMA, "head")
     mate = shift(embeddings, count, to_core)
+    rest, tail_rows = copies_of(
+        parts_kernel, embeddings, [rows - split, tail], pltpu.SemaphoreType.DMA((2,)), "parts"
+    )
     pair_head = shift(head, count, to_pair)
     far = shift(after(tail_rows, mate), count, to_far)
     row, column, positive, positive_row = index_of(
@@ -312,8 +329,8 @@
     far_note = shift(note, count, to_far)
     cross_note = shift(pair_note, count, to_next)
     base = product_of(
-        functools.partial(product_out_kernel, len(windows)),
-        (*windows, *scores, column, positive, log_sum, row, note, mate_note),
+        functools.partial(product_out_kernel, len(windows), split, tail),
+        (*windows, *scores, column, positive, log_sum, row, note, mate_note, pair_note),
         [], VMEM, "product_out",
     )
     cross_note, far_note, base = lax.optimization_barrier((cross_note, far_note, base))

time: 52.7 us -> 52.5 us (level)
  local copies, waits for them, and re-layouts: 2.47 us -> 0.01 us
  waiting for transfers between devices: 14.7 us -> 16.3 us
  Pallas kernels: 12.3 us -> 13.3 us
    unnamed x4 -> x6, local copies, waits for them, and re-layouts: 1.78 us -> 0.01 us
    ppermute x15, waiting for transfers between devices: 14.7 us -> 16.3 us  [shift(): return lax.ppermute(x, AXES, pairs)]
    pallas_call x1 -> x2, Pallas kernels: 1.33 us -> 2.25 us  [copies_of(): pl.pallas_call(kernel, out_shape=[pltpu.VMEM((size, own.shape[1]), own.dt...]
    broadcast_in_dim x1, local copies, waits for them, and re-layouts: 0.69 us -> 0.01 us  [per_device(): offsets[None]]
  transfers between devices with their start and end apart: 15 -> 15, of which waited for: 6 -> 6; matrix products, arithmetic and copies ran while one was open for 1% -> 0% of each run, Pallas kernels for 16% -> 18%
where the time goes in v5:
time: 52.5 us; the launch traced here: 52.2 us
  starting transfers between devices  22.4 us (43%)
  waiting for transfers between devices  16.3 us (31%)
  Pallas kernels  13.3 us (25%)
    ppermute x15, starting transfers between devices, shift(): return lax.ppermute(x, AXES, pairs)  22.4 us
    ppermute x15, waiting for transfers between devices, shift(): return lax.ppermute(x, AXES, pairs)  16.3 us
    pallas_call x2, Pallas kernels, product_of(): pl.pallas_call(kernel, out_shape=jax.ShapeDtypeStruct((rows, depth), jnp....  5.55 us
    pallas_call x3, Pallas kernels, scores_of(): pl.pallas_call(functools.partial(score_kernel, sizes, low, first, last),...  4.73 us
    pallas_call x2, Pallas kernels, copies_of(): pl.pallas_call(kernel, out_shape=[pltpu.VMEM((size, own.shape[1]), own.dt...  2.25 us
  transfers between devices with their start and end apart: 15, of which 6 were waited for; matrix products, arithmetic and copies ran while one was open for 0% of the time, Pallas kernels for 18%

profile of v5, /device:TPU:1, one launch (start us, length us, event | category | flops | bytes accessed | tf_op | source)
XLA Modules:
  0.0 52.2 jit_solution(13259168377261752527)
XLA Ops:
  0.0 0.0 copy-start
  0.0 0.0 copy-start.2
  0.0 0.0 copy-start.1
  0.0 0.1 collective-permute-start
  0.1 1.1 %head.1 = bf16[256,1024]{1,0:T(8,128)(2,1)S(1)} custom-call(bf16[384,1024]{1,0:T(8,128)(2,1)} %refs_7_.1), custom_call_target="tpu_custom_call" | custom-call | tf_op jit(solution)/shard_map/head/pallas_call | solution.py:75
  1.2 2.7 %collective-permute-start.2 = (bf16[256,1024]{1,0:T(8,128)(2,1)S(1)}, bf16[256,1024]{1,0:T(8,128)(2,1)S(1)}, u32[]{:S(2)}, u32[]{:S(2)}) collective-permute-start(bf16[256,1024]{1,0:T(8,128)(2,1)S(1)} %head.1), channel_id=1, source_target_pairs={{0,2},{1,3},{2,0},{3,1},{4,6},{5,7},{6,4},{7,5},{8,10},{9,11},{10,... | collective-permute-start | bytes 1572872 | tf_op jit(solution)/shard_map/ppermute | solution.py:23
  3.9 1.1 %parts.1 = (bf16[128,1024]{1,0:T(8,128)(2,1)S(1)}, bf16[256,1024]{1,0:T(8,128)(2,1)S(1)}) custom-call(bf16[384,1024]{1,0:T(8,128)(2,1)} %refs_7_.1), custom_call_target="tpu_custom_call" | custom-call | tf_op jit(solution)/shard_map/parts/pallas_call | solution.py:75
  5.1 0.0 collective-permute-done.refs_1_
  5.1 3.4 %collective-permute-start.1 = (bf16[256,1024]{1,0:T(8,128)(2,1)S(1)}, bf16[256,1024]{1,0:T(8,128)(2,1)S(1)}, u32[]{:S(2)}, u32[]{:S(2)}) collective-permute-start(bf16[256,1024]{1,0:T(8,128)(2,1)S(1)} %get-tuple-element.32), channel_id=1, source_target_pairs={{1,4},{3,6},{4,1},{5,8},{6,3},{7,10},{8,5},{9,12},{10,7},{11,14},{... | collective-permute-start | bytes 1572872 | tf_op jit(solution)/shard_map/ppermute | solution.py:23
  8.5 0.0 copy-done.2
  8.5 0.0 copy-done.1
  8.6 0.7 %index.1 = (f32[1,2560]{1,0:T(1,128)S(1)}, f32[384,1]{1,0:T(8,128)S(1)}, f32[384,1]{1,0:T(8,128)S(1)}, f32[1,384]{1,0:T(1,128)S(1)}) custom-call(s32[2]{0:T(128)S(1)} %copy-done.1, s32[1,384]{1,0:T(1,128)S(1)} %broadcast_in_dim.3.offset_ref), custom_call_target="tpu_custom_call" | custom-call | tf_op jit(solution)/shard_map/index/pallas_call | solution.py:122
  9.3 0.0 copy-done
  9.3 1.5 %scores_first.1 = (bf16[768,1024]{1,0:T(8,128)(2,1)S(1)}, f32[384,768]{1,0:T(8,128)S(1)}, f32[384,128]{1,0:T(8,128)S(1)}, f32[384,128]{1,0:T(8,128)S(1)}) custom-call(bf16[384,1024]{1,0:T(8,128)(2,1)S(1)} %copy-done, bf16[384,1024]{1,0:T(8,128)(2,1)S(1)} %collective-permute-done.refs_1_, f32[384,1]{1,0:T(8,128)S(1)} %get-tuple-element.33.refs_2_.refs_5_.refs_4_.refs_6_, ...), custom_call_target="tpu_custom_call" | custom-call | tf_op jit(solution)/shard_map/scores_first/pallas_call | solution.py:195
  10.8 0.3 collective-permute-start.4
  11.1 5.0 %collective-permute-done.2.refs_1_ = bf16[256,1024]{1,0:T(8,128)(2,1)S(1)} collective-permute-done((bf16[256,1024]{1,0:T(8,128)(2,1)S(1)}, bf16[256,1024]{1,0:T(8,128)(2,1)S(1)}, u32[]{:S(2)}, u32[]{:S(2)}) %collective-permute-start.2) | collective-permute-done | bytes 524320 | tf_op jit(solution)/shard_map/ppermute | solution.py:23
  16.1 0.0 collective-permute-done.1.refs_0_
  16.1 0.9 %collective-permute-start.3 = (bf16[256,1024]{1,0:T(8,128)(2,1)S(1)}, bf16[256,1024]{1,0:T(8,128)(2,1)S(1)}, u32[]{:S(2)}, u32[]{:S(2)}) collective-permute-start(bf16[256,1024]{1,0:T(8,128)(2,1)S(1)} %collective-permute-done.2.refs_1_), channel_id=1, source_target_pairs={{0,1},{1,0},{2,3},{3,2},{4,5},{5,4},{6,7},{7,6},{8,9},{9,8},{10,11... | collective-permute-start | bytes 1572872 | tf_op jit(solution)/shard_map/ppermute | solution.py:23
  17.0 3.7 %collective-permute-start.8 = (bf16[256,1024]{1,0:T(8,128)(2,1)S(1)}, bf16[256,1024]{1,0:T(8,128)(2,1)S(1)}, u32[]{:S(2)}, u32[]{:S(2)}) collective-permute-start(bf16[256,1024]{1,0:T(8,128)(2,1)S(1)} %collective-permute-done.2.refs_1_), channel_id=1, source_target_pairs={{0,4},{1,5},{4,8},{5,9},{6,2},{7,3},{8,12},{9,13},{10,6},{11,7},{1... | collective-permute-start | bytes 1572872 | tf_op jit(solution)/shard_map/ppermute | solution.py:23
  20.7 1.0 %collective-permute-done.4.refs_3_ = bf16[128,1024]{1,0:T(8,128)(2,1)S(1)} collective-permute-done((bf16[128,1024]{1,0:T(8,128)(2,1)S(1)}, bf16[128,1024]{1,0:T(8,128)(2,1)S(1)}, u32[]{:S(2)}, u32[]{:S(2)}) %collective-permute-start.4) | collective-permute-done | bytes 262176 | tf_op jit(solution)/shard_map/ppermute | solution.py:23
  21.8 0.7 %collective-permute-start.5 = (bf16[128,1024]{1,0:T(8,128)(2,1)S(1)}, bf16[128,1024]{1,0:T(8,128)(2,1)S(1)}, u32[]{:S(2)}, u32[]{:S(2)}) collective-permute-start(bf16[128,1024]{1,0:T(8,128)(2,1)S(1)} %collective-permute-done.4.refs_3_), channel_id=1, source_target_pairs={{0,1},{1,0},{2,3},{3,2},{4,5},{5,4},{6,7},{7,6},{8,9},{9,8},{10,11... | collective-permute-start | bytes 786440 | tf_op jit(solution)/shard_map/ppermute | solution.py:23
  22.4 0.7 %collective-permute-start.6 = (bf16[128,1024]{1,0:T(8,128)(2,1)S(1)}, bf16[128,1024]{1,0:T(8,128)(2,1)S(1)}, u32[]{:S(2)}, u32[]{:S(2)}) collective-permute-start(bf16[128,1024]{1,0:T(8,128)(2,1)S(1)} %get-tuple-element.42), channel_id=1, source_target_pairs={{2,4},{3,5},{4,2},{5,3},{6,8},{7,9},{8,6},{9,7},{10,12},{11,13},{1... | collective-permute-start | bytes 786440 | tf_op jit(solution)/shard_map/ppermute | solution.py:23
  23.1 0.5 collective-permute-done.5.refs_4_
  23.6 0.0 collective-permute-done.3.refs_2_
  23.6 1.7 %scores_next.1 = (bf16[1024,1024]{1,0:T(8,128)(2,1)S(1)}, f32[384,1024]{1,0:T(8,128)S(1)}, f32[384,128]{1,0:T(8,128)S(1)}, f32[384,128]{1,0:T(8,128)S(1)}) custom-call(bf16[256,1024]{1,0:T(8,128)(2,1)S(1)} %collective-permute-done.1.refs_0_, bf16[256,1024]{1,0:T(8,128)(2,1)S(1)} %collective-permute-done.2.refs_1_, ...), custom_call_target="tpu_custom_call" | custom-call | tf_op jit(solution)/shard_map/scores_next/pallas_call | solution.py:195
  25.3 6.7 %collective-permute-done.8.refs_2_ = bf16[256,1024]{1,0:T(8,128)(2,1)S(1)} collective-permute-done((bf16[256,1024]{1,0:T(8,128)(2,1)S(1)}, bf16[256,1024]{1,0:T(8,128)(2,1)S(1)}, u32[]{:S(2)}, u32[]{:S(2)}) %collective-permute-start.8) | collective-permute-done | bytes 524320 | tf_op jit(solution)/shard_map/ppermute | solution.py:23
  32.0 0.8 %collective-permute-start.9 = (bf16[256,1024]{1,0:T(8,128)(2,1)S(1)}, bf16[256,1024]{1,0:T(8,128)(2,1)S(1)}, u32[]{:S(2)}, u32[]{:S(2)}) collective-permute-start(bf16[256,1024]{1,0:T(8,128)(2,1)S(1)} %collective-permute-done.8.refs_2_), channel_id=1, source_target_pairs={{0,1},{1,0},{2,3},{3,2},{4,5},{5,4},{6,7},{7,6},{8,9},{9,8},{10,11... | collective-permute-start | bytes 1572872 | tf_op jit(solution)/shard_map/ppermute | solution.py:23
  32.8 0.0 collective-permute-done.6.refs_0_
  32.8 0.0 collective-permute-start.7
  32.8 1.9 %collective-permute-done.7.refs_1_ = bf16[128,1024]{1,0:T(8,128)(2,1)S(1)} collective-permute-done((bf16[128,1024]{1,0:T(8,128)(2,1)S(1)}, bf16[128,1024]{1,0:T(8,128)(2,1)S(1)}, u32[]{:S(2)}, u32[]{:S(2)}) %collective-permute-start.7) | collective-permute-done | bytes 262176 | tf_op jit(solution)/shard_map/ppermute | solution.py:23
  34.7 0.0 collective-permute-done.9.refs_3_
  34.7 1.5 %scores_last.1 = (bf16[768,1024]{1,0:T(8,128)(2,1)S(1)}, f32[384,768]{1,0:T(8,128)S(1)}, f32[384,128]{1,0:T(8,128)S(1)}, f32[2,384]{1,0:T(2,128)S(1)}) custom-call(bf16[128,1024]{1,0:T(8,128)(2,1)S(1)} %collective-permute-done.6.refs_0_, bf16[128,1024]{1,0:T(8,128)(2,1)S(1)} %collective-permute-done.7.refs_1_, ...), custom_call_target="tpu_custom_call" | custom-call | tf_op jit(solution)/shard_map/scores_last/pallas_call | solution.py:195
  36.2 2.2 %collective-permute-start.10 = (f32[2,384]{1,0:T(2,128)S(1)}, f32[2,384]{1,0:T(2,128)S(1)}, u32[]{:S(2)}, u32[]{:S(2)}) collective-permute-start(f32[2,384]{1,0:T(2,128)S(1)} %get-tuple-element.49.refs_10_), channel_id=1, source_target_pairs={{0,2},{1,3},{2,0},{3,1},{4,6},{5,7},{6,4},{7,5},{8,10},{9,11},{10,... | collective-permute-start | bytes 9224 | tf_op jit(solution)/shard_map/ppermute | solution.py:23
  38.4 0.7 %collective-permute-start.13 = (f32[2,384]{1,0:T(2,128)S(1)}, f32[2,384]{1,0:T(2,128)S(1)}, u32[]{:S(2)}, u32[]{:S(2)}) collective-permute-start(f32[2,384]{1,0:T(2,128)S(1)} %get-tuple-element.49.refs_10_), channel_id=1, source_target_pairs={{0,1},{1,0},{2,3},{3,2},{4,5},{5,4},{6,7},{7,6},{8,9},{9,8},{10,11... | collective-permute-start | bytes 9224 | tf_op jit(solution)/shard_map/ppermute | solution.py:23
  39.0 3.1 %collective-permute-start.12 = (f32[2,384]{1,0:T(2,128)S(1)}, f32[2,384]{1,0:T(2,128)S(1)}, u32[]{:S(2)}, u32[]{:S(2)}) collective-permute-start(f32[2,384]{1,0:T(2,128)S(1)} %get-tuple-element.49.refs_10_), channel_id=1, source_target_pairs={{1,4},{3,6},{4,1},{5,8},{6,3},{7,10},{8,5},{9,12},{10,7},{11,14},{... | collective-permute-start | bytes 9224 | tf_op jit(solution)/shard_map/ppermute | solution.py:23
  42.1 0.0 collective-permute-done.10.refs_12_.refs_6_
  42.1 3.2 %collective-permute-start.11 = (f32[2,384]{1,0:T(2,128)S(1)}, f32[2,384]{1,0:T(2,128)S(1)}, u32[]{:S(2)}, u32[]{:S(2)}) collective-permute-start(f32[2,384]{1,0:T(2,128)S(1)} %collective-permute-done.10.refs_12_.refs_6_), channel_id=1, source_target_pairs={{0,4},{1,5},{4,8},{5,9},{6,2},{7,3},{8,12},{9,13},{10,6},{11,7},{1... | collective-permute-start | bytes 9224 | tf_op jit(solution)/shard_map/ppermute | solution.py:23
  45.3 0.0 collective-permute-done.13.refs_11_
  45.4 3.1 %product_out.1.refs_9_ = f32[384,1024]{1,0:T(8,128)S(1)} custom-call(bf16[768,1024]{1,0:T(8,128)(2,1)S(1)} %get-tuple-element.50.refs_0_, bf16[1024,1024]{1,0:T(8,128)(2,1)S(1)} %get-tuple-element.41.refs_1_.refs_0_, bf16[768,1024]{1,0:T(8,128)(2,1)S(1)} %get-tuple-element.46.refs_2_.refs_1_, f32[384,768]{1,0:T(8,128)S(1)} %get-tuple-element.51.refs_3_, ...), custom_call_target="tpu_custom_call" | custom-call | tf_op jit(solution)/shard_map/product_out/pallas_call | solution.py:276
  48.5 0.0 collective-permute-done.12.refs_5_
  48.5 0.0 collective-permute-done.11.refs_7_
  48.5 0.1 collective-permute-start.14
  48.6 1.2 %collective-permute-done.14.refs_8_ = f32[2,2,384]{2,1,0:T(2,128)S(1)} collective-permute-done((f32[2,2,384]{2,1,0:T(2,128)S(1)}, f32[2,2,384]{2,1,0:T(2,128)S(1)}, u32[]{:S(2)}, u32[]{:S(2)}) %collective-permute-start.14) | collective-permute-done | bytes 6176 | tf_op jit(solution)/shard_map/ppermute | solution.py:23
  49.8 2.4 %product_back.1 = f32[384,1024]{1,0:T(8,128)} custom-call(bf16[1024,1024]{1,0:T(8,128)(2,1)S(1)} %get-tuple-element.41.refs_1_.refs_0_, bf16[768,1024]{1,0:T(8,128)(2,1)S(1)} %get-tuple-element.46.refs_2_.refs_1_, f32[384,1024]{1,0:T(8,128)S(1)} %get-tuple-element.47.refs_4_.refs_2_, f32[384,768]{1,0:T(8,128)S(1)} %get-tuple-element.48.refs_5_.refs_3_, ...), custom_call_target="tpu_custom_call" | custom-call | tf_op jit(solution)/shard_map/product_back/pallas_call | solution.py:276
  (2 shorter events, 0.0 us)
Async XLA Ops:
  0.0 9.3 %copy-start = (bf16[384,1024]{1,0:T(8,128)(2,1)S(1)}, bf16[384,1024]{1,0:T(8,128)(2,1)}, u32[]{:S(2)}) copy-start(bf16[384,1024]{1,0:T(8,128)(2,1)} %refs_7_.1) | copy-start | bytes 2359300
  0.0 8.5 %copy-start.2 = (s32[384]{0:T(512)S(1)}, s32[384]{0:T(512)}, u32[]{:S(2)}) copy-start(s32[384]{0:T(512)} %param.4) | copy-start | bytes 4612
  0.0 8.5 %copy-start.1 = (s32[2]{0:T(128)S(1)}, s32[2]{0:T(128)}, u32[]{:S(2)}) copy-start(s32[2]{0:T(128)} %limits_ref.1) | copy-start | bytes 28
  0.0 5.1 %collective-permute-start = (bf16[384,1024]{1,0:T(8,128)(2,1)}, bf16[384,1024]{1,0:T(8,128)(2,1)S(1)}, u32[]{:S(2)}, u32[]{:S(2)}) collective-permute-start(bf16[384,1024]{1,0:T(8,128)(2,1)} %refs_7_.1), channel_id=1, source_target_pairs={{0,1},{1,0},{2,3},{3,2},{4,5},{5,4},{6,7},{7,6},{8,9},{9,8},{10,11... | collective-permute-start | bytes 2359304 | tf_op jit(solution)/shard_map/ppermute | solution.py:23
  1.2 14.9 %collective-permute-start.2 = (bf16[256,1024]{1,0:T(8,128)(2,1)S(1)}, bf16[256,1024]{1,0:T(8,128)(2,1)S(1)}, u32[]{:S(2)}, u32[]{:S(2)}) collective-permute-start(bf16[256,1024]{1,0:T(8,128)(2,1)S(1)} %head.1), channel_id=1, source_target_pairs={{0,2},{1,3},{2,0},{3,1},{4,6},{5,7},{6,4},{7,5},{8,10},{9,11},{10,... | collective-permute-start | bytes 1572872 | tf_op jit(solution)/shard_map/ppermute | solution.py:23
  5.1 11.1 %collective-permute-start.1 = (bf16[256,1024]{1,0:T(8,128)(2,1)S(1)}, bf16[256,1024]{1,0:T(8,128)(2,1)S(1)}, u32[]{:S(2)}, u32[]{:S(2)}) collective-permute-start(bf16[256,1024]{1,0:T(8,128)(2,1)S(1)} %get-tuple-element.32), channel_id=1, source_target_pairs={{1,4},{3,6},{4,1},{5,8},{6,3},{7,10},{8,5},{9,12},{10,7},{11,14},{... | collective-permute-start | bytes 1572872 | tf_op jit(solution)/shard_map/ppermute | solution.py:23
  10.8 10.9 %collective-permute-start.4 = (bf16[128,1024]{1,0:T(8,128)(2,1)S(1)}, bf16[128,1024]{1,0:T(8,128)(2,1)S(1)}, u32[]{:S(2)}, u32[]{:S(2)}) collective-permute-start(bf16[128,1024]{1,0:T(8,128)(2,1)S(1)} %get-tuple-element.42), channel_id=1, source_target_pairs={{0,2},{1,3},{2,0},{3,1},{4,6},{5,7},{6,4},{7,5},{8,10},{9,11},{10,... | collective-permute-start | bytes 786440 | tf_op jit(solution)/shard_map/ppermute | solution.py:23
  16.1 7.4 %collective-permute-start.3 = (bf16[256,1024]{1,0:T(8,128)(2,1)S(1)}, bf16[256,1024]{1,0:T(8,128)(2,1)S(1)}, u32[]{:S(2)}, u32[]{:S(2)}) collective-permute-start(bf16[256,1024]{1,0:T(8,128)(2,1)S(1)} %collective-permute-done.2.refs_1_), channel_id=1, source_target_pairs={{0,1},{1,0},{2,3},{3,2},{4,5},{5,4},{6,7},{7,6},{8,9},{9,8},{10,11... | collective-permute-start | bytes 1572872 | tf_op jit(solution)/shard_map/ppermute | solution.py:23
  17.0 15.0 %collective-permute-start.8 = (bf16[256,1024]{1,0:T(8,128)(2,1)S(1)}, bf16[256,1024]{1,0:T(8,128)(2,1)S(1)}, u32[]{:S(2)}, u32[]{:S(2)}) collective-permute-start(bf16[256,1024]{1,0:T(8,128)(2,1)S(1)} %collective-permute-done.2.refs_1_), channel_id=1, source_target_pairs={{0,4},{1,5},{4,8},{5,9},{6,2},{7,3},{8,12},{9,13},{10,6},{11,7},{1... | collective-permute-start | bytes 1572872 | tf_op jit(solution)/shard_map/ppermute | solution.py:23
  21.8 1.8 %collective-permute-start.5 = (bf16[128,1024]{1,0:T(8,128)(2,1)S(1)}, bf16[128,1024]{1,0:T(8,128)(2,1)S(1)}, u32[]{:S(2)}, u32[]{:S(2)}) collective-permute-start(bf16[128,1024]{1,0:T(8,128)(2,1)S(1)} %collective-permute-done.4.refs_3_), channel_id=1, source_target_pairs={{0,1},{1,0},{2,3},{3,2},{4,5},{5,4},{6,7},{7,6},{8,9},{9,8},{10,11... | collective-permute-start | bytes 786440 | tf_op jit(solution)/shard_map/ppermute | solution.py:23
  22.4 10.4 %collective-permute-start.6 = (bf16[128,1024]{1,0:T(8,128)(2,1)S(1)}, bf16[128,1024]{1,0:T(8,128)(2,1)S(1)}, u32[]{:S(2)}, u32[]{:S(2)}) collective-permute-start(bf16[128,1024]{1,0:T(8,128)(2,1)S(1)} %get-tuple-element.42), channel_id=1, source_target_pairs={{2,4},{3,5},{4,2},{5,3},{6,8},{7,9},{8,6},{9,7},{10,12},{11,13},{1... | collective-permute-start | bytes 786440 | tf_op jit(solution)/shard_map/ppermute | solution.py:23
  32.0 2.7 %collective-permute-start.9 = (bf16[256,1024]{1,0:T(8,128)(2,1)S(1)}, bf16[256,1024]{1,0:T(8,128)(2,1)S(1)}, u32[]{:S(2)}, u32[]{:S(2)}) collective-permute-start(bf16[256,1024]{1,0:T(8,128)(2,1)S(1)} %collective-permute-done.8.refs_2_), channel_id=1, source_target_pairs={{0,1},{1,0},{2,3},{3,2},{4,5},{5,4},{6,7},{7,6},{8,9},{9,8},{10,11... | collective-permute-start | bytes 1572872 | tf_op jit(solution)/shard_map/ppermute | solution.py:23
  32.8 1.9 %collective-permute-start.7 = (bf16[128,1024]{1,0:T(8,128)(2,1)S(1)}, bf16[128,1024]{1,0:T(8,128)(2,1)S(1)}, u32[]{:S(2)}, u32[]{:S(2)}) collective-permute-start(bf16[128,1024]{1,0:T(8,128)(2,1)S(1)} %collective-permute-done.6.refs_0_), channel_id=1, source_target_pairs={{0,1},{1,0},{2,3},{3,2},{4,5},{5,4},{6,7},{7,6},{8,9},{9,8},{10,11... | collective-permute-start | bytes 786440 | tf_op jit(solution)/shard_map/ppermute | solution.py:23
  36.2 5.9 %collective-permute-start.10 = (f32[2,384]{1,0:T(2,128)S(1)}, f32[2,384]{1,0:T(2,128)S(1)}, u32[]{:S(2)}, u32[]{:S(2)}) collective-permute-start(f32[2,384]{1,0:T(2,128)S(1)} %get-tuple-element.49.refs_10_), channel_id=1, source_target_pairs={{0,2},{1,3},{2,0},{3,1},{4,6},{5,7},{6,4},{7,5},{8,10},{9,11},{10,... | collective-permute-start | bytes 9224 | tf_op jit(solution)/shard_map/ppermute | solution.py:23
  38.4 7.0 %collective-permute-start.13 = (f32[2,384]{1,0:T(2,128)S(1)}, f32[2,384]{1,0:T(2,128)S(1)}, u32[]{:S(2)}, u32[]{:S(2)}) collective-permute-start(f32[2,384]{1,0:T(2,128)S(1)} %get-tuple-element.49.refs_10_), channel_id=1, source_target_pairs={{0,1},{1,0},{2,3},{3,2},{4,5},{5,4},{6,7},{7,6},{8,9},{9,8},{10,11... | collective-permute-start | bytes 9224 | tf_op jit(solution)/shard_map/ppermute | solution.py:23
  39.0 9.5 %collective-permute-start.12 = (f32[2,384]{1,0:T(2,128)S(1)}, f32[2,384]{1,0:T(2,128)S(1)}, u32[]{:S(2)}, u32[]{:S(2)}) collective-permute-start(f32[2,384]{1,0:T(2,128)S(1)} %get-tuple-element.49.refs_10_), channel_id=1, source_target_pairs={{1,4},{3,6},{4,1},{5,8},{6,3},{7,10},{8,5},{9,12},{10,7},{11,14},{... | collective-permute-start | bytes 9224 | tf_op jit(solution)/shard_map/ppermute | solution.py:23
  42.1 6.4 %collective-permute-start.11 = (f32[2,384]{1,0:T(2,128)S(1)}, f32[2,384]{1,0:T(2,128)S(1)}, u32[]{:S(2)}, u32[]{:S(2)}) collective-permute-start(f32[2,384]{1,0:T(2,128)S(1)} %collective-permute-done.10.refs_12_.refs_6_), channel_id=1, source_target_pairs={{0,4},{1,5},{4,8},{5,9},{6,2},{7,3},{8,12},{9,13},{10,6},{11,7},{1... | collective-permute-start | bytes 9224 | tf_op jit(solution)/shard_map/ppermute | solution.py:23
  48.5 1.2 %collective-permute-start.14 = (f32[2,2,384]{2,1,0:T(2,128)S(1)}, f32[2,2,384]{2,1,0:T(2,128)S(1)}, u32[]{:S(2)}, u32[]{:S(2)}) collective-permute-start(f32[2,2,384]{2,1,0:T(2,128)S(1)} %pad_maximum_fusion), channel_id=1, source_target_pairs={{0,1},{1,0},{2,3},{3,2},{4,5},{5,4},{6,7},{7,6},{8,9},{9,8},{10,11... | collective-permute-start | bytes 18440 | tf_op jit(solution)/shard_map/ppermute | solution.py:23

commit v6 on v5

--- a/solution.py
+++ b/solution.py
@@ -12,7 +12,7 @@
 AXES = ("tm", "sub")
 NOWHERE = 1 << 29
 LANES = 128
-STEP = 256
+STEP = 512
 VMEM = pl.BlockSpec(memory_space=pltpu.VMEM)
 COST = pl.CostEstimate(flops=0, bytes_accessed=0, transcendentals=0)
 PARAMS = pltpu.CompilerParams(vmem_limit_bytes=16 << 20)

time: 52.5 us -> 52.5 us (level)
  no operation moved by 1% of the time
where the time goes in v6:
time: 52.5 us; the launch traced here: 52.1 us
  starting transfers between devices  22.4 us (43%)
  waiting for transfers between devices  16.3 us (31%)
  Pallas kernels  13.2 us (25%)
    ppermute x15, starting transfers between devices, shift(): return lax.ppermute(x, AXES, pairs)  22.4 us
    ppermute x15, waiting for transfers between devices, shift(): return lax.ppermute(x, AXES, pairs)  16.3 us
    pallas_call x2, Pallas kernels, product_of(): pl.pallas_call(kernel, out_shape=jax.ShapeDtypeStruct((rows, depth), jnp....  5.49 us
    pallas_call x3, Pallas kernels, scores_of(): pl.pallas_call(functools.partial(score_kernel, sizes, low, first, last),...  4.73 us
    pallas_call x2, Pallas kernels, copies_of(): pl.pallas_call(kernel, out_shape=[pltpu.VMEM((size, own.shape[1]), own.dt...  2.25 us
  transfers between devices with their start and end apart: 15, of which 6 were waited for; matrix products, arithmetic and copies ran while one was open for 0% of the time, Pallas kernels for 18%

profile of v6, /device:TPU:1, one launch (start us, length us, event | category | flops | bytes accessed | tf_op | source)
XLA Modules:
  0.0 52.1 jit_solution(15347926441473149173)
XLA Ops:
  0.0 0.0 copy-start
  0.0 0.0 copy-start.2
  0.0 0.0 copy-start.1
  0.0 0.1 collective-permute-start
  0.1 1.1 %head.1 = bf16[256,1024]{1,0:T(8,128)(2,1)S(1)} custom-call(bf16[384,1024]{1,0:T(8,128)(2,1)} %refs_7_.1), custom_call_target="tpu_custom_call" | custom-call | tf_op jit(solution)/shard_map/head/pallas_call | solution.py:75
  1.2 2.7 %collective-permute-start.2 = (bf16[256,1024]{1,0:T(8,128)(2,1)S(1)}, bf16[256,1024]{1,0:T(8,128)(2,1)S(1)}, u32[]{:S(2)}, u32[]{:S(2)}) collective-permute-start(bf16[256,1024]{1,0:T(8,128)(2,1)S(1)} %head.1), channel_id=1, source_target_pairs={{0,2},{1,3},{2,0},{3,1},{4,6},{5,7},{6,4},{7,5},{8,10},{9,11},{10,... | collective-permute-start | bytes 1572872 | tf_op jit(solution)/shard_map/ppermute | solution.py:23
  3.9 1.1 %parts.1 = (bf16[128,1024]{1,0:T(8,128)(2,1)S(1)}, bf16[256,1024]{1,0:T(8,128)(2,1)S(1)}) custom-call(bf16[384,1024]{1,0:T(8,128)(2,1)} %refs_7_.1), custom_call_target="tpu_custom_call" | custom-call | tf_op jit(solution)/shard_map/parts/pallas_call | solution.py:75
  5.1 0.0 collective-permute-done.refs_1_
  5.1 3.4 %collective-permute-start.1 = (bf16[256,1024]{1,0:T(8,128)(2,1)S(1)}, bf16[256,1024]{1,0:T(8,128)(2,1)S(1)}, u32[]{:S(2)}, u32[]{:S(2)}) collective-permute-start(bf16[256,1024]{1,0:T(8,128)(2,1)S(1)} %get-tuple-element.32), channel_id=1, source_target_pairs={{1,4},{3,6},{4,1},{5,8},{6,3},{7,10},{8,5},{9,12},{10,7},{11,14},{... | collective-permute-start | bytes 1572872 | tf_op jit(solution)/shard_map/ppermute | solution.py:23
  8.5 0.0 copy-done.2
  8.5 0.0 copy-done.1
  8.6 0.7 %index.1 = (f32[1,2560]{1,0:T(1,128)S(1)}, f32[384,1]{1,0:T(8,128)S(1)}, f32[384,1]{1,0:T(8,128)S(1)}, f32[1,384]{1,0:T(1,128)S(1)}) custom-call(s32[2]{0:T(128)S(1)} %copy-done.1, s32[1,384]{1,0:T(1,128)S(1)} %broadcast_in_dim.3.offset_ref), custom_call_target="tpu_custom_call" | custom-call | tf_op jit(solution)/shard_map/index/pallas_call | solution.py:122
  9.3 0.0 copy-done
  9.3 1.5 %scores_first.1 = (bf16[768,1024]{1,0:T(8,128)(2,1)S(1)}, f32[384,768]{1,0:T(8,128)S(1)}, f32[384,128]{1,0:T(8,128)S(1)}, f32[384,128]{1,0:T(8,128)S(1)}) custom-call(bf16[384,1024]{1,0:T(8,128)(2,1)S(1)} %copy-done, bf16[384,1024]{1,0:T(8,128)(2,1)S(1)} %collective-permute-done.refs_1_, f32[384,1]{1,0:T(8,128)S(1)} %get-tuple-element.33.refs_2_.refs_5_.refs_4_.refs_6_, ...), custom_call_target="tpu_custom_call" | custom-call | tf_op jit(solution)/shard_map/scores_first/pallas_call | solution.py:195
  10.8 0.3 collective-permute-start.4
  11.1 5.0 %collective-permute-done.2.refs_1_ = bf16[256,1024]{1,0:T(8,128)(2,1)S(1)} collective-permute-done((bf16[256,1024]{1,0:T(8,128)(2,1)S(1)}, bf16[256,1024]{1,0:T(8,128)(2,1)S(1)}, u32[]{:S(2)}, u32[]{:S(2)}) %collective-permute-start.2) | collective-permute-done | bytes 524320 | tf_op jit(solution)/shard_map/ppermute | solution.py:23
  16.1 0.0 collective-permute-done.1.refs_0_
  16.1 0.9 %collective-permute-start.3 = (bf16[256,1024]{1,0:T(8,128)(2,1)S(1)}, bf16[256,1024]{1,0:T(8,128)(2,1)S(1)}, u32[]{:S(2)}, u32[]{:S(2)}) collective-permute-start(bf16[256,1024]{1,0:T(8,128)(2,1)S(1)} %collective-permute-done.2.refs_1_), channel_id=1, source_target_pairs={{0,1},{1,0},{2,3},{3,2},{4,5},{5,4},{6,7},{7,6},{8,9},{9,8},{10,11... | collective-permute-start | bytes 1572872 | tf_op jit(solution)/shard_map/ppermute | solution.py:23
  17.0 3.7 %collective-permute-start.8 = (bf16[256,1024]{1,0:T(8,128)(2,1)S(1)}, bf16[256,1024]{1,0:T(8,128)(2,1)S(1)}, u32[]{:S(2)}, u32[]{:S(2)}) collective-permute-start(bf16[256,1024]{1,0:T(8,128)(2,1)S(1)} %collective-permute-done.2.refs_1_), channel_id=1, source_target_pairs={{0,4},{1,5},{4,8},{5,9},{6,2},{7,3},{8,12},{9,13},{10,6},{11,7},{1... | collective-permute-start | bytes 1572872 | tf_op jit(solution)/shard_map/ppermute | solution.py:23
  20.7 1.0 %collective-permute-done.4.refs_3_ = bf16[128,1024]{1,0:T(8,128)(2,1)S(1)} collective-permute-done((bf16[128,1024]{1,0:T(8,128)(2,1)S(1)}, bf16[128,1024]{1,0:T(8,128)(2,1)S(1)}, u32[]{:S(2)}, u32[]{:S(2)}) %collective-permute-start.4) | collective-permute-done | bytes 262176 | tf_op jit(solution)/shard_map/ppermute | solution.py:23
  21.8 0.7 %collective-permute-start.5 = (bf16[128,1024]{1,0:T(8,128)(2,1)S(1)}, bf16[128,1024]{1,0:T(8,128)(2,1)S(1)}, u32[]{:S(2)}, u32[]{:S(2)}) collective-permute-start(bf16[128,1024]{1,0:T(8,128)(2,1)S(1)} %collective-permute-done.4.refs_3_), channel_id=1, source_target_pairs={{0,1},{1,0},{2,3},{3,2},{4,5},{5,4},{6,7},{7,6},{8,9},{9,8},{10,11... | collective-permute-start | bytes 786440 | tf_op jit(solution)/shard_map/ppermute | solution.py:23
  22.4 0.7 %collective-permute-start.6 = (bf16[128,1024]{1,0:T(8,128)(2,1)S(1)}, bf16[128,1024]{1,0:T(8,128)(2,1)S(1)}, u32[]{:S(2)}, u32[]{:S(2)}) collective-permute-start(bf16[128,1024]{1,0:T(8,128)(2,1)S(1)} %get-tuple-element.42), channel_id=1, source_target_pairs={{2,4},{3,5},{4,2},{5,3},{6,8},{7,9},{8,6},{9,7},{10,12},{11,13},{1... | collective-permute-start | bytes 786440 | tf_op jit(solution)/shard_map/ppermute | solution.py:23
  23.1 0.5 collective-permute-done.5.refs_4_
  23.6 0.0 collective-permute-done.3.refs_2_
  23.6 1.7 %scores_next.1 = (bf16[1024,1024]{1,0:T(8,128)(2,1)S(1)}, f32[384,1024]{1,0:T(8,128)S(1)}, f32[384,128]{1,0:T(8,128)S(1)}, f32[384,128]{1,0:T(8,128)S(1)}) custom-call(bf16[256,1024]{1,0:T(8,128)(2,1)S(1)} %collective-permute-done.1.refs_0_, bf16[256,1024]{1,0:T(8,128)(2,1)S(1)} %collective-permute-done.2.refs_1_, ...), custom_call_target="tpu_custom_call" | custom-call | tf_op jit(solution)/shard_map/scores_next/pallas_call | solution.py:195
  25.3 6.7 %collective-permute-done.8.refs_2_ = bf16[256,1024]{1,0:T(8,128)(2,1)S(1)} collective-permute-done((bf16[256,1024]{1,0:T(8,128)(2,1)S(1)}, bf16[256,1024]{1,0:T(8,128)(2,1)S(1)}, u32[]{:S(2)}, u32[]{:S(2)}) %collective-permute-start.8) | collective-permute-done | bytes 524320 | tf_op jit(solution)/shard_map/ppermute | solution.py:23
  32.0 0.8 %collective-permute-start.9 = (bf16[256,1024]{1,0:T(8,128)(2,1)S(1)}, bf16[256,1024]{1,0:T(8,128)(2,1)S(1)}, u32[]{:S(2)}, u32[]{:S(2)}) collective-permute-start(bf16[256,1024]{1,0:T(8,128)(2,1)S(1)} %collective-permute-done.8.refs_2_), channel_id=1, source_target_pairs={{0,1},{1,0},{2,3},{3,2},{4,5},{5,4},{6,7},{7,6},{8,9},{9,8},{10,11... | collective-permute-start | bytes 1572872 | tf_op jit(solution)/shard_map/ppermute | solution.py:23
  32.8 0.0 collective-permute-done.6.refs_0_
  32.8 0.0 collective-permute-start.7
  32.8 1.9 %collective-permute-done.7.refs_1_ = bf16[128,1024]{1,0:T(8,128)(2,1)S(1)} collective-permute-done((bf16[128,1024]{1,0:T(8,128)(2,1)S(1)}, bf16[128,1024]{1,0:T(8,128)(2,1)S(1)}, u32[]{:S(2)}, u32[]{:S(2)}) %collective-permute-start.7) | collective-permute-done | bytes 262176 | tf_op jit(solution)/shard_map/ppermute | solution.py:23
  34.7 0.0 collective-permute-done.9.refs_3_
  34.7 1.5 %scores_last.1 = (bf16[768,1024]{1,0:T(8,128)(2,1)S(1)}, f32[384,768]{1,0:T(8,128)S(1)}, f32[384,128]{1,0:T(8,128)S(1)}, f32[2,384]{1,0:T(2,128)S(1)}) custom-call(bf16[128,1024]{1,0:T(8,128)(2,1)S(1)} %collective-permute-done.6.refs_0_, bf16[128,1024]{1,0:T(8,128)(2,1)S(1)} %collective-permute-done.7.refs_1_, ...), custom_call_target="tpu_custom_call" | custom-call | tf_op jit(solution)/shard_map/scores_last/pallas_call | solution.py:195
  36.2 2.2 %collective-permute-start.10 = (f32[2,384]{1,0:T(2,128)S(1)}, f32[2,384]{1,0:T(2,128)S(1)}, u32[]{:S(2)}, u32[]{:S(2)}) collective-permute-start(f32[2,384]{1,0:T(2,128)S(1)} %get-tuple-element.49.refs_10_), channel_id=1, source_target_pairs={{0,2},{1,3},{2,0},{3,1},{4,6},{5,7},{6,4},{7,5},{8,10},{9,11},{10,... | collective-permute-start | bytes 9224 | tf_op jit(solution)/shard_map/ppermute | solution.py:23
  38.4 0.7 %collective-permute-start.13 = (f32[2,384]{1,0:T(2,128)S(1)}, f32[2,384]{1,0:T(2,128)S(1)}, u32[]{:S(2)}, u32[]{:S(2)}) collective-permute-start(f32[2,384]{1,0:T(2,128)S(1)} %get-tuple-element.49.refs_10_), channel_id=1, source_target_pairs={{0,1},{1,0},{2,3},{3,2},{4,5},{5,4},{6,7},{7,6},{8,9},{9,8},{10,11... | collective-permute-start | bytes 9224 | tf_op jit(solution)/shard_map/ppermute | solution.py:23
  39.0 3.1 %collective-permute-start.12 = (f32[2,384]{1,0:T(2,128)S(1)}, f32[2,384]{1,0:T(2,128)S(1)}, u32[]{:S(2)}, u32[]{:S(2)}) collective-permute-start(f32[2,384]{1,0:T(2,128)S(1)} %get-tuple-element.49.refs_10_), channel_id=1, source_target_pairs={{1,4},{3,6},{4,1},{5,8},{6,3},{7,10},{8,5},{9,12},{10,7},{11,14},{... | collective-permute-start | bytes 9224 | tf_op jit(solution)/shard_map/ppermute | solution.py:23
  42.1 0.0 collective-permute-done.10.refs_12_.refs_6_
  42.1 3.2 %collective-permute-start.11 = (f32[2,384]{1,0:T(2,128)S(1)}, f32[2,384]{1,0:T(2,128)S(1)}, u32[]{:S(2)}, u32[]{:S(2)}) collective-permute-start(f32[2,384]{1,0:T(2,128)S(1)} %collective-permute-done.10.refs_12_.refs_6_), channel_id=1, source_target_pairs={{0,4},{1,5},{4,8},{5,9},{6,2},{7,3},{8,12},{9,13},{10,6},{11,7},{1... | collective-permute-start | bytes 9224 | tf_op jit(solution)/shard_map/ppermute | solution.py:23
  45.3 0.0 collective-permute-done.13.refs_11_
  45.4 3.1 %product_out.1.refs_9_ = f32[384,1024]{1,0:T(8,128)S(1)} custom-call(bf16[768,1024]{1,0:T(8,128)(2,1)S(1)} %get-tuple-element.50.refs_0_, bf16[1024,1024]{1,0:T(8,128)(2,1)S(1)} %get-tuple-element.41.refs_1_.refs_0_, bf16[768,1024]{1,0:T(8,128)(2,1)S(1)} %get-tuple-element.46.refs_2_.refs_1_, f32[384,768]{1,0:T(8,128)S(1)} %get-tuple-element.51.refs_3_, ...), custom_call_target="tpu_custom_call" | custom-call | tf_op jit(solution)/shard_map/product_out/pallas_call | solution.py:276
  48.5 0.0 collective-permute-done.12.refs_5_
  48.5 0.0 collective-permute-done.11.refs_7_
  48.5 0.1 collective-permute-start.14
  48.6 1.2 %collective-permute-done.14.refs_8_ = f32[2,2,384]{2,1,0:T(2,128)S(1)} collective-permute-done((f32[2,2,384]{2,1,0:T(2,128)S(1)}, f32[2,2,384]{2,1,0:T(2,128)S(1)}, u32[]{:S(2)}, u32[]{:S(2)}) %collective-permute-start.14) | collective-permute-done | bytes 6176 | tf_op jit(solution)/shard_map/ppermute | solution.py:23
  49.8 2.4 %product_back.1 = f32[384,1024]{1,0:T(8,128)} custom-call(bf16[1024,1024]{1,0:T(8,128)(2,1)S(1)} %get-tuple-element.41.refs_1_.refs_0_, bf16[768,1024]{1,0:T(8,128)(2,1)S(1)} %get-tuple-element.46.refs_2_.refs_1_, f32[384,1024]{1,0:T(8,128)S(1)} %get-tuple-element.47.refs_4_.refs_2_, f32[384,768]{1,0:T(8,128)S(1)} %get-tuple-element.48.refs_5_.refs_3_, ...), custom_call_target="tpu_custom_call" | custom-call | tf_op jit(solution)/shard_map/product_back/pallas_call | solution.py:276
  (2 shorter events, 0.0 us)
Async XLA Ops:
  0.0 9.3 %copy-start = (bf16[384,1024]{1,0:T(8,128)(2,1)S(1)}, bf16[384,1024]{1,0:T(8,128)(2,1)}, u32[]{:S(2)}) copy-start(bf16[384,1024]{1,0:T(8,128)(2,1)} %refs_7_.1) | copy-start | bytes 2359300
  0.0 8.5 %copy-start.2 = (s32[384]{0:T(512)S(1)}, s32[384]{0:T(512)}, u32[]{:S(2)}) copy-start(s32[384]{0:T(512)} %param.4) | copy-start | bytes 4612
  0.0 8.5 %copy-start.1 = (s32[2]{0:T(128)S(1)}, s32[2]{0:T(128)}, u32[]{:S(2)}) copy-start(s32[2]{0:T(128)} %limits_ref.1) | copy-start | bytes 28
  0.0 5.1 %collective-permute-start = (bf16[384,1024]{1,0:T(8,128)(2,1)}, bf16[384,1024]{1,0:T(8,128)(2,1)S(1)}, u32[]{:S(2)}, u32[]{:S(2)}) collective-permute-start(bf16[384,1024]{1,0:T(8,128)(2,1)} %refs_7_.1), channel_id=1, source_target_pairs={{0,1},{1,0},{2,3},{3,2},{4,5},{5,4},{6,7},{7,6},{8,9},{9,8},{10,11... | collective-permute-start | bytes 2359304 | tf_op jit(solution)/shard_map/ppermute | solution.py:23
  1.2 14.9 %collective-permute-start.2 = (bf16[256,1024]{1,0:T(8,128)(2,1)S(1)}, bf16[256,1024]{1,0:T(8,128)(2,1)S(1)}, u32[]{:S(2)}, u32[]{:S(2)}) collective-permute-start(bf16[256,1024]{1,0:T(8,128)(2,1)S(1)} %head.1), channel_id=1, source_target_pairs={{0,2},{1,3},{2,0},{3,1},{4,6},{5,7},{6,4},{7,5},{8,10},{9,11},{10,... | collective-permute-start | bytes 1572872 | tf_op jit(solution)/shard_map/ppermute | solution.py:23
  5.1 11.1 %collective-permute-start.1 = (bf16[256,1024]{1,0:T(8,128)(2,1)S(1)}, bf16[256,1024]{1,0:T(8,128)(2,1)S(1)}, u32[]{:S(2)}, u32[]{:S(2)}) collective-permute-start(bf16[256,1024]{1,0:T(8,128)(2,1)S(1)} %get-tuple-element.32), channel_id=1, source_target_pairs={{1,4},{3,6},{4,1},{5,8},{6,3},{7,10},{8,5},{9,12},{10,7},{11,14},{... | collective-permute-start | bytes 1572872 | tf_op jit(solution)/shard_map/ppermute | solution.py:23
  10.8 10.9 %collective-permute-start.4 = (bf16[128,1024]{1,0:T(8,128)(2,1)S(1)}, bf16[128,1024]{1,0:T(8,128)(2,1)S(1)}, u32[]{:S(2)}, u32[]{:S(2)}) collective-permute-start(bf16[128,1024]{1,0:T(8,128)(2,1)S(1)} %get-tuple-element.42), channel_id=1, source_target_pairs={{0,2},{1,3},{2,0},{3,1},{4,6},{5,7},{6,4},{7,5},{8,10},{9,11},{10,... | collective-permute-start | bytes 786440 | tf_op jit(solution)/shard_map/ppermute | solution.py:23
  16.1 7.4 %collective-permute-start.3 = (bf16[256,1024]{1,0:T(8,128)(2,1)S(1)}, bf16[256,1024]{1,0:T(8,128)(2,1)S(1)}, u32[]{:S(2)}, u32[]{:S(2)}) collective-permute-start(bf16[256,1024]{1,0:T(8,128)(2,1)S(1)} %collective-permute-done.2.refs_1_), channel_id=1, source_target_pairs={{0,1},{1,0},{2,3},{3,2},{4,5},{5,4},{6,7},{7,6},{8,9},{9,8},{10,11... | collective-permute-start | bytes 1572872 | tf_op jit(solution)/shard_map/ppermute | solution.py:23
  17.0 15.0 %collective-permute-start.8 = (bf16[256,1024]{1,0:T(8,128)(2,1)S(1)}, bf16[256,1024]{1,0:T(8,128)(2,1)S(1)}, u32[]{:S(2)}, u32[]{:S(2)}) collective-permute-start(bf16[256,1024]{1,0:T(8,128)(2,1)S(1)} %collective-permute-done.2.refs_1_), channel_id=1, source_target_pairs={{0,4},{1,5},{4,8},{5,9},{6,2},{7,3},{8,12},{9,13},{10,6},{11,7},{1... | collective-permute-start | bytes 1572872 | tf_op jit(solution)/shard_map/ppermute | solution.py:23
  21.8 1.8 %collective-permute-start.5 = (bf16[128,1024]{1,0:T(8,128)(2,1)S(1)}, bf16[128,1024]{1,0:T(8,128)(2,1)S(1)}, u32[]{:S(2)}, u32[]{:S(2)}) collective-permute-start(bf16[128,1024]{1,0:T(8,128)(2,1)S(1)} %collective-permute-done.4.refs_3_), channel_id=1, source_target_pairs={{0,1},{1,0},{2,3},{3,2},{4,5},{5,4},{6,7},{7,6},{8,9},{9,8},{10,11... | collective-permute-start | bytes 786440 | tf_op jit(solution)/shard_map/ppermute | solution.py:23
  22.4 10.4 %collective-permute-start.6 = (bf16[128,1024]{1,0:T(8,128)(2,1)S(1)}, bf16[128,1024]{1,0:T(8,128)(2,1)S(1)}, u32[]{:S(2)}, u32[]{:S(2)}) collective-permute-start(bf16[128,1024]{1,0:T(8,128)(2,1)S(1)} %get-tuple-element.42), channel_id=1, source_target_pairs={{2,4},{3,5},{4,2},{5,3},{6,8},{7,9},{8,6},{9,7},{10,12},{11,13},{1... | collective-permute-start | bytes 786440 | tf_op jit(solution)/shard_map/ppermute | solution.py:23
  32.0 2.7 %collective-permute-start.9 = (bf16[256,1024]{1,0:T(8,128)(2,1)S(1)}, bf16[256,1024]{1,0:T(8,128)(2,1)S(1)}, u32[]{:S(2)}, u32[]{:S(2)}) collective-permute-start(bf16[256,1024]{1,0:T(8,128)(2,1)S(1)} %collective-permute-done.8.refs_2_), channel_id=1, source_target_pairs={{0,1},{1,0},{2,3},{3,2},{4,5},{5,4},{6,7},{7,6},{8,9},{9,8},{10,11... | collective-permute-start | bytes 1572872 | tf_op jit(solution)/shard_map/ppermute | solution.py:23
  32.8 1.9 %collective-permute-start.7 = (bf16[128,1024]{1,0:T(8,128)(2,1)S(1)}, bf16[128,1024]{1,0:T(8,128)(2,1)S(1)}, u32[]{:S(2)}, u32[]{:S(2)}) collective-permute-start(bf16[128,1024]{1,0:T(8,128)(2,1)S(1)} %collective-permute-done.6.refs_0_), channel_id=1, source_target_pairs={{0,1},{1,0},{2,3},{3,2},{4,5},{5,4},{6,7},{7,6},{8,9},{9,8},{10,11... | collective-permute-start | bytes 786440 | tf_op jit(solution)/shard_map/ppermute | solution.py:23
  36.2 5.9 %collective-permute-start.10 = (f32[2,384]{1,0:T(2,128)S(1)}, f32[2,384]{1,0:T(2,128)S(1)}, u32[]{:S(2)}, u32[]{:S(2)}) collective-permute-start(f32[2,384]{1,0:T(2,128)S(1)} %get-tuple-element.49.refs_10_), channel_id=1, source_target_pairs={{0,2},{1,3},{2,0},{3,1},{4,6},{5,7},{6,4},{7,5},{8,10},{9,11},{10,... | collective-permute-start | bytes 9224 | tf_op jit(solution)/shard_map/ppermute | solution.py:23
  38.4 7.0 %collective-permute-start.13 = (f32[2,384]{1,0:T(2,128)S(1)}, f32[2,384]{1,0:T(2,128)S(1)}, u32[]{:S(2)}, u32[]{:S(2)}) collective-permute-start(f32[2,384]{1,0:T(2,128)S(1)} %get-tuple-element.49.refs_10_), channel_id=1, source_target_pairs={{0,1},{1,0},{2,3},{3,2},{4,5},{5,4},{6,7},{7,6},{8,9},{9,8},{10,11... | collective-permute-start | bytes 9224 | tf_op jit(solution)/shard_map/ppermute | solution.py:23
  39.0 9.5 %collective-permute-start.12 = (f32[2,384]{1,0:T(2,128)S(1)}, f32[2,384]{1,0:T(2,128)S(1)}, u32[]{:S(2)}, u32[]{:S(2)}) collective-permute-start(f32[2,384]{1,0:T(2,128)S(1)} %get-tuple-element.49.refs_10_), channel_id=1, source_target_pairs={{1,4},{3,6},{4,1},{5,8},{6,3},{7,10},{8,5},{9,12},{10,7},{11,14},{... | collective-permute-start | bytes 9224 | tf_op jit(solution)/shard_map/ppermute | solution.py:23
  42.1 6.4 %collective-permute-start.11 = (f32[2,384]{1,0:T(2,128)S(1)}, f32[2,384]{1,0:T(2,128)S(1)}, u32[]{:S(2)}, u32[]{:S(2)}) collective-permute-start(f32[2,384]{1,0:T(2,128)S(1)} %collective-permute-done.10.refs_12_.refs_6_), channel_id=1, source_target_pairs={{0,4},{1,5},{4,8},{5,9},{6,2},{7,3},{8,12},{9,13},{10,6},{11,7},{1... | collective-permute-start | bytes 9224 | tf_op jit(solution)/shard_map/ppermute | solution.py:23
  48.5 1.2 %collective-permute-start.14 = (f32[2,2,384]{2,1,0:T(2,128)S(1)}, f32[2,2,384]{2,1,0:T(2,128)S(1)}, u32[]{:S(2)}, u32[]{:S(2)}) collective-permute-start(f32[2,2,384]{2,1,0:T(2,128)S(1)} %pad_maximum_fusion), channel_id=1, source_target_pairs={{0,1},{1,0},{2,3},{3,2},{4,5},{5,4},{6,7},{7,6},{8,9},{9,8},{10,11... | collective-permute-start | bytes 18440 | tf_op jit(solution)/shard_map/ppermute | solution.py:23
